TPU v7x, 32 devices: a whole 2x2x4 slice. The times are simulated.
32 devices in a mesh: ctx: 8 (over z, core), fsdp: 4 (over y, x).
Axes of the slice: x: 2, y: 2, z: 4, core: 2. Of those that a mesh axis runs over, the one named last changes fastest.
Arguments:
- inputs: bfloat16 [2, 4, 2048, 1024], P(None, 'fsdp', 'ctx'), may hold values from -6 to 6
- block_slots: int32 [2, 4, 16], P(None, 'fsdp'), may hold values from 0 to 15, as said below
- doc_starts: int32 [2, 4, 4], P(None, 'fsdp'), may hold values from 0 to 2047, as said below
- mem_index: int32 [2, 4, 2048, 8, 32], P(None, 'fsdp', 'ctx'), may hold values from 0 to 2047
- mem_keys: bfloat16 [4, 2048, 1024], P('fsdp', 'ctx'), may hold values from -8 to 8
- mem_values: bfloat16 [4, 2048, 1024], P('fsdp', 'ctx'), may hold values from -6 to 6
- out_grad: bfloat16 [2, 4, 2048, 1024], P(None, 'fsdp', 'ctx'), may hold values from -6 to 6
- local_gain_in: bfloat16 [1024], P('fsdp'), may hold values from 0.5 to 1.5
- local_bias_in: bfloat16 [1024], P('fsdp'), may hold values from -1.25 to 1.25
- local_w_qkv: bfloat16 [1024, 3072], P('fsdp'), may hold values from -0.1875 to 0.1875
- local_rel_bias: bfloat16 [8, 32], P('fsdp'), may hold values from -3 to 3
- local_w_out: bfloat16 [1024, 1024], P('fsdp'), may hold values from -0.75 to 0.75
- local_gain_mid: bfloat16 [1024], P('fsdp'), may hold values from 0.5 to 1.5
- local_bias_mid: bfloat16 [1024], P('fsdp'), may hold values from -1.25 to 1.25
- local_w_in: bfloat16 [1024, 4096], P('fsdp'), may hold values from -0.1875 to 0.1875
- local_w_down: bfloat16 [4096, 1024], P('fsdp'), may hold values from -0.09375 to 0.09375
- recall_gain_in: bfloat16 [1024], P('fsdp'), may hold values from 0.5 to 1.5
- recall_bias_in: bfloat16 [1024], P('fsdp'), may hold values from -1.25 to 1.25
- recall_w_qkv: bfloat16 [1024, 3072], P('fsdp'), may hold values from -0.1875 to 0.1875
- recall_rel_bias: bfloat16 [8, 32], P('fsdp'), may hold values from -3 to 3
- recall_w_out: bfloat16 [1024, 1024], P('fsdp'), may hold values from -0.75 to 0.75
- recall_gain_mid: bfloat16 [1024], P('fsdp'), may hold values from 0.5 to 1.5
- recall_bias_mid: bfloat16 [1024], P('fsdp'), may hold values from -1.25 to 1.25
- recall_w_in: bfloat16 [1024, 4096], P('fsdp'), may hold values from -0.1875 to 0.1875
- recall_w_down: bfloat16 [4096, 1024], P('fsdp'), may hold values from -0.09375 to 0.09375
- recall_gate: bfloat16 [8], P('fsdp'), may hold values from -8 to 8
Outputs:
- outputs: bfloat16 [2, 4, 2048, 1024], P(None, 'fsdp', 'ctx')
- input_grad: float32 [2, 4, 2048, 1024], P(None, 'fsdp', 'ctx')
- grad_local_gain_in: float32 [1024], P('fsdp')
- grad_local_bias_in: float32 [1024], P('fsdp')
- grad_local_w_qkv: float32 [1024, 3072], P('fsdp')
- grad_local_rel_bias: float32 [8, 32], P('fsdp')
- grad_local_w_out: float32 [1024, 1024], P('fsdp')
- grad_local_gain_mid: float32 [1024], P('fsdp')
- grad_local_bias_mid: float32 [1024], P('fsdp')
- grad_local_w_in: float32 [1024, 4096], P('fsdp')
- grad_local_w_down: float32 [4096, 1024], P('fsdp')
- grad_recall_gain_in: float32 [1024], P('fsdp')
- grad_recall_bias_in: float32 [1024], P('fsdp')
- grad_recall_w_qkv: float32 [1024, 3072], P('fsdp')
- grad_recall_rel_bias: float32 [8, 32], P('fsdp')
- grad_recall_w_out: float32 [1024, 1024], P('fsdp')
- grad_recall_gain_mid: float32 [1024], P('fsdp')
- grad_recall_bias_mid: float32 [1024], P('fsdp')
- grad_recall_w_in: float32 [1024, 4096], P('fsdp')
- grad_recall_w_down: float32 [4096, 1024], P('fsdp')
- grad_recall_gate: float32 [8], P('fsdp')
Inputs may be any that keep to these rules, and one draw needn't show every extreme that they name: `block_slots`: the two slots of every device of ctx (slots 2 c and 2 c + 1) hold stream blocks j and 15 - j; each block of a stream stands once. `doc_starts`: the first start is 0; the others do not fall and lie in the stream's second half; equal starts give empty documents.
All inputs are finite; a program needn't handle non-finite values.
Results may differ from a plain program's by a relative error of at most 0.034.
Values may be sent and summed in bfloat16 or wider, within the bound.
No kernel may reach another device: no remote copies, remote signals or barrier semaphores. Data moves between devices by JAX's collectives and lax.ppermute only.
A program may use at most 512 MiB of HBM per device.

v0:
```python
import math

import jax
import jax.numpy as jnp
import numpy as np
from jax import lax
from jax.sharding import PartitionSpec as P

HEADS = 8
HEAD_DIM = 128
BUCKETS = 32
WIN = 512
BLK = 128


EPS = 1e-05
NEGATIVE = -1000000000.0
FAR_DISTANCE = 128


def bucket_table(total_count, buckets):
    exact_count = buckets // 2
    result = []
    for distance in range(total_count):
        if distance < exact_count:
            result.append(distance)
        else:
            scaled = math.log(distance / exact_count) / math.log(FAR_DISTANCE / exact_count)
            result.append(min(exact_count + int(scaled * (buckets - exact_count)), buckets - 1))
    return np.array(result, dtype=np.int32)


def window_tables():
    reach_blocks = WIN // BLK
    span_keys = (reach_blocks + 1) * BLK
    distance = reach_blocks * BLK + np.arange(BLK)[:, None] - np.arange(span_keys)[None, :]
    inside = (distance >= 0) & (distance < WIN)
    buckets = bucket_table(WIN, BUCKETS)[np.clip(distance, 0, WIN - 1)]
    return (reach_blocks, span_keys, inside, buckets)


def key_side_tables():
    reach_blocks = WIN // BLK
    span_rows = (reach_blocks + 1) * BLK
    distance = np.arange(span_rows)[:, None] - np.arange(BLK)[None, :]
    inside = (distance >= 0) & (distance < WIN)
    buckets = bucket_table(WIN, BUCKETS)[np.clip(distance, 0, WIN - 1)]
    return (inside, buckets)


def norm_forward(vector, gain, offset):
    centre = vector - jnp.mean(vector, -1, keepdims=True)
    spread = jnp.mean(centre * centre, -1, keepdims=True)
    return centre * lax.rsqrt(spread + EPS) * gain + offset


def doc_of(starts, positions):
    return jnp.sum((starts <= positions[..., None]).astype(jnp.int32), -1) - 1


def window_setup(slot_table, starts, my_index):
    reach_blocks, span_keys, inside, buckets = window_tables()
    total_slots = slot_table.shape[0]
    inverse = jnp.argsort(slot_table)
    own_blocks = lax.dynamic_slice_in_dim(slot_table, 2 * my_index, 2)
    key_blocks = (
        own_blocks[:, None] - reach_blocks + jnp.arange(reach_blocks + 1, dtype=jnp.int32)[None, :]
    )
    key_slots = inverse[jnp.clip(key_blocks, 0, total_slots - 1)]
    query_pos = own_blocks[:, None] * BLK + jnp.arange(BLK, dtype=jnp.int32)[None, :]
    key_pos = (own_blocks[:, None] - reach_blocks) * BLK + jnp.arange(span_keys, dtype=jnp.int32)[
        None, :
    ]
    key_doc = jnp.where(key_pos >= 0, doc_of(starts, key_pos), -1)
    query_doc = doc_of(starts, query_pos)
    allowed = jnp.asarray(inside)[None] & (query_doc[:, :, None] == key_doc[:, None, :])
    onehot = (jnp.asarray(buckets)[:, :, None] == jnp.arange(BUCKETS)[None, None, :]).astype(
        jnp.bfloat16
    )
    inside_k, buckets_k = key_side_tables()
    seeing_blocks = own_blocks[:, None] + jnp.arange(reach_blocks + 1, dtype=jnp.int32)[None, :]
    seeing_valid = seeing_blocks < total_slots
    seeing_slots = inverse[jnp.clip(seeing_blocks, 0, total_slots - 1)]
    seeing_pos = (
        seeing_blocks[:, :, None] * BLK + jnp.arange(BLK, dtype=jnp.int32)[None, None, :]
    ).reshape(2, -1)
    seeing_doc = doc_of(starts, seeing_pos)
    valid_rows = jnp.repeat(seeing_valid, BLK, axis=1)
    allowed_k = (
        jnp.asarray(inside_k)[None]
        & valid_rows[:, :, None]
        & (seeing_doc[:, :, None] == query_doc[:, None, :])
    )
    onehot_k = (jnp.asarray(buckets_k)[:, :, None] == jnp.arange(BUCKETS)[None, None, :]).astype(
        jnp.bfloat16
    )
    return (key_slots, allowed, onehot, seeing_slots, allowed_k, onehot_k)


def window_of(everyone, key_slots):
    last_width = everyone.shape[-1]
    blocks = everyone.reshape(-1, BLK, last_width)[key_slots.reshape(-1)]
    return blocks.reshape(key_slots.shape[0], -1, last_width)


def local_scores(queries, key_win, rel_table, onehot, allowed):
    rel_scores = jnp.einsum("hn,ijn->hij", rel_table, onehot, preferred_element_type=jnp.float32)
    scores = jnp.einsum("sihd,sjhd->shij", queries, key_win, preferred_element_type=jnp.float32)
    scores = scores * HEAD_DIM ** (-0.5) + rel_scores[None]
    return jnp.where(allowed[:, None], scores, NEGATIVE)


def split_product(weight, right):
    upper = weight.astype(jnp.bfloat16)
    lower = (weight - upper.astype(jnp.float32)).astype(jnp.bfloat16)
    return jnp.dot(upper, right, preferred_element_type=jnp.float32) + jnp.dot(
        lower, right, preferred_element_type=jnp.float32
    )


def recall_weights(query_head, key_head, index_head):
    row_count = key_head.shape[0]
    counts = jnp.sum(
        (index_head[:, :, None] == jnp.arange(row_count, dtype=jnp.int32)[None, None, :]).astype(
            jnp.float32
        ),
        1,
    )
    scores = jnp.einsum(
        "td,md->tm", query_head, key_head, preferred_element_type=jnp.float32
    ) * HEAD_DIM ** (-0.5)
    chosen = counts > 0
    top_score = jnp.max(jnp.where(chosen, scores, NEGATIVE), -1, keepdims=True)
    exps = jnp.exp(jnp.where(chosen, scores - top_score, NEGATIVE))
    total = jnp.sum(counts * exps, -1, keepdims=True)
    return (counts, exps / total)


def recall_out_head(items):
    query_head, key_head, value_head, index_head = items
    counts, probs = recall_weights(query_head, key_head, index_head)
    weight = counts * probs.astype(jnp.bfloat16).astype(jnp.float32)
    return split_product(weight, value_head)


def recall_grad_head(items):
    query_head, key_head, value_head, index_head, grad_head = items
    counts, probs = recall_weights(query_head, key_head, index_head)
    grad_prob = jnp.einsum("td,md->tm", grad_head, value_head, preferred_element_type=jnp.float32)
    centre = jnp.sum(counts * probs * grad_prob, -1, keepdims=True)
    score_low = (probs * (grad_prob - centre)).astype(jnp.bfloat16).astype(jnp.float32)
    return split_product(counts * score_low, key_head) * HEAD_DIM ** (-0.5)


def head_major(query_flat, rows_idx):
    queries = jnp.transpose(query_flat.reshape(-1, HEADS, HEAD_DIM), (1, 0, 2))
    return (queries, jnp.transpose(rows_idx, (1, 0, 2)))


def split_window(everyone, key_slots, model_width):
    window = window_of(everyone, key_slots)
    key_win = window[..., :model_width].reshape(2, -1, HEADS, HEAD_DIM)
    val_win = window[..., model_width:].reshape(2, -1, HEADS, HEAD_DIM)
    return (key_win, val_win)


def forward_layer(stream, weights, window_info, memory_part, recall):
    key_slots, allowed, onehot = window_info[:3]
    model_width = stream.shape[-1]
    normed_low = norm_forward(
        stream, weights[0].astype(jnp.float32), weights[1].astype(jnp.float32)
    ).astype(jnp.bfloat16)
    qkv_low = jnp.dot(normed_low, weights[2], preferred_element_type=jnp.float32).astype(
        jnp.bfloat16
    )
    everyone = lax.all_gather(qkv_low[:, model_width:], "ctx", axis=0, tiled=True)
    key_win, val_win = split_window(everyone, key_slots, model_width)
    queries = qkv_low[:, :model_width].reshape(2, BLK, HEADS, HEAD_DIM)
    scores = local_scores(queries, key_win, weights[3], onehot, allowed)
    row_max = jnp.max(scores, -1, keepdims=True)
    exponent = jnp.exp(scores - row_max)
    row_sum = jnp.sum(exponent, -1, keepdims=True)
    attn_prob = exponent / row_sum
    log_total = row_max + jnp.log(row_sum)
    local_out = jnp.einsum(
        "shij,sjhd->sihd",
        attn_prob.astype(jnp.bfloat16),
        val_win,
        preferred_element_type=jnp.float32,
    ).reshape(2 * BLK, HEADS, HEAD_DIM)
    if recall:
        heads_k, heads_v, rows_idx = memory_part
        query_heads, index_heads = head_major(qkv_low[:, :model_width], rows_idx)
        mem_heads = lax.map(recall_out_head, (query_heads, heads_k, heads_v, index_heads))
        mem_out = jnp.transpose(mem_heads, (1, 0, 2))
        gate_value = jax.nn.sigmoid(weights[9].astype(jnp.float32))[None, :, None]
        mixed_heads = gate_value * mem_out + (1.0 - gate_value) * local_out
    else:
        mem_out = local_out
        mixed_heads = local_out
    mixed_low = mixed_heads.reshape(2 * BLK, model_width).astype(jnp.bfloat16)
    hidden = stream + jnp.dot(mixed_low, weights[4], preferred_element_type=jnp.float32)
    normed_mid = norm_forward(
        hidden, weights[5].astype(jnp.float32), weights[6].astype(jnp.float32)
    ).astype(jnp.bfloat16)
    up_proj = jnp.dot(normed_mid, weights[7], preferred_element_type=jnp.float32)
    act_low = jax.nn.gelu(up_proj).astype(jnp.bfloat16)
    result = hidden + jnp.dot(act_low, weights[8], preferred_element_type=jnp.float32)
    stored = (
        stream,
        normed_low,
        qkv_low,
        log_total,
        local_out,
        mem_out,
        mixed_low,
        hidden,
        normed_mid,
        up_proj,
        act_low,
        everyone,
    )
    return (result, stored)


def backward_layer(grad_out, stored, weights, window_info, memory_part, recall):
    (
        stream,
        normed_low,
        qkv_low,
        log_total,
        local_out,
        mem_out,
        mixed_low,
        hidden,
        normed_mid,
        up_proj,
        act_low,
        kept_pairs,
    ) = stored
    key_slots, allowed, onehot = window_info[:3]
    model_width = stream.shape[-1]
    out_low = grad_out.astype(jnp.bfloat16)
    grad_down = jnp.einsum("tf,td->fd", act_low, out_low, preferred_element_type=jnp.float32)
    grad_act = jnp.einsum("td,fd->tf", out_low, weights[8], preferred_element_type=jnp.float32)
    gelu_value, gelu_back = jax.vjp(jax.nn.gelu, up_proj)
    up_low = gelu_back(grad_act)[0].astype(jnp.bfloat16)
    grad_in = jnp.einsum("td,tf->df", normed_mid, up_low, preferred_element_type=jnp.float32)
    grad_mid_norm = jnp.einsum("tf,df->td", up_low, weights[7], preferred_element_type=jnp.float32)
    norm_value, norm_back = jax.vjp(
        norm_forward, hidden, weights[5].astype(jnp.float32), weights[6].astype(jnp.float32)
    )
    hidden_part, grad_gain_mid, grad_bias_mid = norm_back(grad_mid_norm)
    grad_hidden = grad_out + hidden_part
    branch_low = grad_hidden.astype(jnp.bfloat16)
    grad_wout = jnp.einsum("td,te->de", mixed_low, branch_low, preferred_element_type=jnp.float32)
    grad_mixed = jnp.einsum("te,de->td", branch_low, weights[4], preferred_element_type=jnp.float32)
    grad_mixed = grad_mixed.reshape(-1, HEADS, HEAD_DIM)
    if recall:
        heads_k, heads_v, rows_idx = memory_part
        gate_value = jax.nn.sigmoid(weights[9].astype(jnp.float32))
        gate_heads = gate_value[None, :, None]
        grad_gate = (
            jnp.sum(grad_mixed * (mem_out - local_out), axis=(0, 2))
            * gate_value
            * (1.0 - gate_value)
        )
        mem_grad_low = (gate_heads * grad_mixed).astype(jnp.bfloat16)
        loc_grad_low = ((1.0 - gate_heads) * grad_mixed).astype(jnp.bfloat16)
        query_heads, index_heads = head_major(qkv_low[:, :model_width], rows_idx)
        grad_heads = jnp.transpose(mem_grad_low, (1, 0, 2))
        query_mem = lax.map(
            recall_grad_head, (query_heads, heads_k, heads_v, index_heads, grad_heads)
        )
        query_mem = jnp.transpose(query_mem, (1, 0, 2)).reshape(-1, model_width)
    else:
        loc_grad_low = grad_mixed.astype(jnp.bfloat16)
        query_mem = jnp.zeros((2 * BLK, model_width), jnp.float32)
    everyone = lax.all_gather(qkv_low[:, model_width:], "ctx", axis=0, tiled=True)
    key_win, val_win = split_window(everyone, key_slots, model_width)
    queries = qkv_low[:, :model_width].reshape(2, BLK, HEADS, HEAD_DIM)
    scores = local_scores(queries, key_win, weights[3], onehot, allowed)
    attn_prob = jnp.exp(scores - log_total)
    loc_grad_four = loc_grad_low.reshape(2, BLK, HEADS, HEAD_DIM)
    grad_prob = jnp.einsum(
        "sihd,sjhd->shij", loc_grad_four, val_win, preferred_element_type=jnp.float32
    )
    row_centre = jnp.sum(attn_prob * grad_prob, -1, keepdims=True)
    score_low = (attn_prob * (grad_prob - row_centre)).astype(jnp.bfloat16)
    grad_rel = jnp.einsum("shij,ijn->hn", score_low, onehot, preferred_element_type=jnp.float32)
    grad_query = jnp.einsum(
        "shij,sjhd->sihd", score_low, key_win, preferred_element_type=jnp.float32
    ) * HEAD_DIM ** (-0.5)
    grad_key = jnp.einsum(
        "shij,sihd->sjhd", score_low, queries, preferred_element_type=jnp.float32
    ) * HEAD_DIM ** (-0.5)
    grad_val = jnp.einsum(
        "shij,sihd->sjhd",
        attn_prob.astype(jnp.bfloat16),
        loc_grad_four,
        preferred_element_type=jnp.float32,
    )
    span_keys = key_win.shape[1]
    grad_pair = jnp.concatenate(
        [grad_key.reshape(2, span_keys, model_width), grad_val.reshape(2, span_keys, model_width)],
        -1,
    )
    total_slots = everyone.shape[0] // BLK
    spread_back = jnp.zeros((total_slots, BLK, 2 * model_width), jnp.float32)
    spread_back = spread_back.at[key_slots.reshape(-1)].add(
        grad_pair.reshape(-1, BLK, 2 * model_width)
    )
    own_pair = lax.psum_scatter(
        spread_back.reshape(-1, 2 * model_width).astype(jnp.bfloat16),
        "ctx",
        scatter_dimension=0,
        tiled=True,
    ).astype(jnp.float32)
    grad_q_total = grad_query.reshape(2 * BLK, model_width) + query_mem
    qkv_grad_low = jnp.concatenate([grad_q_total, own_pair], -1).astype(jnp.bfloat16)
    grad_qkv = jnp.einsum("td,tc->dc", normed_low, qkv_grad_low, preferred_element_type=jnp.float32)
    grad_normed = jnp.einsum(
        "tc,dc->td", qkv_grad_low, weights[2], preferred_element_type=jnp.float32
    )
    first_value, first_back = jax.vjp(
        norm_forward, stream, weights[0].astype(jnp.float32), weights[1].astype(jnp.float32)
    )
    stream_part, grad_gain_in, grad_bias_in = first_back(grad_normed)
    grad_stream = grad_hidden + stream_part
    grads = [
        grad_gain_in,
        grad_bias_in,
        grad_qkv,
        grad_rel,
        grad_wout,
        grad_gain_mid,
        grad_bias_mid,
        grad_in,
        grad_down,
    ]
    if recall:
        grads = grads + [grad_gate]
    return (grad_stream, grads)


def local(
    inputs,
    block_slots,
    doc_starts,
    mem_index,
    mem_keys,
    mem_values,
    out_grad,
    local_gain_in,
    local_bias_in,
    local_w_qkv,
    local_rel_bias,
    local_w_out,
    local_gain_mid,
    local_bias_mid,
    local_w_in,
    local_w_down,
    recall_gain_in,
    recall_bias_in,
    recall_w_qkv,
    recall_rel_bias,
    recall_w_out,
    recall_gain_mid,
    recall_bias_mid,
    recall_w_in,
    recall_w_down,
    recall_gate,
):
    my_index = lax.axis_index("ctx")
    fsdp_count = lax.axis_size("fsdp")
    memory_k, memory_v = (
        lax.all_gather(mem_keys[0], "ctx", axis=0, tiled=True),
        lax.all_gather(mem_values[0], "ctx", axis=0, tiled=True),
    )
    heads_k = jnp.transpose(memory_k.reshape(-1, HEADS, HEAD_DIM), (1, 0, 2))
    heads_v = jnp.transpose(memory_v.reshape(-1, HEADS, HEAD_DIM), (1, 0, 2))
    local_params = (
        local_gain_in,
        local_bias_in,
        local_w_qkv,
        local_rel_bias,
        local_w_out,
        local_gain_mid,
        local_bias_mid,
        local_w_in,
        local_w_down,
    )
    recall_params = (
        recall_gain_in,
        recall_bias_in,
        recall_w_qkv,
        recall_rel_bias,
        recall_w_out,
        recall_gain_mid,
        recall_bias_mid,
        recall_w_in,
        recall_w_down,
        recall_gate,
    )
    fetched = (
        lax.all_gather(local_gain_in, "fsdp", axis=0, tiled=True),
        lax.all_gather(local_bias_in, "fsdp", axis=0, tiled=True),
        lax.all_gather(local_w_qkv, "fsdp", axis=0, tiled=True),
        lax.all_gather(local_rel_bias, "fsdp", axis=0, tiled=True),
        lax.all_gather(local_w_out, "fsdp", axis=0, tiled=True),
        lax.all_gather(local_gain_mid, "fsdp", axis=0, tiled=True),
        lax.all_gather(local_bias_mid, "fsdp", axis=0, tiled=True),
        lax.all_gather(local_w_in, "fsdp", axis=0, tiled=True),
        lax.all_gather(local_w_down, "fsdp", axis=0, tiled=True),
        lax.all_gather(recall_gain_in, "fsdp", axis=0, tiled=True),
        lax.all_gather(recall_bias_in, "fsdp", axis=0, tiled=True),
        lax.all_gather(recall_w_qkv, "fsdp", axis=0, tiled=True),
        lax.all_gather(recall_rel_bias, "fsdp", axis=0, tiled=True),
        lax.all_gather(recall_w_out, "fsdp", axis=0, tiled=True),
        lax.all_gather(recall_gain_mid, "fsdp", axis=0, tiled=True),
        lax.all_gather(recall_bias_mid, "fsdp", axis=0, tiled=True),
        lax.all_gather(recall_w_in, "fsdp", axis=0, tiled=True),
        lax.all_gather(recall_w_down, "fsdp", axis=0, tiled=True),
        lax.all_gather(recall_gate, "fsdp", axis=0, tiled=True),
    )
    held_local = fetched[:9]
    held_recall = fetched[9:]
    initial = [
        jnp.zeros((param.shape[0] * fsdp_count,) + param.shape[1:], jnp.float32)
        for param in local_params + recall_params
    ]

    def step(grad_totals, slices):
        stream_in, slot_table, starts, rows_idx, grad_top = slices
        window_info = window_setup(slot_table, starts, my_index)
        memory_part = (heads_k, heads_v, rows_idx)
        first_out, first_stored = forward_layer(
            stream_in.astype(jnp.float32), held_local, window_info, None, False
        )
        second_out, second_stored = forward_layer(
            first_out, held_recall, window_info, memory_part, True
        )
        grad_middle, second_grads = backward_layer(
            grad_top.astype(jnp.float32), second_stored, held_recall, window_info, memory_part, True
        )
        grad_first, first_grads = backward_layer(
            grad_middle, first_stored, held_local, window_info, None, False
        )
        updated = [
            running + update for running, update in zip(grad_totals, first_grads + second_grads)
        ]
        return (updated, (second_out.astype(jnp.bfloat16), grad_first))

    totals, (layer_out, input_grad) = lax.scan(
        step,
        initial,
        (inputs[:, 0], block_slots[:, 0], doc_starts[:, 0], mem_index[:, 0], out_grad[:, 0]),
    )
    shards = (
        lax.psum_scatter(
            totals[0].astype(jnp.bfloat16), "fsdp", scatter_dimension=0, tiled=True
        ).astype(jnp.float32),
        lax.psum_scatter(
            totals[1].astype(jnp.bfloat16), "fsdp", scatter_dimension=0, tiled=True
        ).astype(jnp.float32),
        lax.psum_scatter(
            totals[2].astype(jnp.bfloat16), "fsdp", scatter_dimension=0, tiled=True
        ).astype(jnp.float32),
        lax.psum_scatter(
            totals[3].astype(jnp.bfloat16), "fsdp", scatter_dimension=0, tiled=True
        ).astype(jnp.float32),
        lax.psum_scatter(
            totals[4].astype(jnp.bfloat16), "fsdp", scatter_dimension=0, tiled=True
        ).astype(jnp.float32),
        lax.psum_scatter(
            totals[5].astype(jnp.bfloat16), "fsdp", scatter_dimension=0, tiled=True
        ).astype(jnp.float32),
        lax.psum_scatter(
            totals[6].astype(jnp.bfloat16), "fsdp", scatter_dimension=0, tiled=True
        ).astype(jnp.float32),
        lax.psum_scatter(
            totals[7].astype(jnp.bfloat16), "fsdp", scatter_dimension=0, tiled=True
        ).astype(jnp.float32),
        lax.psum_scatter(
            totals[8].astype(jnp.bfloat16), "fsdp", scatter_dimension=0, tiled=True
        ).astype(jnp.float32),
        lax.psum_scatter(
            totals[9].astype(jnp.bfloat16), "fsdp", scatter_dimension=0, tiled=True
        ).astype(jnp.float32),
        lax.psum_scatter(
            totals[10].astype(jnp.bfloat16), "fsdp", scatter_dimension=0, tiled=True
        ).astype(jnp.float32),
        lax.psum_scatter(
            totals[11].astype(jnp.bfloat16), "fsdp", scatter_dimension=0, tiled=True
        ).astype(jnp.float32),
        lax.psum_scatter(
            totals[12].astype(jnp.bfloat16), "fsdp", scatter_dimension=0, tiled=True
        ).astype(jnp.float32),
        lax.psum_scatter(
            totals[13].astype(jnp.bfloat16), "fsdp", scatter_dimension=0, tiled=True
        ).astype(jnp.float32),
        lax.psum_scatter(
            totals[14].astype(jnp.bfloat16), "fsdp", scatter_dimension=0, tiled=True
        ).astype(jnp.float32),
        lax.psum_scatter(
            totals[15].astype(jnp.bfloat16), "fsdp", scatter_dimension=0, tiled=True
        ).astype(jnp.float32),
        lax.psum_scatter(
            totals[16].astype(jnp.bfloat16), "fsdp", scatter_dimension=0, tiled=True
        ).astype(jnp.float32),
        lax.psum_scatter(
            totals[17].astype(jnp.bfloat16), "fsdp", scatter_dimension=0, tiled=True
        ).astype(jnp.float32),
        lax.psum_scatter(
            totals[18].astype(jnp.bfloat16), "fsdp", scatter_dimension=0, tiled=True
        ).astype(jnp.float32),
    )
    summed = (
        lax.psum(shards[0].astype(jnp.bfloat16), "ctx").astype(jnp.float32),
        lax.psum(shards[1].astype(jnp.bfloat16), "ctx").astype(jnp.float32),
        lax.psum(shards[2].astype(jnp.bfloat16), "ctx").astype(jnp.float32),
        lax.psum(shards[3].astype(jnp.bfloat16), "ctx").astype(jnp.float32),
        lax.psum(shards[4].astype(jnp.bfloat16), "ctx").astype(jnp.float32),
        lax.psum(shards[5].astype(jnp.bfloat16), "ctx").astype(jnp.float32),
        lax.psum(shards[6].astype(jnp.bfloat16), "ctx").astype(jnp.float32),
        lax.psum(shards[7].astype(jnp.bfloat16), "ctx").astype(jnp.float32),
        lax.psum(shards[8].astype(jnp.bfloat16), "ctx").astype(jnp.float32),
        lax.psum(shards[9].astype(jnp.bfloat16), "ctx").astype(jnp.float32),
        lax.psum(shards[10].astype(jnp.bfloat16), "ctx").astype(jnp.float32),
        lax.psum(shards[11].astype(jnp.bfloat16), "ctx").astype(jnp.float32),
        lax.psum(shards[12].astype(jnp.bfloat16), "ctx").astype(jnp.float32),
        lax.psum(shards[13].astype(jnp.bfloat16), "ctx").astype(jnp.float32),
        lax.psum(shards[14].astype(jnp.bfloat16), "ctx").astype(jnp.float32),
        lax.psum(shards[15].astype(jnp.bfloat16), "ctx").astype(jnp.float32),
        lax.psum(shards[16].astype(jnp.bfloat16), "ctx").astype(jnp.float32),
        lax.psum(shards[17].astype(jnp.bfloat16), "ctx").astype(jnp.float32),
        lax.psum(shards[18].astype(jnp.bfloat16), "ctx").astype(jnp.float32),
    )
    return (
        layer_out[:, None],
        input_grad[:, None],
        summed[0],
        summed[1],
        summed[2],
        summed[3],
        summed[4],
        summed[5],
        summed[6],
        summed[7],
        summed[8],
        summed[9],
        summed[10],
        summed[11],
        summed[12],
        summed[13],
        summed[14],
        summed[15],
        summed[16],
        summed[17],
        summed[18],
    )


def solution(mesh):
    placed = (
        P(None, "fsdp", "ctx", None),
        P(None, "fsdp", None),
        P(None, "fsdp", None),
        P(None, "fsdp", "ctx", None, None),
        P("fsdp", "ctx", None),
        P("fsdp", "ctx", None),
        P(None, "fsdp", "ctx", None),
        P("fsdp"),
        P("fsdp"),
        P("fsdp", None),
        P("fsdp", None),
        P("fsdp", None),
        P("fsdp"),
        P("fsdp"),
        P("fsdp", None),
        P("fsdp", None),
        P("fsdp"),
        P("fsdp"),
        P("fsdp", None),
        P("fsdp", None),
        P("fsdp", None),
        P("fsdp"),
        P("fsdp"),
        P("fsdp", None),
        P("fsdp", None),
        P("fsdp"),
    )
    return jax.shard_map(
        local,
        mesh=mesh,
        in_specs=placed,
        out_specs=(
            P(None, "fsdp", "ctx", None),
            P(None, "fsdp", "ctx", None),
            P("fsdp"),
            P("fsdp"),
            P("fsdp", None),
            P("fsdp", None),
            P("fsdp", None),
            P("fsdp"),
            P("fsdp"),
            P("fsdp", None),
            P("fsdp", None),
            P("fsdp"),
            P("fsdp"),
            P("fsdp", None),
            P("fsdp", None),
            P("fsdp", None),
            P("fsdp"),
            P("fsdp"),
            P("fsdp", None),
            P("fsdp", None),
            P("fsdp"),
        ),
        check_vma=False,
    )
```

profile of v0, /device:TPU:0, one launch (start us, length us, event | category | flops | bytes accessed | tf_op | source)
XLA Modules:
  0.0 3363.8 jit_solution(6479216988751754711)
XLA Ops:
  124.3 20.1 all-gather.29.cloned.1.call-done
  144.4 37.0 %all-gather.37.cloned.1.call-done = bf16[1024,1024]{1,0:T(8,128)(2,1)} async-done(((bf16[256,1024]{1,0:T(8,128)(2,1)}), bf16[1024,1024]{1,0:T(8,128)(2,1)}) %all-gather.37.cloned.1.call-update) | async-done | bytes 2097168 | tf_op jit(solution)/shard_map/all_gather | solution.py:419
  181.4 71.9 %all-gather.25.cloned.1.call-done = bf16[1024,3072]{1,0:T(8,128)(2,1)} async-done(((bf16[256,3072]{1,0:T(8,128)(2,1)}), bf16[1024,3072]{1,0:T(8,128)(2,1)}) %all-gather.25.cloned.1.call-update) | async-done | bytes 6291472 | tf_op jit(solution)/shard_map/all_gather | solution.py:408
  253.3 71.9 %all-gather.35.cloned.1.call-done = bf16[1024,3072]{1,0:T(8,128)(2,1)} async-done(((bf16[256,3072]{1,0:T(8,128)(2,1)}), bf16[1024,3072]{1,0:T(8,128)(2,1)}) %all-gather.35.cloned.1.call-update) | async-done | bytes 6291472 | tf_op jit(solution)/shard_map/all_gather | solution.py:417
  325.2 89.5 %all-gather.27.cloned.1.call-done = bf16[4096,1024]{1,0:T(8,128)(2,1)} async-done(((bf16[1024,1024]{1,0:T(8,128)(2,1)}), bf16[4096,1024]{1,0:T(8,128)(2,1)}) %all-gather.27.cloned.1.call-update) | async-done | bytes 8388624 | tf_op jit(solution)/shard_map/all_gather | solution.py:423
  414.7 89.5 %all-gather.31.cloned.1.call-done = bf16[1024,4096]{1,0:T(8,128)(2,1)} async-done(((bf16[256,4096]{1,0:T(8,128)(2,1)}), bf16[1024,4096]{1,0:T(8,128)(2,1)}) %all-gather.31.cloned.1.call-update) | async-done | bytes 8388624 | tf_op jit(solution)/shard_map/all_gather | solution.py:413
  504.2 89.5 %all-gather.33.cloned.1.call-done = bf16[4096,1024]{1,0:T(8,128)(2,1)} async-done(((bf16[1024,1024]{1,0:T(8,128)(2,1)}), bf16[4096,1024]{1,0:T(8,128)(2,1)}) %all-gather.33.cloned.1.call-update) | async-done | bytes 8388624 | tf_op jit(solution)/shard_map/all_gather | solution.py:414
  593.7 89.3 %all-gather.39.cloned.1.call-done = bf16[1024,4096]{1,0:T(8,128)(2,1)} async-done(((bf16[256,4096]{1,0:T(8,128)(2,1)}), bf16[1024,4096]{1,0:T(8,128)(2,1)}) %all-gather.39.cloned.1.call-update) | async-done | bytes 8388624 | tf_op jit(solution)/shard_map/all_gather | solution.py:422
  683.0 1812.1 %while.107 = (s32[]{:T(128)}, f32[1024]{0:T(1024)}, f32[1024]{0:T(1024)}, f32[1024,3072]{1,0:T(8,128)}, f32[8,32]{1,0:T(8,128)}, /*index=5*/f32[1024,1024]{1,0:T...) while((s32[]{:T(128)}, f32[1024]{0:T(1024)}, ...), condition=%wide.region_52.53_spmd.clone.clone, body=%wide.region_0.52_spmd.sunk.clone.clone.sunk | while | flops 44186148864 | bytes 1675290880 | solution.py:454
  710.7 64.5 %all-gather.45.cloned.1.call-done = bf16[2048,2048]{1,0:T(8,128)(2,1)} async-done(((bf16[256,2048]{1,0:T(8,128)(2,1)}), bf16[2048,2048]{1,0:T(8,128)(2,1)}) %all-gather.45.cloned.1.call-update) | async-done | bytes 8388624 | tf_op jit(solution)/shard_map/while/body/eval_jaxpr/all_gather | solution.py:279
  832.3 191.2 %while.108 = (s32[]{:T(128)}, f32[8,256,128]{2,0,1:T(8,128)}, s32[8,256,32]{2,1,0:T(8,128)}, bf16[8,256,128]{2,1,0:T(8,128)(2,1)}, bf16[8,2048,128]{2,1,0:T(8,12...) while((s32[]{:T(128)}, f32[8,256,128]{2,0,1:T(8,128)}, s32[8,256,32]{2,1,0:T(8,128)}, ...), condition=%wide.region_16.16_spmd, body=%wide.region_12.15_spmd.sunk | while | flops 467172864 | bytes 21275740 | solution.py:194
  833.4 12.2 convert_reduce_fusion.19
  857.2 12.2 convert_reduce_fusion.19
  881.2 12.2 convert_reduce_fusion.19
  905.0 12.2 convert_reduce_fusion.19
  928.9 12.2 convert_reduce_fusion.19
  952.8 12.2 convert_reduce_fusion.19
  976.6 12.2 convert_reduce_fusion.19
  1000.5 12.2 convert_reduce_fusion.19
  1152.8 21.3 scatter_fusion
  1183.3 175.5 %while.109 = (s32[]{:T(128)}, f32[8,256,128]{1,2,0:T(8,128)}, s32[8,256,32]{2,1,0:T(8,128)}, bf16[8,256,128]{2,1,0:T(8,128)(2,1)}, bf16[8,2048,128]{2,1,0:T(8,12...) while((s32[]{:T(128)}, f32[8,256,128]{1,2,0:T(8,128)}, ...), condition=%wide.region_29.29_spmd, body=%wide.region_24.28_spmd.sunk | while | flops 603520256 | bytes 33665624 | solution.py:272
  1184.2 12.2 convert_reduce_fusion.20
  1206.1 12.2 convert_reduce_fusion.20
  1228.1 12.2 convert_reduce_fusion.20
  1250.0 12.2 convert_reduce_fusion.20
  1271.9 12.2 convert_reduce_fusion.20
  1293.8 12.2 convert_reduce_fusion.20
  1315.7 12.2 convert_reduce_fusion.20
  1337.6 12.2 convert_reduce_fusion.20
  1446.8 21.3 scatter_fusion.1
  1543.7 22.9 reduce-scatter.29.cloned.1.call-done
  1613.3 62.9 %all-gather.45.cloned.1.call-done = bf16[2048,2048]{1,0:T(8,128)(2,1)} async-done(((bf16[256,2048]{1,0:T(8,128)(2,1)}), bf16[2048,2048]{1,0:T(8,128)(2,1)}) %all-gather.45.cloned.1.call-update) | async-done | bytes 8388624 | tf_op jit(solution)/shard_map/while/body/eval_jaxpr/all_gather | solution.py:279
  1732.9 191.2 %while.108 = (s32[]{:T(128)}, f32[8,256,128]{2,0,1:T(8,128)}, s32[8,256,32]{2,1,0:T(8,128)}, bf16[8,256,128]{2,1,0:T(8,128)(2,1)}, bf16[8,2048,128]{2,1,0:T(8,12...) while((s32[]{:T(128)}, f32[8,256,128]{2,0,1:T(8,128)}, s32[8,256,32]{2,1,0:T(8,128)}, ...), condition=%wide.region_16.16_spmd, body=%wide.region_12.15_spmd.sunk | while | flops 467172864 | bytes 21275740 | solution.py:194
  2053.3 21.0 scatter_fusion
  2083.4 175.6 %while.109 = (s32[]{:T(128)}, f32[8,256,128]{1,2,0:T(8,128)}, s32[8,256,32]{2,1,0:T(8,128)}, bf16[8,256,128]{2,1,0:T(8,128)(2,1)}, bf16[8,2048,128]{2,1,0:T(8,12...) while((s32[]{:T(128)}, f32[8,256,128]{1,2,0:T(8,128)}, ...), condition=%wide.region_29.29_spmd, body=%wide.region_24.28_spmd.sunk | while | flops 603520256 | bytes 33665624 | solution.py:272
  2347.3 21.0 scatter_fusion.1
  2393.5 14.4 select_add_fusion.38
  2441.5 14.4 select_add_fusion.32
  2558.0 15.4 reduce-scatter.21.cloned.1.call-done
  2573.5 73.2 %reduce-scatter.11.cloned.1.call-done = bf16[256,3072]{1,0:T(8,128)(2,1)} async-done(((bf16[1024,3072]{1,0:T(8,128)(2,1)}), bf16[256,3072]{1,0:T(8,128)(2,1)}) %reduce-scatter.11.cloned.1.call-update) | async-done | bytes 1572880 | tf_op jit(solution)/shard_map/reduce_scatter | solution.py:466
  2646.7 73.2 %reduce-scatter.19.cloned.1.call-done = bf16[256,3072]{1,0:T(8,128)(2,1)} async-done(((bf16[1024,3072]{1,0:T(8,128)(2,1)}), bf16[256,3072]{1,0:T(8,128)(2,1)}) %reduce-scatter.19.cloned.1.call-update) | async-done | bytes 1572880 | tf_op jit(solution)/shard_map/reduce_scatter | solution.py:493
  2719.9 89.5 %reduce-scatter.15.cloned.1.call-done = bf16[256,4096]{1,0:T(8,128)(2,1)} async-done(((bf16[1024,4096]{1,0:T(8,128)(2,1)}), bf16[256,4096]{1,0:T(8,128)(2,1)}) %reduce-scatter.15.cloned.1.call-update) | async-done | bytes 2097168 | tf_op jit(solution)/shard_map/reduce_scatter | solution.py:481
  2809.4 89.6 %reduce-scatter.17.cloned.1.call-done = bf16[1024,1024]{1,0:T(8,128)(2,1)} async-done(((bf16[4096,1024]{1,0:T(8,128)(2,1)}), bf16[1024,1024]{1,0:T(8,128)(2,1)}) %reduce-scatter.17.cloned.1.call-update) | async-done | bytes 2097168 | tf_op jit(solution)/shard_map/reduce_scatter | solution.py:484
  2899.0 89.5 %reduce-scatter.23.cloned.1.call-done = bf16[256,4096]{1,0:T(8,128)(2,1)} async-done(((bf16[1024,4096]{1,0:T(8,128)(2,1)}), bf16[256,4096]{1,0:T(8,128)(2,1)}) %reduce-scatter.23.cloned.1.call-update) | async-done | bytes 2097168 | tf_op jit(solution)/shard_map/reduce_scatter | solution.py:508
  2988.5 89.6 %reduce-scatter.25.cloned.1.call-done = bf16[1024,1024]{1,0:T(8,128)(2,1)} async-done(((bf16[4096,1024]{1,0:T(8,128)(2,1)}), bf16[1024,1024]{1,0:T(8,128)(2,1)}) %reduce-scatter.25.cloned.1.call-update) | async-done | bytes 2097168 | tf_op jit(solution)/shard_map/reduce_scatter | solution.py:511
  3079.6 15.3 all-reduce.14
  3095.7 14.7 all-reduce.12
  3116.5 222.3 %all-reduce.17.cloned.1.call-done = (bf16[256,3072]{1,0:T(8,128)(2,1)}, bf16[256,1024]{1,0:T(8,128)(2,1)}, bf16[256,4096]{1,0:T(8,128)(2,1)}, bf16[1024,1024]{1,...) async-done(((bf16[256,3072]{1,0:T(8,128)(2,1)}, bf16[256,1024]{1,0:T(8,128)(2,1)}, ...) | async-done | bytes 12582928 | tf_op jit(solution)/shard_map/psum | solution.py:521
  (1402 shorter events, 1545.5 us)
Async XLA Ops:
  7.2 104.2 %all-gather.41.cloned.1.call-start = ((), (), s32[]{:S(2)}) async-start(), calls=%async_computation.26 | async-start | bytes 4718592 | tf_op jit(solution)/shard_map/all_gather | solution.py:377
  9.3 108.6 %all-gather.43.cloned.1.call-start = ((), (), s32[]{:S(2)}) async-start(), calls=%async_computation.27 | async-start | bytes 4718592 | tf_op jit(solution)/shard_map/all_gather | solution.py:378
  11.4 133.0 %all-gather.29.cloned.1.call-start = ((), (), s32[]{:S(2)}) async-start(), calls=%async_computation.12 | async-start | bytes 2621440 | tf_op jit(solution)/shard_map/all_gather | solution.py:410
  12.2 169.3 %all-gather.37.cloned.1.call-start = ((), (), s32[]{:S(2)}) async-start(), calls=%async_computation.16 | async-start | bytes 2621440 | tf_op jit(solution)/shard_map/all_gather | solution.py:419
  12.7 240.6 %all-gather.25.cloned.1.call-start = ((), (), s32[]{:S(2)}) async-start(), calls=%async_computation.10 | async-start | bytes 7864320 | tf_op jit(solution)/shard_map/all_gather | solution.py:408
  13.3 311.9 %all-gather.35.cloned.1.call-start = ((), (), s32[]{:S(2)}) async-start(), calls=%async_computation.15 | async-start | bytes 7864320 | tf_op jit(solution)/shard_map/all_gather | solution.py:417
  13.9 400.8 %all-gather.27.cloned.1.call-start = ((), (), s32[]{:S(2)}) async-start(), calls=%async_computation.11 | async-start | bytes 10485760 | tf_op jit(solution)/shard_map/all_gather | solution.py:423
  14.8 80.8 %copy-start.149 = (bf16[2,32]{1,0:T(2,128)(2,1)S(1)}, bf16[2,32]{1,0:T(2,128)(2,1)}, u32[]{:S(2)}) copy-start(bf16[2,32]{1,0:T(2,128)(2,1)} %param.44) | copy-start | bytes 388
  14.8 88.4 %copy-start.150 = (bf16[2,32]{1,0:T(2,128)(2,1)S(1)}, bf16[2,32]{1,0:T(2,128)(2,1)}, u32[]{:S(2)}) copy-start(bf16[2,32]{1,0:T(2,128)(2,1)} %param.53) | copy-start | bytes 388
  14.8 489.4 %all-gather.31.cloned.1.call-start = ((), (), s32[]{:S(2)}) async-start(), calls=%async_computation.13 | async-start | bytes 10485760 | tf_op jit(solution)/shard_map/all_gather | solution.py:413
  15.6 578.1 %all-gather.33.cloned.1.call-start = ((), (), s32[]{:S(2)}) async-start(), calls=%async_computation.14 | async-start | bytes 10485760 | tf_op jit(solution)/shard_map/all_gather | solution.py:414
  16.3 666.7 %all-gather.39.cloned.1.call-start = ((), (), s32[]{:S(2)}) async-start(), calls=%async_computation.17 | async-start | bytes 10485760 | tf_op jit(solution)/shard_map/all_gather | solution.py:422
  117.9 565.1 %copy-start.140 = (s32[2,1,16]{2,1,0:T(1,128)S(1)}, s32[2,1,16]{2,1,0:T(1,128)}, u32[]{:S(2)}) copy-start(s32[2,1,16]{2,1,0:T(1,128)} %param.35) | copy-start | bytes 388
  683.0 92.2 %all-gather.45.cloned.1.call-start = ((), (), s32[]{:S(2)}) async-start(), calls=%async_computation.29 | async-start | bytes 9437184 | tf_op jit(solution)/shard_map/while/body/eval_jaxpr/all_gather | solution.py:279
  693.0 330.4 %all-gather.47.cloned.1.call-start = ((), (), s32[]{:S(2)}) async-start(), calls=%async_computation.30 | async-start | bytes 9437184 | tf_op jit(solution)/shard_map/while/body/eval_jaxpr/all_gather | solution.py:176
  693.9 102.9 %copy-start.34 = (bf16[2,128,8,128]{1,3,2,0:T(8,128)(2,1)}, bf16[2,128,8,128]{1,3,2,0:T(8,128)(2,1)S(1)}, u32[]{:S(2)}) copy-start(bf16[2,128,8,128]{1,3,2,0:T(8,128)(2,1)S(1)} %copy.345) | copy-start | bytes 1572868 | tf_op jit(solution)/shard_map/while
  700.2 111.5 %copy-start.55 = (f32[1024]{0:T(1024)}, f32[1024]{0:T(1024)S(1)}, u32[]{:S(2)}) copy-start(f32[1024]{0:T(1024)S(1)} %convert_element_type.1064) | copy-start | bytes 12292 | tf_op jit(solution)/shard_map/while
  700.2 111.5 %copy-start.62 = (f32[1024]{0:T(1024)}, f32[1024]{0:T(1024)S(1)}, u32[]{:S(2)}) copy-start(f32[1024]{0:T(1024)S(1)} %convert_element_type.1063) | copy-start | bytes 12292 | tf_op jit(solution)/shard_map/while
  700.9 120.1 %copy-start.57 = (f32[1024]{0:T(1024)}, f32[1024]{0:T(1024)S(1)}, u32[]{:S(2)}) copy-start(f32[1024]{0:T(1024)S(1)} %convert_element_type.1065) | copy-start | bytes 12292 | tf_op jit(solution)/shard_map/while
  701.6 119.4 %copy-start.64 = (f32[1024]{0:T(1024)}, f32[1024]{0:T(1024)S(1)}, u32[]{:S(2)}) copy-start(f32[1024]{0:T(1024)S(1)} %convert_element_type.1066) | copy-start | bytes 12292 | tf_op jit(solution)/shard_map/while
  704.7 376.4 %copy-start.59 = (f32[1024]{0:T(1024)}, f32[1024]{0:T(1024)S(1)}, u32[]{:S(2)}) copy-start(f32[1024]{0:T(1024)S(1)} %convert_element_type.1067) | copy-start | bytes 12292 | tf_op jit(solution)/shard_map/while
  704.8 353.5 %copy-start.66 = (f32[1024]{0:T(1024)}, f32[1024]{0:T(1024)S(1)}, u32[]{:S(2)}) copy-start(f32[1024]{0:T(1024)S(1)} %convert_element_type.1068) | copy-start | bytes 12292 | tf_op jit(solution)/shard_map/while
  710.4 373.2 %copy-start.124 = (f32[8]{0:T(128)}, f32[8]{0:T(128)S(1)}, u32[]{:S(2)}) copy-start(f32[8]{0:T(128)S(1)} %get-tuple-element.2128) | copy-start | bytes 100 | tf_op jit(solution)/shard_map/while
  827.8 534.9 %reduce-scatter.27.cloned.1.call-start = ((), (), s32[]{:S(2)}) async-start(), calls=%async_computation.31 | async-start | bytes 9437184 | tf_op jit(solution)/shard_map/while/body/eval_jaxpr/reduce_scatter | solution.py:313
  830.1 214.8 %copy-start.39 = (bf16[2,128,8,128]{1,3,2,0:T(8,128)(2,1)}, bf16[2,128,8,128]{1,3,2,0:T(8,128)(2,1)S(1)}, u32[]{:S(2)}) copy-start(bf16[2,128,8,128]{1,3,2,0:T(8,128)(2,1)S(1)} %copy.350) | copy-start | bytes 1572868 | tf_op jit(solution)/shard_map/while
  1183.2 383.4 %reduce-scatter.29.cloned.1.call-start = ((), (), s32[]{:S(2)}) async-start(), calls=%async_computation.32 | async-start | bytes 9437184 | tf_op jit(solution)/shard_map/while/body/eval_jaxpr/reduce_scatter | solution.py:313
  1585.7 90.5 %all-gather.45.cloned.1.call-start = ((), (), s32[]{:S(2)}) async-start(), calls=%async_computation.29 | async-start | bytes 9437184 | tf_op jit(solution)/shard_map/while/body/eval_jaxpr/all_gather | solution.py:279
  1595.7 328.4 %all-gather.47.cloned.1.call-start = ((), (), s32[]{:S(2)}) async-start(), calls=%async_computation.30 | async-start | bytes 9437184 | tf_op jit(solution)/shard_map/while/body/eval_jaxpr/all_gather | solution.py:176
  1596.6 101.2 %copy-start.34 = (bf16[2,128,8,128]{1,3,2,0:T(8,128)(2,1)}, bf16[2,128,8,128]{1,3,2,0:T(8,128)(2,1)S(1)}, u32[]{:S(2)}) copy-start(bf16[2,128,8,128]{1,3,2,0:T(8,128)(2,1)S(1)} %copy.345) | copy-start | bytes 1572868 | tf_op jit(solution)/shard_map/while
  1602.8 109.5 %copy-start.55 = (f32[1024]{0:T(1024)}, f32[1024]{0:T(1024)S(1)}, u32[]{:S(2)}) copy-start(f32[1024]{0:T(1024)S(1)} %convert_element_type.1064) | copy-start | bytes 12292 | tf_op jit(solution)/shard_map/while
  1602.8 109.5 %copy-start.62 = (f32[1024]{0:T(1024)}, f32[1024]{0:T(1024)S(1)}, u32[]{:S(2)}) copy-start(f32[1024]{0:T(1024)S(1)} %convert_element_type.1063) | copy-start | bytes 12292 | tf_op jit(solution)/shard_map/while
  1603.5 118.0 %copy-start.57 = (f32[1024]{0:T(1024)}, f32[1024]{0:T(1024)S(1)}, u32[]{:S(2)}) copy-start(f32[1024]{0:T(1024)S(1)} %convert_element_type.1065) | copy-start | bytes 12292 | tf_op jit(solution)/shard_map/while
  1604.2 117.4 %copy-start.64 = (f32[1024]{0:T(1024)}, f32[1024]{0:T(1024)S(1)}, u32[]{:S(2)}) copy-start(f32[1024]{0:T(1024)S(1)} %convert_element_type.1066) | copy-start | bytes 12292 | tf_op jit(solution)/shard_map/while
  1607.4 374.5 %copy-start.59 = (f32[1024]{0:T(1024)}, f32[1024]{0:T(1024)S(1)}, u32[]{:S(2)}) copy-start(f32[1024]{0:T(1024)S(1)} %convert_element_type.1067) | copy-start | bytes 12292 | tf_op jit(solution)/shard_map/while
  1607.4 351.6 %copy-start.66 = (f32[1024]{0:T(1024)}, f32[1024]{0:T(1024)S(1)}, u32[]{:S(2)}) copy-start(f32[1024]{0:T(1024)S(1)} %convert_element_type.1068) | copy-start | bytes 12292 | tf_op jit(solution)/shard_map/while
  1613.0 371.4 %copy-start.124 = (f32[8]{0:T(128)}, f32[8]{0:T(128)S(1)}, u32[]{:S(2)}) copy-start(f32[8]{0:T(128)S(1)} %get-tuple-element.2128) | copy-start | bytes 100 | tf_op jit(solution)/shard_map/while
  1728.4 534.5 %reduce-scatter.27.cloned.1.call-start = ((), (), s32[]{:S(2)}) async-start(), calls=%async_computation.31 | async-start | bytes 9437184 | tf_op jit(solution)/shard_map/while/body/eval_jaxpr/reduce_scatter | solution.py:313
  1730.7 214.8 %copy-start.39 = (bf16[2,128,8,128]{1,3,2,0:T(8,128)(2,1)}, bf16[2,128,8,128]{1,3,2,0:T(8,128)(2,1)S(1)}, u32[]{:S(2)}) copy-start(bf16[2,128,8,128]{1,3,2,0:T(8,128)(2,1)S(1)} %copy.350) | copy-start | bytes 1572868 | tf_op jit(solution)/shard_map/while
  2083.4 384.2 %reduce-scatter.29.cloned.1.call-start = ((), (), s32[]{:S(2)}) async-start(), calls=%async_computation.32 | async-start | bytes 9437184 | tf_op jit(solution)/shard_map/while/body/eval_jaxpr/reduce_scatter | solution.py:313
  2495.2 62.9 %reduce-scatter.13.cloned.1.call-start = ((), (), s32[]{:S(2)}) async-start(), calls=%async_computation.19 | async-start | bytes 2621440 | tf_op jit(solution)/shard_map/reduce_scatter | solution.py:472
  2499.1 74.4 %reduce-scatter.21.cloned.1.call-start = ((), (), s32[]{:S(2)}) async-start(), calls=%async_computation.23 | async-start | bytes 2621440 | tf_op jit(solution)/shard_map/reduce_scatter | solution.py:499
  2503.0 143.7 %reduce-scatter.11.cloned.1.call-start = ((), (), s32[]{:S(2)}) async-start(), calls=%async_computation.18 | async-start | bytes 7864320 | tf_op jit(solution)/shard_map/reduce_scatter | solution.py:466
  2511.7 208.2 %reduce-scatter.19.cloned.1.call-start = ((), (), s32[]{:S(2)}) async-start(), calls=%async_computation.22 | async-start | bytes 7864320 | tf_op jit(solution)/shard_map/reduce_scatter | solution.py:493
  2520.4 289.0 %reduce-scatter.15.cloned.1.call-start = ((), (), s32[]{:S(2)}) async-start(), calls=%async_computation.20 | async-start | bytes 10485760 | tf_op jit(solution)/shard_map/reduce_scatter | solution.py:481
  2529.6 369.4 %reduce-scatter.17.cloned.1.call-start = ((), (), s32[]{:S(2)}) async-start(), calls=%async_computation.21 | async-start | bytes 10485760 | tf_op jit(solution)/shard_map/reduce_scatter | solution.py:484
  2538.9 449.6 %reduce-scatter.23.cloned.1.call-start = ((), (), s32[]{:S(2)}) async-start(), calls=%async_computation.24 | async-start | bytes 10485760 | tf_op jit(solution)/shard_map/reduce_scatter | solution.py:508
  2548.3 529.8 %reduce-scatter.25.cloned.1.call-start = ((), (), s32[]{:S(2)}) async-start(), calls=%async_computation.25 | async-start | bytes 10485760 | tf_op jit(solution)/shard_map/reduce_scatter | solution.py:511
  2558.0 780.8 %all-reduce.17.cloned.1.call-start = ((), (), s32[]{:S(2)}) async-start(), calls=%async_computation.28 | async-start | bytes 25165824 | tf_op jit(solution)/shard_map/psum | solution.py:521
  (299 other events, 2165.7 us)
Sparse Core Ops, SparseCore 0:
  10.2 52.1 all-gather.40
  64.6 44.3 all-gather.42
  110.8 33.5 all-gather.28
  146.1 35.2 all-gather.36
  183.1 70.1 all-gather.24
  255.0 70.1 all-gather.34
  327.1 87.5 all-gather.26
  416.5 87.5 all-gather.30
  506.0 87.5 all-gather.32
  595.4 87.5 all-gather.38
  693.2 82.0 all-gather.44
  827.9 80.6 all-gather.46
  1183.3 88.3 reduce-scatter.26
  1477.8 88.7 reduce-scatter.28
  1595.8 80.3 all-gather.44
  1728.5 80.6 all-gather.46
  2083.5 88.6 reduce-scatter.26
  2377.7 89.2 reduce-scatter.28
  2499.5 34.9 reduce-scatter.12
  2538.2 35.1 reduce-scatter.20
  2576.4 70.1 reduce-scatter.10
  2649.6 70.2 reduce-scatter.18
  2723.0 86.3 reduce-scatter.14
  2812.6 86.3 reduce-scatter.16
  2902.1 86.3 reduce-scatter.22
  2991.7 86.3 reduce-scatter.24
  3081.0 257.7 all-reduce.16
where the time goes:
time: 3380 us; the launch traced here: 3360 us
  waiting for transfers between devices  1460 us (43%)
  other arithmetic  729 us (22%)
  matrix products  577 us (17%)
  local copies, waits for them, and re-layouts  454 us (13%)
  blocking collectives  118 us (3%)
    reduce_sum x32, other arithmetic, recall_weights(): jnp.sum((index_head[:, :, None] == jnp.arange(row_count, dtype=jnp.int32)...  389 us
    psum x1, waiting for transfers between devices, local(): lax.psum(shards[2].astype(jnp.bfloat16), 'ctx').astype(jnp.float32)  222 us
    all_gather x2, waiting for transfers between devices, backward_layer(): lax.all_gather(qkv_low[:, model_width:], 'ctx', axis=0, tiled=True)  127 us
    reduce_scatter x1, waiting for transfers between devices, local(): lax.psum_scatter(totals[17].astype(jnp.bfloat16), 'fsdp', scatter_dimensi...  89.6 us
    reduce_scatter x1, waiting for transfers between devices, local(): lax.psum_scatter(totals[8].astype(jnp.bfloat16), 'fsdp', scatter_dimensio...  89.6 us
    reduce_scatter x1, waiting for transfers between devices, local(): lax.psum_scatter(totals[7].astype(jnp.bfloat16), 'fsdp', scatter_dimensio...  89.5 us
    all_gather x1, waiting for transfers between devices, local(): lax.all_gather(local_w_down, 'fsdp', axis=0, tiled=True)  89.5 us
    reduce_scatter x1, waiting for transfers between devices, local(): lax.psum_scatter(totals[16].astype(jnp.bfloat16), 'fsdp', scatter_dimensi...  89.5 us
  transfers between devices with their start and end apart: 27, of which 19 were waited for; matrix products, arithmetic and copies ran while one was open for 30% of the time, Pallas kernels for 0%

commit v1 on v0

v1 whole, which is shorter than its diff:
```python
import functools
import math

import jax
import jax.numpy as jnp
import numpy as np
from jax import lax
from jax.experimental import pallas as pl
from jax.experimental.pallas import tpu as pltpu
from jax.sharding import PartitionSpec as P

HEADS = 8
HD = 128
BUCKETS = 32
WIN = 512
BLK = 128
TOPK = 32
SPAN = WIN + BLK
ROWS = 2 * BLK
LINE = 4
EPS = 1e-05
NEG = -1000000000.0
FAR_DISTANCE = 128
SCALE = HD ** (-0.5)
F32 = jnp.float32
BF16 = jnp.bfloat16
MIB = 1 << 20


def bucket_table(total_count, buckets):
    exact_count = buckets // 2
    result = []
    for distance in range(total_count):
        if distance < exact_count:
            result.append(distance)
        else:
            scaled = math.log(distance / exact_count) / math.log(FAR_DISTANCE / exact_count)
            result.append(min(exact_count + int(scaled * (buckets - exact_count)), buckets - 1))
    return np.array(result, dtype=np.int32)


def window_buckets():
    distance = WIN + np.arange(BLK)[:, None] - np.arange(SPAN)[None, :]
    inside = (distance >= 0) & (distance < WIN)
    buckets = bucket_table(WIN, BUCKETS)[np.clip(distance, 0, WIN - 1)]
    return np.where(inside, buckets, -1).astype(np.int32)


def dot(a, b):
    return lax.dot_general(a, b, (((1,), (0,)), ((), ())), preferred_element_type=F32)


def dot_nt(a, b):
    return lax.dot_general(a, b, (((1,), (1,)), ((), ())), preferred_element_type=F32)


def dot_tn(a, b):
    return lax.dot_general(a, b, (((0,), (0,)), ((), ())), preferred_element_type=F32)


def params(mib):
    return pltpu.CompilerParams(vmem_limit_bytes=mib * MIB)


def cost(flops, nbytes):
    return pl.CostEstimate(flops=int(flops), bytes_accessed=int(nbytes), transcendentals=0)


def vmem():
    return pl.BlockSpec(memory_space=pltpu.VMEM)


def smem():
    return pl.BlockSpec(memory_space=pltpu.SMEM)


def anyspace():
    return pl.BlockSpec(memory_space=pl.ANY)


def shape(dims, kind):
    return jax.ShapeDtypeStruct(tuple(dims), kind)


def whole(dims):
    zeros = (0,) * len(dims)
    return pl.BlockSpec(tuple(dims), lambda *_: zeros)


def single(dims):
    zeros = (0,) * len(dims)
    return pl.BlockSpec(tuple(dims), lambda _: zeros)


def xor_perm(count, bit):
    return [(i, i ^ bit) for i in range(count)]


def bit_list(count):
    bits = []
    bit = 1
    while bit < count:
        bits.append(bit)
        bit *= 2
    return bits


def swap_ctx(x, bit):
    return lax.ppermute(x, "ctx", xor_perm(lax.axis_size("ctx"), bit))


def swap_fsdp(x, bit):
    return lax.ppermute(x, "fsdp", xor_perm(lax.axis_size("fsdp"), bit))


def exchange(x):
    return lax.all_to_all(x, "ctx", 0, 0, tiled=False)


def side_columns(side, half):
    return pl.ds(pl.multiple_of(side * half, HD), half)


def pack_kernel(plan, key, *refs):
    weights, out, held, sems = refs[:-3], refs[-3], refs[-2], refs[-1]
    copies = []
    for n, (i, row, rows, half, to_row, to_column) in enumerate(plan):
        copies.append(
            pltpu.make_async_copy(
                weights[i].at[row : row + rows, side_columns(key[0], half)],
                held.at[to_row : to_row + rows, to_column : to_column + half],
                sems.at[n],
            )
        )
    for copy in copies:
        copy.start()
    for copy in copies:
        copy.wait()
    last = pltpu.make_async_copy(held, out, sems.at[len(plan)])
    last.start()
    last.wait()


def pack(weights, plan, rows, core):
    columns = max(to_column + half for *_, half, _, to_column in plan)
    dims = (rows, columns)
    return pl.pallas_call(
        functools.partial(pack_kernel, plan),
        in_specs=[smem()] + [anyspace()] * len(weights),
        out_specs=anyspace(),
        out_shape=shape(dims, BF16),
        scratch_shapes=[pltpu.VMEM(dims, BF16), pltpu.SemaphoreType.DMA((len(plan) + 1,))],
        compiler_params=params(56),
        cost_estimate=cost(0, 4 * rows * columns),
        name="pack",
    )(core, *weights)


def unfold_kernel(count, plan, shards, key, mine, twin, *refs):
    total = len(shards)
    outs, held, arrive, leave = refs[:total], refs[total : 2 * total], refs[-2], refs[-1]
    groups, n = [], 0
    for i, shard in enumerate(shards):
        for f in range(count):
            copies = []
            for j, row, rows, half, from_row, from_column in plan:
                if j != i:
                    continue
                for ref, side in ((mine, key[0]), (twin, 1 - key[0])):
                    copies.append(
                        pltpu.make_async_copy(
                            ref.at[f, from_row : from_row + rows, from_column : from_column + half],
                            held[i].at[
                                f * shard + row : f * shard + row + rows, side_columns(side, half)
                            ],
                            arrive.at[n],
                        )
                    )
                    n += 1
            span = slice(f * shard, (f + 1) * shard)
            groups.append(
                (copies, pltpu.make_async_copy(held[i].at[span], outs[i].at[span], leave.at[len(groups)]))
            )
    for copies, _ in groups:
        for copy in copies:
            copy.start()
    for copies, last in groups:
        for copy in copies:
            copy.wait()
        last.start()
    for _, last in groups:
        last.wait()


def unfold_weights(mine, weights, plan, core):
    count = lax.axis_size("fsdp")
    twin = swap_ctx(mine, 1)
    shards = [w.shape[0] for w in weights]
    full = [(w.shape[0] * count, w.shape[1]) for w in weights]
    return pl.pallas_call(
        functools.partial(unfold_kernel, count, plan, shards),
        out_shape=[shape(dims, BF16) for dims in full],
        in_specs=[smem(), anyspace(), anyspace()],
        out_specs=[anyspace()] * len(full),
        scratch_shapes=[pltpu.VMEM(dims, BF16) for dims in full]
        + [
            pltpu.SemaphoreType.DMA((2 * count * len(plan),)),
            pltpu.SemaphoreType.DMA((count * len(full),)),
        ],
        compiler_params=params(60),
        cost_estimate=cost(0, 8 * mine.size),
        name="unfold",
    )(core, mine, twin)


def merge(mine, twin, plan, dims, core):
    half = len(mine)

    def body(key, *refs):
        first, second, outs = refs[:half], refs[half : 2 * half], refs[2 * half :]
        for source, side in ((first, key[0]), (second, 1 - key[0])):
            for i, row, rows, width, n, from_row, from_column, offset, size in plan:
                column = pl.multiple_of(side * width + offset, HD)
                outs[i][row : row + rows, pl.ds(column, size)] = source[n][
                    from_row : from_row + rows, from_column : from_column + size
                ].astype(F32)

    return pl.pallas_call(
        body,
        grid=(1,),
        in_specs=[smem()] + [single(x.shape) for x in (*mine, *twin)],
        out_specs=[single(d) for d in dims],
        out_shape=[shape(d, F32) for d in dims],
        compiler_params=params(56),
        cost_estimate=cost(0, sum(8 * a * b for a, b in dims)),
        name="merge",
    )(core, *mine, *twin)


def fetch_small(vector):
    count = lax.axis_size("fsdp")
    have = {0: vector}
    for bit in bit_list(count):
        for r in list(have):
            have[r ^ bit] = swap_fsdp(have[r], bit)
    stacked = jnp.stack([have[r] for r in range(count)])
    return jnp.take(stacked, lax.axis_index("fsdp") ^ jnp.arange(count), axis=0)


def add_terms(terms):
    total = terms[0].astype(F32)
    for term in terms[1:]:
        total = total + term.astype(F32)
    return total.astype(BF16)


def reduce_steps(keep, send, bits):
    count = lax.axis_size("fsdp")
    ctx_count = lax.axis_size("ctx")
    me_ctx = lax.axis_index("ctx")
    core = me_ctx & 1
    z = (me_ctx >> 1) & (LINE - 1)
    terms = [keep, (yield "ctx", xor_perm(ctx_count, 1), send)]
    left = count
    for bit in bits:
        left //= 2
        got = yield "fsdp", xor_perm(count, bit), add_terms([t[left:] for t in terms])
        terms = [t[:left] for t in terms] + [got]
    mine = add_terms([t[0] for t in terms])

    def along(pairs):
        stride = 2 * LINE
        return [
            (g * stride + 2 * a + c, g * stride + 2 * b + c)
            for g in range(ctx_count // stride)
            for a, b in pairs
            for c in range(2)
        ]

    inner = add_terms([mine, (yield "ctx", along([(0, 1), (3, 2)]), mine)])
    both = add_terms([inner, (yield "ctx", along([(1, 2), (2, 1)]), inner)])
    outer = yield "ctx", along([(1, 0), (2, 3)]), both
    full = jnp.where((z == 0) | (z == LINE - 1), outer, both)
    bit = 2 * LINE
    while bit < ctx_count:
        full = add_terms([full, (yield "ctx", xor_perm(ctx_count, bit), full)])
        bit *= 2
    return full, (yield "ctx", xor_perm(ctx_count, 1), full)


def sum_lines(mine):
    ctx_count = lax.axis_size("ctx")
    groups = [[g for g in range(ctx_count) if g % 2 == c] for c in range(2)]
    return lax.psum(mine, "ctx", axis_index_groups=groups)


class Lane:
    def __init__(self):
        self.active = []
        self.done = {}

    def add(self, key, steps):
        self.active.append((key, steps, next(steps)))

    def drain(self):
        while self.active:
            left = []
            for key, steps, (axis, pairs, operand) in self.active:
                try:
                    left.append((key, steps, steps.send(lax.ppermute(operand, axis, pairs))))
                except StopIteration as stop:
                    self.done[key] = stop.value
            self.active = left


def grad_kernel(key, a0, a1, k0, k1, s0, s1, *refs):
    keep, send = refs[-2:]
    left0, left1 = a0[...], a1[...]
    keep[0] = (dot_tn(left0, k0[...]) + dot_tn(left1, k1[...])).astype(BF16)
    send[0] = (dot_tn(left0, s0[...]) + dot_tn(left1, s1[...])).astype(BF16)


def shard_order(bits):
    order = [0]
    for bit in reversed(bits):
        order = order + [r | bit for r in order]
    return order


def weight_grad(a, b, shard, tile, first, tiles, bits=None, into=None, place=(0, 0), dims=None):
    count = lax.axis_size("fsdp")
    me = lax.axis_index("fsdp")
    core = lax.axis_index("ctx") & 1
    rows, width = b[0].shape
    across = width // 2 // tile
    chunks = a[0].shape[1] // (count * shard)
    order = jnp.arange(count) if bits is None else me ^ jnp.array(shard_order(bits))
    key = jnp.concatenate([core.reshape(1), order]).astype(jnp.int32)
    dims = dims or (count, shard, chunks * tiles * tile)
    row, column = place
    a_spec = pl.BlockSpec((rows, shard), lambda i, t, k: (0, k[1 + i] * chunks + t // tiles))

    def b_spec(twin):
        return pl.BlockSpec(
            (rows, tile),
            lambda i, t, k: (0, (1 - k[0] if twin else k[0]) * across + first + t % tiles),
        )

    o_spec = pl.BlockSpec((1, shard, tile), lambda i, t, k: (i, row, column + t))
    extra = list(into or [])
    return pl.pallas_call(
        grad_kernel,
        grid_spec=pltpu.PrefetchScalarGridSpec(
            num_scalar_prefetch=1,
            grid=(count, chunks * tiles),
            in_specs=[a_spec, a_spec, b_spec(False), b_spec(False), b_spec(True), b_spec(True)]
            + [anyspace()] * len(extra),
            out_specs=[o_spec, o_spec],
        ),
        out_shape=[shape(dims, BF16)] * 2,
        input_output_aliases={7: 0, 8: 1} if extra else {},
        compiler_params=params(56),
        cost_estimate=cost(
            8 * rows * shard * count * chunks * tiles * tile,
            4 * shard * count * chunks * tiles * tile + 8 * rows * width,
        ),
        name="weight_grad",
    )(key, a[0], a[1], b[0], b[1], b[0], b[1], *extra)


def norm_parts(x):
    centre = x - jnp.mean(x, -1, keepdims=True)
    rstd = lax.rsqrt(jnp.mean(centre * centre, -1, keepdims=True) + EPS)
    return centre * rstd, rstd


def norm_back(x, gain, grad):
    hat, rstd = norm_parts(x)
    scaled = grad * gain
    out = rstd * (
        scaled
        - jnp.mean(scaled, -1, keepdims=True)
        - hat * jnp.mean(scaled * hat, -1, keepdims=True)
    )
    grad_gain = jnp.sum(grad * hat, 0, keepdims=True)
    grad_bias = jnp.sum(grad, 0, keepdims=True)
    return out, grad_gain, grad_bias


GROUP = 4


def qkv_kernel(x_ref, gain, bias, weight, normed, pieces):
    @pl.when(pl.program_id(0) == 0)
    def _():
        hat, _ = norm_parts(x_ref[...].astype(F32))
        normed[...] = (hat * gain[...] + bias[...]).astype(BF16)

    group = dot(normed[...], weight[...]).astype(BF16)
    for copy in range(pieces.shape[0]):
        for h in range(GROUP):
            pieces[copy, h] = group[:, h * HD : (h + 1) * HD]


def qkv_forward(x, gain, bias, weight):
    count = lax.axis_size("ctx")
    width = x.shape[1]
    parts = HEADS // GROUP
    copies = count // HEADS
    normed, pieces = pl.pallas_call(
        qkv_kernel,
        grid=(3 * parts,),
        in_specs=[
            whole(x.shape),
            whole((1, width)),
            whole((1, width)),
            pl.BlockSpec((width, GROUP * HD), lambda t: (0, t)),
        ],
        out_specs=[
            whole((ROWS, width)),
            pl.BlockSpec((copies, GROUP, ROWS, HD), lambda t: (0, t % parts, 0, t // parts)),
        ],
        out_shape=[shape((ROWS, width), BF16), shape((copies, HEADS, ROWS, 3 * HD), BF16)],
        compiler_params=params(56),
        cost_estimate=cost(6 * ROWS * width * width, 8 * width * width),
        name="qkv",
    )(x, gain, bias, weight)
    return normed, pieces.reshape(count, ROWS, 3 * HD)


def gelu(u):
    inner = math.sqrt(2.0 / math.pi) * (u + 0.044715 * u * u * u)
    return 0.5 * u * (1.0 + jnp.tanh(inner))


def gelu_slope(u):
    c = math.sqrt(2.0 / math.pi)
    square = u * u
    t = jnp.tanh(c * (u + 0.044715 * u * square))
    return 0.5 * (1.0 + t) + 0.5 * u * (1.0 - t * t) * (c * (1.0 + 3.0 * 0.044715 * square))


def mlp_kernel(steps, x_ref, w_out, gain, bias, w_in, w_down, pieces, *refs):
    mixed, hidden, normed, up, act, out, total = refs
    step = pl.program_id(0)

    @pl.when(step == 0)
    def _():
        for s in range(HEADS):
            mixed[:, s * HD : (s + 1) * HD] = pieces[s]
        h = x_ref[...].astype(F32) + dot(mixed[...], w_out[...])
        hidden[...] = h
        hat, _ = norm_parts(h)
        normed[...] = (hat * gain[...] + bias[...]).astype(BF16)
        total[...] = h

    u = dot(normed[...], w_in[...])
    up[...] = u.astype(BF16)
    a = gelu(u).astype(BF16)
    act[...] = a
    total[...] += dot(a, w_down[...])

    @pl.when(step == steps - 1)
    def _():
        out[...] = total[...].astype(out.dtype)


def mlp_forward(x, pieces, w_out, gain, bias, w_in, w_down, kind):
    width = x.shape[1]
    ff = w_in.shape[1]
    tile = 512
    steps = ff // tile
    row = (ROWS, width)
    return pl.pallas_call(
        functools.partial(mlp_kernel, steps),
        grid=(steps,),
        in_specs=[
            whole(row),
            whole(w_out.shape),
            whole((1, width)),
            whole((1, width)),
            pl.BlockSpec((width, tile), lambda j: (0, j)),
            pl.BlockSpec((tile, width), lambda j: (j, 0)),
            whole((HEADS, ROWS, HD)),
        ],
        out_specs=[
            whole(row),
            whole(row),
            whole(row),
            pl.BlockSpec((ROWS, tile), lambda j: (0, j)),
            pl.BlockSpec((ROWS, tile), lambda j: (0, j)),
            whole(row),
        ],
        scratch_shapes=[pltpu.VMEM(row, F32)],
        out_shape=[
            shape(row, BF16),
            shape(row, F32),
            shape(row, BF16),
            shape((ROWS, ff), BF16),
            shape((ROWS, ff), BF16),
            shape(row, kind),
        ],
        compiler_params=params(56),
        cost_estimate=cost(2 * ROWS * width * (width + 2 * ff), 2 * width * (width + 2 * ff)),
        name="mlp",
    )(x, w_out, gain, bias, w_in, w_down, pieces)


def mlp_back_kernel(steps, g_ref, up, w_in, w_down, hidden, gain, w_out, *refs):
    du, grad_low, grad_hidden, grad_gain, grad_bias, pieces, total, low = refs
    step = pl.program_id(0)

    @pl.when(step == 0)
    def _():
        low[...] = g_ref[...].astype(BF16)
        total[...] = jnp.zeros_like(total)

    d_act = dot_nt(low[...], w_down[...])
    d_up = (gelu_slope(up[...].astype(F32)) * d_act).astype(BF16)
    du[...] = d_up
    total[...] += dot_nt(d_up, w_in[...])

    @pl.when(step == steps - 1)
    def _():
        part, g_gain, g_bias = norm_back(hidden[...], gain[...], total[...])
        grad_gain[...] = g_gain
        grad_bias[...] = g_bias
        dh = g_ref[...].astype(F32) + part
        grad_hidden[...] = dh
        hb = dh.astype(BF16)
        grad_low[...] = hb
        mixed = dot_nt(hb, w_out[...]).astype(BF16)
        for s in range(pieces.shape[0]):
            h = s % HEADS
            pieces[s] = mixed[:, h * HD : (h + 1) * HD]


def mlp_backward(grad, up, w_in, w_down, hidden, gain, w_out):
    count = lax.axis_size("ctx")
    width = hidden.shape[1]
    ff = w_in.shape[1]
    tile = 512
    steps = ff // tile
    row = (ROWS, width)
    return pl.pallas_call(
        functools.partial(mlp_back_kernel, steps),
        grid=(steps,),
        in_specs=[
            whole(row),
            pl.BlockSpec((ROWS, tile), lambda j: (0, j)),
            pl.BlockSpec((width, tile), lambda j: (0, j)),
            pl.BlockSpec((tile, width), lambda j: (j, 0)),
            whole(row),
            whole((1, width)),
            whole(w_out.shape),
        ],
        out_specs=[
            pl.BlockSpec((ROWS, tile), lambda j: (0, j)),
            whole(row),
            whole(row),
            whole((1, width)),
            whole((1, width)),
            whole((count, ROWS, HD)),
        ],
        scratch_shapes=[pltpu.VMEM(row, F32), pltpu.VMEM(row, BF16)],
        out_shape=[
            shape((ROWS, ff), BF16),
            shape(row, BF16),
            shape(row, F32),
            shape((1, width), F32),
            shape((1, width), F32),
            shape((count, ROWS, HD), BF16),
        ],
        compiler_params=params(56),
        cost_estimate=cost(2 * ROWS * width * (width + 2 * ff), 2 * width * (width + 2 * ff)),
        name="mlp_back",
    )(grad, up, w_in, w_down, hidden, gain, w_out)


def qkv_back_kernel(x_ref, gain, grad_hidden, weight, pieces, *refs):
    dqkv, grad_x, grad_low, grad_gain, grad_bias, total = refs
    step = pl.program_id(0)

    @pl.when(step == 0)
    def _():
        total[...] = jnp.zeros_like(total)

    for h in range(GROUP):
        dqkv[:, h * HD : (h + 1) * HD] = pieces[h]
    total[...] += dot_nt(dqkv[...], weight[...])

    @pl.when(step == pl.num_programs(0) - 1)
    def _():
        part, g_gain, g_bias = norm_back(x_ref[...].astype(F32), gain[...], total[...])
        grad_gain[...] = g_gain
        grad_bias[...] = g_bias
        result = grad_hidden[...] + part
        grad_x[...] = result
        grad_low[...] = result.astype(BF16)


def qkv_backward(x, gain, grad_hidden, weight, pieces):
    width = x.shape[1]
    row = (ROWS, width)
    parts = HEADS // GROUP
    wide = GROUP * HD
    return pl.pallas_call(
        qkv_back_kernel,
        grid=(3 * parts,),
        in_specs=[
            whole(row),
            whole((1, width)),
            whole(row),
            pl.BlockSpec((width, wide), lambda t: (0, t)),
            pl.BlockSpec((GROUP, ROWS, HD), lambda t: (t % parts, 0, t // parts)),
        ],
        out_specs=[
            pl.BlockSpec((ROWS, wide), lambda t: (0, t)),
            whole(row),
            whole(row),
            whole((1, width)),
            whole((1, width)),
        ],
        scratch_shapes=[pltpu.VMEM(row, F32)],
        out_shape=[
            shape((ROWS, 3 * width), BF16),
            shape(row, F32),
            shape(row, BF16),
            shape((1, width), F32),
            shape((1, width), F32),
        ],
        compiler_params=params(56),
        cost_estimate=cost(6 * ROWS * width * width, 6 * width * width),
        name="qkv_back",
    )(x, gain, grad_hidden, weight, pieces)


CHUNK = 64


def pick_scores(score_ref, index_ref, base, chunk):
    rows = pl.ds(pl.multiple_of(chunk * CHUNK, CHUNK), CHUNK)
    index = index_ref[pl.ds(pl.multiple_of(base + chunk * CHUNK, CHUNK), CHUNK), :]
    low = index & (HD - 1)
    high = index >> 7
    found = jnp.zeros((CHUNK, HD), F32)
    for tile in range(score_ref.shape[1] // HD):
        part = jnp.take_along_axis(
            score_ref[rows, tile * HD : (tile + 1) * HD], low, axis=1, mode="promise_in_bounds"
        )
        found = jnp.where(high == tile, part, found)
    return found


def scatter_rows(value_ref, value_base, index_ref, flat_ref, base, dense_ref, group):
    wide = 2 * HD
    start = pl.multiple_of(base + group * 16, 16)
    values = value_ref[pl.ds(pl.multiple_of(value_base + group * 16, 16), 16), :].astype(BF16)
    high = (index_ref[pl.ds(start, 16), :] >> 8).astype(F32).astype(BF16)
    query = lax.broadcasted_iota(jnp.int32, (16, HD), 0)
    lane = lax.broadcasted_iota(jnp.int32, (16, HD), 1) >> 5
    zero = jnp.zeros((16, HD), BF16)
    spots = [
        values * (query == lane + 4 * u).astype(F32).astype(BF16) for u in range(4)
    ]
    bands = []
    for h in range(dense_ref.shape[1] // wide):
        hit = high == jnp.array(h, BF16)
        bands.append(jnp.concatenate([jnp.where(hit, spot, zero) for spot in spots], 1))
    left = jnp.concatenate(bands, 0)
    flat = (flat_ref[pl.ds(pl.multiple_of((base + group * 16) // 4, 4), 4), :] & (wide - 1)).astype(F32).astype(BF16)
    place = lax.broadcasted_iota(jnp.int32, (wide, HD), 0).astype(F32).astype(BF16)
    one, none = jnp.ones((wide, HD), BF16), jnp.zeros((wide, HD), BF16)
    right = jnp.concatenate(
        [jnp.where(place == flat[u : u + 1, :], one, none) for u in range(4)], 1
    )
    spreadout = dot_nt(left, right)
    rows = pl.ds(pl.multiple_of(group * 16, 16), 16)
    for h in range(dense_ref.shape[1] // wide):
        dense_ref[rows, h * wide : (h + 1) * wide] = spreadout[h * 16 : (h + 1) * 16, :].astype(BF16)


def attend_kernel(recall, count, info, rel, buckets, pieces, *refs):
    if recall:
        mem, index, flat = refs[:3]
        refs = refs[3:]
    queries, keys, values, probs, outs = refs[:5]
    refs = refs[5:]
    if recall:
        weights, gap, mixed, bias, scores, dense = refs
    else:
        mixed, bias = refs

    def table(n, carry):
        rows = pl.ds(pl.multiple_of(n * 8, 8), 8)
        bucket = buckets[rows, :]
        part = jnp.full(bucket.shape, NEG, F32)
        for b in range(BUCKETS):
            part = jnp.where(bucket == b, rel[b], part)
        bias[rows, :] = part
        return carry

    lax.fori_loop(0, BLK // 8, table, 0)
    keys[0:WIN, :] = jnp.zeros((WIN, HD), BF16)
    values[0:WIN, :] = jnp.zeros((WIN, HD), BF16)
    for s in range(count):
        queries[s * ROWS : (s + 1) * ROWS, :] = pieces[s, :, :HD]
        for half in range(2):
            row = pl.multiple_of(info[2 * s + half] * BLK + WIN, BLK)
            span = slice(half * BLK, (half + 1) * BLK)
            keys[pl.ds(row, BLK), :] = pieces[s, span, HD : 2 * HD]
            values[pl.ds(row, BLK), :] = pieces[s, span, 2 * HD :]

    def one(s, carry):
        base = pl.multiple_of(s * ROWS, ROWS)
        for half in range(2):
            block = info[2 * s + half]
            row = pl.multiple_of(block * BLK, BLK)
            mine = pl.ds(pl.multiple_of(base + half * BLK, BLK), BLK)
            score = dot_nt(queries[mine, :], keys[pl.ds(row, SPAN), :]) * SCALE + bias[...]
            at = row + lax.broadcasted_iota(jnp.int32, (BLK, 1), 0)
            begin = jnp.zeros((BLK, 1), jnp.int32)
            for d in range(4):
                start = info[2 * count + d]
                begin = jnp.where(at >= start, jnp.maximum(begin, start), begin)
            key_at = row - WIN + lax.broadcasted_iota(jnp.int32, (1, SPAN), 1)
            score = jnp.where(key_at >= begin, score, NEG)
            exps = jnp.exp(score - jnp.max(score, -1, keepdims=True))
            prob = (exps * (1.0 / jnp.sum(exps, -1, keepdims=True))).astype(BF16)
            probs[2 * s + half] = prob
            mixed[mine, :] = dot(prob, values[pl.ds(row, SPAN), :])
        if recall:
            tile = pl.ds(base, ROWS)
            scores[...] = dot_nt(queries[tile, :], mem[:, :HD]) * SCALE

            def choose(chunk, inner):
                found = pick_scores(scores, index, base, chunk)
                exps = jnp.exp(found - jnp.max(found, -1, keepdims=True))
                weight = exps * ((HD // TOPK) / jnp.sum(exps, -1, keepdims=True))
                weights[pl.ds(pl.multiple_of(base + chunk * CHUNK, CHUNK), CHUNK), :] = weight
                return inner

            lax.fori_loop(0, ROWS // CHUNK, choose, 0)

            def place(group, inner):
                scatter_rows(weights, base, index, flat, base, dense, group)
                return inner

            lax.fori_loop(0, ROWS // 16, place, 0)
            found = dot(dense[...], mem[:, HD:])
            near = mixed[tile, :]
            gap[tile, :] = found - near
            gate = rel[BUCKETS]
            mixed[tile, :] = gate * found + (1.0 - gate) * near
        return carry

    lax.fori_loop(0, count, one, 0)
    for s in range(count):
        outs[s] = mixed[s * ROWS : (s + 1) * ROWS, :].astype(BF16)


def attend(pieces, info, rel, buckets, memory):
    count = lax.axis_size("ctx")
    total = count * ROWS
    recall = memory is not None
    operands = [info, rel, buckets, pieces]
    outs = [
        shape((total, HD), BF16),
        shape((total + WIN, HD), BF16),
        shape((total + WIN, HD), BF16),
        shape((2 * count, BLK, SPAN), BF16),
        shape((count, ROWS, HD), BF16),
    ]
    scratch = [pltpu.VMEM((total, HD), F32), pltpu.VMEM((BLK, SPAN), F32)]
    if recall:
        operands += list(memory)
        outs += [shape((total, HD), F32), shape((total, HD), F32)]
        rows = memory[0].shape[0]
        scratch += [pltpu.VMEM((ROWS, rows), F32), pltpu.VMEM((ROWS, rows), BF16)]
    result = pl.pallas_call(
        functools.partial(attend_kernel, recall, count),
        grid=(1,),
        in_specs=[smem(), smem()] + [single(x.shape) for x in operands[2:]],
        out_specs=[single(x.shape) for x in outs],
        out_shape=outs,
        scratch_shapes=scratch,
        compiler_params=params(60),
        cost_estimate=cost(45e9 if recall else 12e9, 8e6),
        name="recall_attend" if recall else "local_attend",
    )(*operands)
    return list(result[:4]) + list(result[5:]), result[4]


def attend_back_kernel(recall, count, info, rel, buckets, pieces, *refs):
    queries, keys, values, probs = refs[:4]
    refs = refs[4:]
    if recall:
        weights, gap, mem, index, flat, grad_rel, gate_sum = refs[:7]
        refs = refs[7:]
    else:
        grad_rel, refs = refs[0], refs[1:]
    outs, spread_sum, grads, dq, dk, dv = refs[:6]
    if recall:
        scores, dense, picked, mem_low = refs[6:]
        gate_sum[...] = jnp.zeros_like(gate_sum)
        gate = rel[BUCKETS]

    for s in range(count):
        grads[s * ROWS : (s + 1) * ROWS, :] = pieces[s]
    dk[...] = jnp.zeros_like(dk)
    dv[...] = jnp.zeros_like(dv)
    spread_sum[...] = jnp.zeros_like(spread_sum)

    def one(s, carry):
        base = pl.multiple_of(s * ROWS, ROWS)
        for half in range(2):
            block = info[2 * s + half]
            row = pl.multiple_of(block * BLK, BLK)
            mine = pl.ds(pl.multiple_of(base + half * BLK, BLK), BLK)
            near = pl.ds(row, SPAN)
            grad = grads[mine, :]
            if recall:
                grad = ((1.0 - gate) * grad.astype(F32)).astype(BF16)
            prob_low = probs[2 * s + half]
            prob = prob_low.astype(F32)
            d_prob = dot_nt(grad, values[near, :])
            product = prob * d_prob
            d_score = product - prob * jnp.sum(product, -1, keepdims=True)
            spread_sum[...] += d_score
            low = d_score.astype(BF16)
            dq[mine, :] = dot(low, keys[near, :]) * SCALE
            dk[near, :] += dot_tn(low, queries[mine, :]) * SCALE
            dv[near, :] += dot_tn(prob_low, grad)
        if recall:
            tile = pl.ds(base, ROWS)
            grad = grads[tile, :].astype(F32)
            gate_sum[...] += jnp.sum((grad * gap[tile, :]).reshape(ROWS // 8, 8, HD), 0)
            mem_low[...] = (gate * grad).astype(BF16)
            scores[...] = dot_nt(mem_low[...], mem[:, HD:])

            def choose(chunk, inner):
                found = pick_scores(scores, index, base, chunk)
                rows = pl.ds(pl.multiple_of(base + chunk * CHUNK, CHUNK), CHUNK)
                weight = weights[rows, :]
                product = weight * found
                centre = jnp.sum(product, -1, keepdims=True) * (TOPK / HD)
                local_rows = pl.ds(pl.multiple_of(chunk * CHUNK, CHUNK), CHUNK)
                picked[local_rows, :] = product - weight * centre
                return inner

            lax.fori_loop(0, ROWS // CHUNK, choose, 0)

            def place(group, inner):
                scatter_rows(picked, 0, index, flat, base, dense, group)
                return inner

            lax.fori_loop(0, ROWS // 16, place, 0)
            dq[tile, :] += dot(dense[...], mem[:, :HD]) * SCALE
        return carry

    lax.fori_loop(0, count, one, 0)
    for b in range(BUCKETS):
        part = jnp.sum(jnp.where(buckets[...] == b, spread_sum[...], 0.0), 0, keepdims=True)
        line = part[:, :HD]
        for n in range(1, SPAN // HD):
            line = line + part[:, n * HD : (n + 1) * HD]
        grad_rel[b : b + 1, :] = line
    for s in range(count):
        outs[s, :, :HD] = dq[s * ROWS : (s + 1) * ROWS, :].astype(BF16)
        for half in range(2):
            row = pl.multiple_of(info[2 * s + half] * BLK + WIN, BLK)
            span = slice(half * BLK, (half + 1) * BLK)
            outs[s, span, HD : 2 * HD] = dk[pl.ds(row, BLK), :].astype(BF16)
            outs[s, span, 2 * HD :] = dv[pl.ds(row, BLK), :].astype(BF16)


def attend_back(pieces, info, rel, buckets, saved, memory):
    count = lax.axis_size("ctx")
    total = count * ROWS
    recall = memory is not None
    operands = [info, rel, buckets, pieces, *saved]
    outs = [shape((BUCKETS, HD), F32)]
    scratch = [
        pltpu.VMEM((BLK, SPAN), F32),
        pltpu.VMEM((total, HD), BF16),
        pltpu.VMEM((total, HD), F32),
        pltpu.VMEM((total + WIN, HD), F32),
        pltpu.VMEM((total + WIN, HD), F32),
    ]
    if recall:
        operands += list(memory)
        rows = memory[0].shape[0]
        outs += [shape((8, HD), F32)]
        scratch += [
            pltpu.VMEM((ROWS, rows), F32),
            pltpu.VMEM((ROWS, rows), BF16),
            pltpu.VMEM((ROWS, HD), F32),
            pltpu.VMEM((ROWS, HD), BF16),
        ]
    outs += [shape((count, ROWS, 3 * HD), BF16)]
    result = pl.pallas_call(
        functools.partial(attend_back_kernel, recall, count),
        grid=(1,),
        in_specs=[smem(), smem()] + [single(x.shape) for x in operands[2:]],
        out_specs=[single(x.shape) for x in outs],
        out_shape=outs,
        scratch_shapes=scratch,
        compiler_params=params(60),
        cost_estimate=cost(50e9 if recall else 20e9, 8e6),
        name="recall_back" if recall else "local_back",
    )(*operands)
    return list(result[:-1]), result[-1]


def memory_rows(keys, values):
    count = lax.axis_size("ctx")

    def pieces(array):
        return [array[:, h * HD : (h + 1) * HD] for h in range(HEADS)]

    both = [jnp.concatenate(pair, 1) for pair in zip(pieces(keys), pieces(values))]
    stacked = jnp.stack(both * (count // HEADS))
    return exchange(stacked).reshape(count * ROWS, 2 * HD)


def memory_index(mem_index):
    count = lax.axis_size("ctx")
    micro = mem_index.shape[0]
    by_head = jnp.transpose(mem_index, (2, 0, 1, 3)).reshape(HEADS, micro, ROWS * TOPK // HD, HD)
    got = exchange(jnp.concatenate([by_head] * (count // HEADS), 0))
    result = []
    for m in range(micro):
        flat = got[:, m].reshape(-1, HD)
        index = jnp.tile(flat.reshape(count * ROWS, TOPK), (1, HD // TOPK))
        result.append((index, flat))
    return result


def local(
    inputs,
    block_slots,
    doc_starts,
    mem_index,
    mem_keys,
    mem_values,
    out_grad,
    *weights,
):
    me = lax.axis_index("ctx")
    me_fsdp = lax.axis_index("fsdp")
    count = lax.axis_size("ctx")
    fsdp = lax.axis_size("fsdp")
    micro = inputs.shape[0]
    width = inputs.shape[-1]
    my_head = me & (HEADS - 1)

    layers = [list(weights[:9]), list(weights[9:19])]
    small_of = [[0, 1, 5, 6, 3], [0, 1, 5, 6, 3, 9]]
    small = jnp.concatenate(
        [layers[n][i].reshape(-1) for n in range(2) for i in small_of[n]]
    )
    lengths = [layers[n][i].size for n in range(2) for i in small_of[n]]
    padded = -(-small.shape[0] // HD) * HD
    small = jnp.pad(small, (0, padded - small.shape[0])).reshape(-1, HD)
    gathered = fetch_small(small).reshape(fsdp, -1).astype(F32)
    tables = []
    offset = 0
    for length in lengths:
        tables.append(gathered[:, offset : offset + length])
        offset += length
    norms, rels = [], []
    for n in range(2):
        own = tables[5 * n : 5 * n + 5]
        norms.append([t.reshape(1, width) for t in own[:4]])
        rels.append(own[4].reshape(HEADS, BUCKETS))
    gates = jax.nn.sigmoid(tables[10].reshape(HEADS))
    gate = lax.dynamic_slice_in_dim(gates, my_head, 1, 0)

    buckets = jnp.asarray(window_buckets())
    mine = [
        jnp.concatenate([lax.dynamic_index_in_dim(rels[n], my_head, 0, keepdims=False), gate])
        for n in range(2)
    ]

    ups = bit_list(fsdp)
    downs = ups[::-1]
    tie = lax.optimization_barrier
    core = (me & 1).reshape(1).astype(jnp.int32)
    shard = width // fsdp
    wide = layers[0][7].shape[1]
    chunks = layers[0][8].shape[0] // shard
    half, half_qkv, half_in = width // 2, 3 * width // 2, wide // 2
    plan_a = [(0, 0, shard, half_qkv, 0, 0), (1, 0, shard, half, 0, half_qkv)]
    plan_b = [(0, 0, shard, half_in, 0, 0)] + [
        (1, n * shard, shard, half, shard, n * half) for n in range(chunks)
    ]

    groups = [
        (n, ids, plan, units * shard)
        for n in range(2)
        for ids, plan, units in (((2, 4), plan_a, 1), ((7, 8), plan_b, 2))
    ]
    packed = []
    for n, ids, plan, count_rows in groups:
        raw = [layers[n][i] for i in ids]
        if packed:
            packed[-1], raw = tie((packed[-1], raw))
        packed.append(pack(raw, plan, count_rows, core))
    gathered = [lax.all_gather(p, "fsdp", axis=0, tiled=False) for p in packed]
    full = [{}, {}]

    def unfold(g, value):
        n, ids, plan, _ = groups[g]
        mine = gathered[g]
        if value is not None:
            value, mine = tie((value, mine))
        for i, w in zip(ids, unfold_weights(mine, [layers[n][i] for i in ids], plan, core)):
            full[n][i] = w
        return value

    unfold(0, None)

    infos = [
        jnp.concatenate([block_slots[m, 0], doc_starts[m, 0]]).astype(jnp.int32) for m in range(micro)
    ]
    rows = memory_rows(mem_keys[0], mem_values[0])
    indices = memory_index(mem_index[:, 0])
    memories = [(rows, *indices[m]) for m in range(micro)]

    state = [inputs[m, 0] for m in range(micro)]
    kept = [[None] * micro, [None] * micro]
    for n in range(2):
        gain_in, bias_in, gain_mid, bias_mid = norms[n]
        w = full[n]
        work = [dict(x=state[m]) for m in range(micro)]
        for m in range(micro):
            work[m]["n1"], pieces = qkv_forward(work[m]["x"], gain_in, bias_in, w[2])
            if m == micro - 1:
                pieces = unfold(1 + 2 * n, pieces)
            work[m]["pieces"] = exchange(pieces)
        for m in range(micro):
            work[m]["saved"], outs = attend(
                work[m]["pieces"], infos[m], mine[n], buckets, memories[m] if n else None
            )
            if n == 0 and m == micro - 1:
                outs = unfold(2, outs)
            work[m]["outs"] = exchange(outs)
        for m in range(micro):
            mixed, hidden, normed_mid, up, act, state[m] = mlp_forward(
                work[m]["x"],
                work[m]["outs"],
                w[4],
                gain_mid,
                bias_mid,
                w[7],
                w[8],
                BF16 if n else F32,
            )
            work[m].update(mixed=mixed, hidden=hidden, n2=normed_mid, up=up, act=act)
        kept[n] = work
    outputs = jnp.stack(state)[:, None]

    lane = Lane()
    smalls = [None, None]
    top = [out_grad[m, 0] for m in range(micro)]
    top_low = top

    def pair(source, name):
        return [item[name] for item in source]

    def launch(key, bits, *what):
        lane.add(key, reduce_steps(*weight_grad(*what, bits=bits), bits))

    def chip_sum(keep, send):
        return add_terms([keep, swap_ctx(send, 1)])

    def shard_sum(x):
        return lax.psum_scatter(x, "fsdp", scatter_dimension=0, tiled=False)

    dims_a = (fsdp, shard, 2 * width)
    dims_b = (fsdp, 2 * shard, half_in)
    sums = {}
    for n in (1, 0):
        gain_in, bias_in, gain_mid, bias_mid = norms[n]
        w = full[n]
        ks = kept[n]
        back = [None] * micro
        for m in range(micro):
            k = ks[m]
            grad = top[m]
            if n == 0 and m == 0:
                grad, sums["b1"], sums["a1"] = tie((grad, sums["b1"], sums["a1"]))
                sums["b1"] = sum_lines(sums["b1"])
                sums["a1"] = shard_sum(sums["a1"])
            du, hb, dh, g_gain_mid, g_bias_mid, pieces = mlp_backward(
                grad, k["up"], w[7], w[8], k["hidden"], gain_mid, w[4]
            )
            back[m] = dict(
                du=du, hb=hb, dh=dh, norms=[g_gain_mid, g_bias_mid], pieces=exchange(pieces)
            )
        act, n2, mixed = pair(ks, "act"), pair(ks, "n2"), pair(ks, "mixed")
        du, hb = pair(back, "du"), pair(back, "hb")
        both = weight_grad(n2, du, shard, width, 0, half_in // width, dims=dims_b)
        both = weight_grad(act, top_low, shard, half, 0, 1, into=both, place=(1, 0), dims=dims_b)
        back[0]["pieces"], both = tie((back[0]["pieces"], both))
        chip = chip_sum(*both)
        for m in range(micro):
            pieces = back[m]["pieces"]
            if m == 1:
                pieces, chip = tie((pieces, chip))
                sums["b%d" % n] = shard_sum(chip)
                if n == 0:
                    pieces, sums["a1"], sums["b1"] = tie((pieces, sums["a1"], sums["b1"]))
                    sums["a1"] = sum_lines(sums["a1"])
            back[m]["extra"], outs = attend_back(
                pieces, infos[m], mine[n], buckets, ks[m]["saved"], memories[m] if n else None
            )
            back[m]["outs"] = exchange(outs)
        for m in range(micro):
            k = ks[m]
            outs = back[m]["outs"]
            if n == 0 and m == 1:
                outs, sums["b0"], sums["a1"] = tie((outs, sums["b0"], sums["a1"]))
                sums["b0"] = sum_lines(sums["b0"])
            dqkv, dx, dx_low, g_gain_in, g_bias_in = qkv_backward(
                k["x"], gain_in, back[m]["dh"], w[2], outs
            )
            back[m].update(dqkv=dqkv, dx=dx, dx_low=dx_low)
            back[m]["norms"] = [g_gain_in, g_bias_in] + back[m]["norms"]
        n1, dqkv = pair(ks, "n1"), pair(back, "dqkv")
        if n:
            both = weight_grad(n1, dqkv, shard, half, 0, 3, dims=dims_a)
            both = weight_grad(mixed, hb, shard, half, 0, 1, into=both, place=(0, 3), dims=dims_a)
            sums["a1"] = chip_sum(*both)
        else:
            launch("out", ups, mixed, hb, shard, half, 0, 1)
            launch("low", ups, n1, dqkv, shard, half_qkv // 2, 0, 1)
            launch("high", downs, n1, dqkv, shard, half_qkv // 2, 1, 1)
        share = HEADS / count
        spot = (jnp.arange(HEADS) == my_head).astype(F32) * share
        rel = jnp.sum(sum(item["extra"][0] for item in back), -1)
        parts = [sum(item["norms"][i] for item in back).reshape(fsdp, -1) for i in range(4)]
        parts.append((spot[:, None] * rel[None, :]).reshape(fsdp, -1))
        if n:
            value = sum(jnp.sum(item["extra"][1]) for item in back) * (gate * (1.0 - gate))[0]
            parts.append((spot * value).reshape(fsdp, -1))
        smalls[n] = parts
        top = pair(back, "dx")
        top_low = pair(back, "dx_low")
    lane.drain()
    dims = [(shard, 3 * width), (shard, width), (shard, wide), (chunks * shard, width)]

    def joined(parts, plan, sizes):
        return merge([p[0] for p in parts], [p[1] for p in parts], plan, sizes, core)

    ready = {key: (value, swap_ctx(value, 1)) for key, value in sums.items()}
    move_b = [(0, 0, shard, half_in, 0, 0, 0, 0, half_in)] + [
        (1, n * shard, shard, half, 0, shard, n * half, 0, half) for n in range(chunks)
    ]
    move_qkv = (0, 0, shard, half_qkv, 0, 0, 0, 0, half_qkv)
    move_out = (1, 0, shard, half, 0, 0, half_qkv, 0, half)
    grads = [{}, {}]
    for n in range(2):
        grads[n][7], grads[n][8] = joined([ready["b%d" % n]], move_b, dims[2:])
    grads[1][2], grads[1][4] = joined([ready["a1"]], [move_qkv, move_out], dims[:2])
    size = half_qkv // 2
    moves = [(0, 0, shard, half_qkv, n, 0, 0, n * size, size) for n in range(2)]
    moves.append((1, 0, shard, half, 2, 0, 0, 0, half))
    done = lane.done
    grads[0][2], grads[0][4] = joined([done["low"], done["high"], done["out"]], moves, dims[:2])

    flat = jnp.concatenate(smalls[0] + smalls[1], 1)
    columns = flat.shape[1]
    flat = jnp.pad(flat, ((0, 0), (0, -columns % HD)))
    for bit in bit_list(count):
        flat = flat + swap_ctx(flat, bit)
    for bit in ups:
        flat = flat + swap_fsdp(flat, bit)
    row = lax.dynamic_index_in_dim(flat, me_fsdp, 0, keepdims=False)
    cuts = []
    offset = 0
    for part in smalls[0] + smalls[1]:
        cuts.append(row[offset : offset + part.shape[1]])
        offset += part.shape[1]
    result = []
    for n in range(2):
        own = cuts[5 * n : 5 * n + 5]
        result += [
            own[0],
            own[1],
            grads[n][2],
            own[4].reshape(-1, BUCKETS),
            grads[n][4],
            own[2],
            own[3],
            grads[n][7],
            grads[n][8],
        ]
    result.append(cuts[10])
    return (outputs, jnp.stack(top)[:, None], *result)


def solution(mesh):
    vector, matrix = P("fsdp"), P("fsdp", None)
    rows = P(None, "fsdp", "ctx", None)
    layer = (vector, vector, matrix, matrix, matrix, vector, vector, matrix, matrix)
    table = P(None, "fsdp", None)
    memory = P("fsdp", "ctx", None)
    return jax.shard_map(
        local,
        mesh=mesh,
        in_specs=(rows, table, table, P(None, "fsdp", "ctx", None, None), memory, memory, rows)
        + layer
        + layer
        + (vector,),
        out_specs=(rows, rows) + layer + layer + (vector,),
        check_vma=False,
    )
```

time: 3380 us -> 1450 us (0.43)
  waiting for transfers between devices: 1460 us -> 503 us
  Pallas kernels: 0 us -> 679 us
  other arithmetic: 729 us -> 59.8 us
  matrix products: 577 us -> 0 us
  local copies, waits for them, and re-layouts: 454 us -> 29.7 us
  starting transfers between devices: 1.13 us -> 125 us
  blocking collectives: 118 us -> 19.5 us
    pallas_call x0 -> x45, Pallas kernels: none -> 679 us  [the longest x4 162 us: attend(): pl.pallas_call(functools.partial(attend_kernel, recall, count), grid=(1,)...]
    all_gather x14 -> x4, waiting for transfers between devices: 686 us -> 107 us  [local(): gathered = [lax.all_gather(p, 'fsdp', axis=0, tiled=False) for p in packed]]
    dot_general x192 -> x0, matrix products: 577 us -> none  [the longest x32 54.8 us: split_product(): jnp.dot(lower, right, preferred_element_type=jnp.float32)]
    reduce_scatter x12 -> x0, waiting for transfers between devices: 543 us -> none  [the longest x1 89.6 us: local(): lax.psum_scatter(totals[17].astype(jnp.bfloat16), 'fsdp', scatter_dimensi...]
    reduce_sum x96 -> x4, other arithmetic: 450 us -> 1.42 us  [the longest x2 1.2 us: local(): jnp.sum(item['extra'][1])]
    psum x1 -> x3, waiting for transfers between devices: 222 us -> 41.3 us  [sum_lines(): return lax.psum(mine, 'ctx', axis_index_groups=groups)]
    all_to_all x0 -> x17, waiting for transfers between devices: none -> 152 us  [exchange(): return lax.all_to_all(x, 'ctx', 0, 0, tiled=False)]
    convert_element_type x78 -> x17, other arithmetic: 142 us -> 36.7 us  [the longest x15 36.6 us: add_terms(): return total.astype(BF16)]
  transfers between devices with their start and end apart: 27 -> 66, of which waited for: 19 -> 26; matrix products, arithmetic and copies ran while one was open for 30% -> 6% of each run, Pallas kernels for 0% -> 47%
where the time goes in v1:
time: 1450 us; the launch traced here: 1430 us
  Pallas kernels  679 us (47%)
  waiting for transfers between devices  503 us (35%)
  starting transfers between devices  125 us (9%)
  other arithmetic  59.8 us (4%)
  local copies, waits for them, and re-layouts  29.7 us (2%)
  blocking collectives  19.5 us (1%)
  between operations  18.6 us (1%)
    pallas_call x4, Pallas kernels, attend(): pl.pallas_call(functools.partial(attend_kernel, recall, count), grid=(1,)...  162 us
    pallas_call x4, Pallas kernels, attend_back(): pl.pallas_call(functools.partial(attend_back_kernel, recall, count), grid...  161 us
    all_to_all x17, waiting for transfers between devices, exchange(): return lax.all_to_all(x, 'ctx', 0, 0, tiled=False)  152 us
    all_gather x4, waiting for transfers between devices, local(): gathered = [lax.all_gather(p, 'fsdp', axis=0, tiled=False) for p in packed]  107 us
    unnamed x13, waiting for transfers between devices  104 us
    pallas_call x9, Pallas kernels, weight_grad(): pl.pallas_call(grad_kernel, grid_spec=pltpu.PrefetchScalarGridSpec(num_sc...  92.9 us
    all_to_all x17, starting transfers between devices, exchange(): return lax.all_to_all(x, 'ctx', 0, 0, tiled=False)  75.6 us
    ppermute x21, waiting for transfers between devices, drain(): left.append((key, steps, steps.send(lax.ppermute(operand, axis, pairs))))  73.2 us
  transfers between devices with their start and end apart: 66, of which 26 were waited for; matrix products, arithmetic and copies ran while one was open for 6% of the time, Pallas kernels for 47%

profile of v1, /device:TPU:0, one launch (start us, length us, event | category | flops | bytes accessed | tf_op | source)
XLA Modules:
  0.0 1434.5 jit_solution(384785932818184400)
XLA Ops:
  14.9 51.0 %all-gather.9.cloned.1.call-done = bf16[1024,2048]{1,0:T(8,128)(2,1)} async-done(((bf16[256,2048]{1,0:T(8,128)(2,1)}), bf16[1024,2048]{1,0:T(8,128)(2,1)}) %all-gather.9.cloned.1.call-update) | async-done | bytes 4194320 | tf_op jit(solution)/shard_map/all_gather | solution.py:1009
  100.5 55.5 %all-gather.11.cloned.1.call-done = bf16[2048,2048]{1,0:T(8,128)(2,1)} async-done(((bf16[512,2048]{1,0:T(8,128)(2,1)}), bf16[2048,2048]{1,0:T(8,128)(2,1)}) %all-gather.11.cloned.1.call-update) | async-done | bytes 8388624 | tf_op jit(solution)/shard_map/all_gather | solution.py:1009
  169.1 29.4 %all-to-all-done.2.pieces = bf16[8,256,384]{2,1,0:T(8,128)(2,1)S(1)} async-done(((bf16[8,256,384]{2,1,0:T(8,128)(2,1)}), bf16[8,256,384]{2,1,0:T(8,128)(2,1)S(1)}, u32[]{:S(2)}, u32[]{:S(2)}) %all-to-all-start.2) | async-done | bytes 1572896 | tf_op jit(solution)/shard_map/all_to_all | solution.py:117
  205.3 12.1 local_attend.3
  223.5 17.5 %all-to-all-done.pieces = bf16[8,256,384]{2,1,0:T(8,128)(2,1)S(1)} async-done(((bf16[8,256,384]{2,1,0:T(8,128)(2,1)}), bf16[8,256,384]{2,1,0:T(8,128)(2,1)S(1)}, u32[]{:S(2)}, u32[]{:S(2)}) %all-to-all-start) | async-done | bytes 1572896 | tf_op jit(solution)/shard_map/all_to_all | solution.py:117
  245.2 12.1 local_attend.2
  257.2 13.9 all-to-all-done.5
  271.1 19.5 %all_to_all.90.pieces = bf16[8,256,128]{2,1,0:T(8,128)(2,1)} all-to-all(bf16[8,256,128]{2,1,0:T(8,128)(2,1)} %get-tuple-element.208), channel_id=1, replica_groups=mesh['ctx'=8,'fsdp'=4] {'ctx'}, dimensions={0} | all-to-all | bytes 1048576 | tf_op jit(solution)/shard_map/all_to_all | solution.py:117
  303.0 12.1 unfold.5
  315.0 15.6 %mlp.4 = (bf16[256,1024]{1,0:T(8,128)(2,1)}, f32[256,1024]{1,0:T(8,128)}, bf16[256,1024]{1,0:T(8,128)(2,1)}, bf16[256,4096]{1,0:T(8,128)(2,1)}, bf16[256,4096]{1,0:T(8,128)(2,1)}, /*index=5*/f32[256,1024]{1,0:T(8,128)}) custom-call(bf16[256,1024]{1,0:T(8,128)(2,1)} %get-tuple-element.440.x_ref, bf16[1024,1024]{1,0:T(8,128)(2,1)} %get-tuple-element.198.w_out, ...), custom_call_target="tpu_custom_call" | custom-call | flops 4831838208 | bytes 18874368 | tf_op jit(solution)/shard_map/mlp/pallas_call | solution.py:474
  351.6 15.5 %mlp.5 = (bf16[256,1024]{1,0:T(8,128)(2,1)}, f32[256,1024]{1,0:T(8,128)}, bf16[256,1024]{1,0:T(8,128)(2,1)}, bf16[256,4096]{1,0:T(8,128)(2,1)}, bf16[256,4096]{1,0:T(8,128)(2,1)}, /*index=5*/f32[256,1024]{1,0:T(8,128)}) custom-call(bf16[256,1024]{1,0:T(8,128)(2,1)} %get-tuple-element.441.x_ref, bf16[1024,1024]{1,0:T(8,128)(2,1)} %get-tuple-element.198.w_out, ...), custom_call_target="tpu_custom_call" | custom-call | flops 4831838208 | bytes 18874368 | tf_op jit(solution)/shard_map/mlp/pallas_call | solution.py:474
  367.1 7.4 qkv.6
  384.7 69.1 %recall_attend.2 = (bf16[2048,128]{1,0:T(8,128)(2,1)}, bf16[2560,128]{1,0:T(8,128)(2,1)}, bf16[2560,128]{1,0:T(8,128)(2,1)}, bf16[16,128,640]{2,1,0:T(8,128)(2,1...) custom-call(s32[20]{0:T(128)} %pad_add_fusion.info, f32[33]{0:T(128)} %pad_maximum_fusion.2.rel, ...), custom_call_target="tpu_custom_call" | custom-call | flops 44999999488 | bytes 8000000 | tf_op jit(solution)/shard_map/recall_attend/pallas_call | solution.py:780
  459.9 69.0 %recall_attend.3 = (bf16[2048,128]{1,0:T(8,128)(2,1)}, bf16[2560,128]{1,0:T(8,128)(2,1)}, bf16[2560,128]{1,0:T(8,128)(2,1)}, bf16[16,128,640]{2,1,0:T(8,128)(2,1...) custom-call(s32[20]{0:T(128)} %pad_add_fusion.1.info, f32[33]{0:T(128)} %pad_maximum_fusion.2.rel, ...), custom_call_target="tpu_custom_call" | custom-call | flops 44999999488 | bytes 8000000 | tf_op jit(solution)/shard_map/recall_attend/pallas_call | solution.py:780
  536.2 12.1 unfold.7
  548.2 15.6 %mlp.6 = (bf16[256,1024]{1,0:T(8,128)(2,1)}, f32[256,1024]{1,0:T(8,128)}, bf16[256,1024]{1,0:T(8,128)(2,1)}, bf16[256,4096]{1,0:T(8,128)(2,1)}, bf16[256,4096]{1,0:T(8,128)(2,1)}, /*index=5*/bf16[256,1024]{1,0:T(8,128)(2,1)}) custom-call(f32[256,1024]{1,0:T(8,128)} %get-tuple-element.209.x_ref, bf16[1024,1024]{1,0:T(8,128)(2,1)} %get-tuple-element.216.w_out, ...), custom_call_target="tpu_custom_call" | custom-call | flops 4831838208 | bytes 18874368 | tf_op jit(solution)/shard_map/mlp/pallas_call | solution.py:474
  563.8 16.7 %mlp_back.4 = (bf16[256,4096]{1,0:T(8,128)(2,1)}, bf16[256,1024]{1,0:T(8,128)(2,1)}, f32[256,1024]{1,0:T(8,128)}, f32[1,1024]{1,0:T(1,128)}, f32[1,1024]{1,0:T(1,128)}, /*index=5*/bf16[8,256,128]{2,1,0:T(8,128)(2,1)}) custom-call(bf16[256,1024]{1,0:T(8,128)(2,1)} %get-tuple-element.438.g_ref.k0.s0, bf16[256,4096]{1,0:T(8,128)(2,1)} %get-tuple-element.232.up, ...), custom_call_target="tpu_custom_call" | custom-call | flops 4831838208 | bytes 18874368 | tf_op jit(solution)/shard_map/mlp_back/pallas_call | solution.py:545
  585.7 15.6 %mlp.7 = (bf16[256,1024]{1,0:T(8,128)(2,1)}, f32[256,1024]{1,0:T(8,128)}, bf16[256,1024]{1,0:T(8,128)(2,1)}, bf16[256,4096]{1,0:T(8,128)(2,1)}, bf16[256,4096]{1,0:T(8,128)(2,1)}, /*index=5*/bf16[256,1024]{1,0:T(8,128)(2,1)}) custom-call(f32[256,1024]{1,0:T(8,128)} %get-tuple-element.218.x_ref, bf16[1024,1024]{1,0:T(8,128)(2,1)} %get-tuple-element.216.w_out, ...), custom_call_target="tpu_custom_call" | custom-call | flops 4831838208 | bytes 18874368 | tf_op jit(solution)/shard_map/mlp/pallas_call | solution.py:474
  601.3 16.8 %mlp_back.5 = (bf16[256,4096]{1,0:T(8,128)(2,1)}, bf16[256,1024]{1,0:T(8,128)(2,1)}, f32[256,1024]{1,0:T(8,128)}, f32[1,1024]{1,0:T(1,128)}, f32[1,1024]{1,0:T(1,128)}, /*index=5*/bf16[8,256,128]{2,1,0:T(8,128)(2,1)}) custom-call(bf16[256,1024]{1,0:T(8,128)(2,1)} %get-tuple-element.439.g_ref.k1.s1, bf16[256,4096]{1,0:T(8,128)(2,1)} %get-tuple-element.241.up, ...), custom_call_target="tpu_custom_call" | custom-call | flops 4831838208 | bytes 18874368 | tf_op jit(solution)/shard_map/mlp_back/pallas_call | solution.py:545
  618.1 13.6 weight_grad.9
  631.7 14.9 %weight_grad.10 = (bf16[4,512,2048]{2,1,0:T(8,128)(2,1)}, bf16[4,512,2048]{2,1,0:T(8,128)(2,1)}) custom-call(s32[5]{0:T(128)} %pad_add_fusion.2.key, bf16[256,4096]{1,0:T(8,128)(2,1)} %get-tuple-element.236.a0, bf16[256,4096]{1,0:T(8,128)(2,1)} %get-tuple-element.237.a1, ...), custom_call_target="tpu_custom_call", output_to_operand_aliasing={{0}: (7, {}), {1}: (8, {})} | custom-call | flops 4294967296 | bytes 10485760 | tf_op jit(solution)/shard_map/weight_grad/pallas_call | solution.py:351
  652.4 7.9 collective-permute-done.7
  660.3 10.5 add_convert_fusion.1
  671.6 66.9 %recall_back.2 = (f32[32,128]{1,0:T(8,128)}, f32[8,128]{1,0:T(8,128)}, bf16[8,256,384]{2,1,0:T(8,128)(2,1)}) custom-call(s32[20]{0:T(128)} %pad_add_fusion.info, f32[33]{0:T(128)} %pad_maximum_fusion.2.rel, s32[128,640]{1,0:T(8,128)} %constant.62.clone.buckets, bf16[8,256,128]{2,1,0:T(8,128)(2,1)} %copy-done.25, ...), custom_call_target="tpu_custom_call" | custom-call | flops 49999998976 | bytes 8000000 | tf_op jit(solution)/shard_map/recall_back/pallas_call | solution.py:901
  743.5 67.3 %recall_back.3 = (f32[32,128]{1,0:T(8,128)}, f32[8,128]{1,0:T(8,128)}, bf16[8,256,384]{2,1,0:T(8,128)(2,1)}) custom-call(s32[20]{0:T(128)} %pad_add_fusion.1.info, f32[33]{0:T(128)} %pad_maximum_fusion.2.rel, s32[128,640]{1,0:T(8,128)} %constant.62.clone.buckets, bf16[8,256,128]{2,1,0:T(8,128)(2,1)} %copy-done.27, ...), custom_call_target="tpu_custom_call" | custom-call | flops 49999998976 | bytes 8000000 | tf_op jit(solution)/shard_map/recall_back/pallas_call | solution.py:901
  816.1 9.1 qkv_back.4
  825.1 28.5 %all-to-all-done.13.pieces = bf16[8,256,384]{2,1,0:T(8,128)(2,1)S(1)} async-done(((bf16[8,256,384]{2,1,0:T(8,128)(2,1)}), bf16[8,256,384]{2,1,0:T(8,128)(2,1)S(1)}, u32[]{:S(2)}, u32[]{:S(2)}) %all-to-all-start.13) | async-done | bytes 1572896 | tf_op jit(solution)/shard_map/all_to_all | solution.py:117
  854.8 9.0 qkv_back.5
  863.8 13.2 weight_grad.11
  895.9 16.9 %mlp_back.6 = (bf16[256,4096]{1,0:T(8,128)(2,1)}, bf16[256,1024]{1,0:T(8,128)(2,1)}, f32[256,1024]{1,0:T(8,128)}, f32[1,1024]{1,0:T(1,128)}, f32[1,1024]{1,0:T(1,128)}, /*index=5*/bf16[8,256,128]{2,1,0:T(8,128)(2,1)}) custom-call(f32[256,1024]{1,0:T(8,128)} %get-tuple-element.282.g_ref, bf16[256,4096]{1,0:T(8,128)(2,1)} %get-tuple-element.283.up, ...), custom_call_target="tpu_custom_call" | custom-call | flops 4831838208 | bytes 18874368 | tf_op jit(solution)/shard_map/mlp_back/pallas_call | solution.py:545
  916.3 16.9 %mlp_back.7 = (bf16[256,4096]{1,0:T(8,128)(2,1)}, bf16[256,1024]{1,0:T(8,128)(2,1)}, f32[256,1024]{1,0:T(8,128)}, f32[1,1024]{1,0:T(1,128)}, f32[1,1024]{1,0:T(1,128)}, /*index=5*/bf16[8,256,128]{2,1,0:T(8,128)(2,1)}) custom-call(f32[256,1024]{1,0:T(8,128)} %get-tuple-element.294.g_ref, bf16[256,4096]{1,0:T(8,128)(2,1)} %get-tuple-element.295.up, ...), custom_call_target="tpu_custom_call" | custom-call | flops 4831838208 | bytes 18874368 | tf_op jit(solution)/shard_map/mlp_back/pallas_call | solution.py:545
  933.3 13.6 weight_grad.13
  946.9 15.0 %weight_grad.14 = (bf16[4,512,2048]{2,1,0:T(8,128)(2,1)}, bf16[4,512,2048]{2,1,0:T(8,128)(2,1)}) custom-call(s32[5]{0:T(128)} %pad_add_fusion.2.key, bf16[256,4096]{1,0:T(8,128)(2,1)} %get-tuple-element.287.a0, bf16[256,4096]{1,0:T(8,128)(2,1)} %get-tuple-element.288.a1, ...), custom_call_target="tpu_custom_call", output_to_operand_aliasing={{0}: (7, {}), {1}: (8, {})} | custom-call | flops 4294967296 | bytes 10485760 | tf_op jit(solution)/shard_map/weight_grad/pallas_call | solution.py:351
  967.9 7.6 collective-permute-done.9
  975.4 10.5 add_convert_fusion
  986.0 11.3 all-to-all-done.16.pieces
  1002.7 55.2 %reduce-scatter.12.cloned.1.call-done = bf16[1,256,2048]{2,1,0:T(8,128)(2,1)} async-done(((bf16[4,256,2048]{2,1,0:T(8,128)(2,1)}), bf16[1,256,2048]{2,1,0:T(8,128)(2,1)}) %reduce-scatter.12.cloned.1.call-update) | async-done | bytes 1048592
  1058.7 13.2 local_back.2
  1076.6 13.3 local_back.3
  1089.8 45.4 %all-to-all-done.15.pieces = bf16[8,256,384]{2,1,0:T(8,128)(2,1)S(1)} async-done(((bf16[8,256,384]{2,1,0:T(8,128)(2,1)}), bf16[8,256,384]{2,1,0:T(8,128)(2,1)S(1)}, u32[]{:S(2)}, u32[]{:S(2)}) %all-to-all-start.15) | async-done | bytes 1572896 | tf_op jit(solution)/shard_map/all_to_all | solution.py:117
  1156.2 19.1 %collective-permute-done.28 = bf16[2,256,512]{2,1,0:T(8,128)(2,1)} collective-permute-done((bf16[2,256,512]{2,1,0:T(8,128)(2,1)S(1)}, bf16[2,256,512]{2,1,0:T(8,128)(2,1)}, u32[]{:S(2)}, u32[]{:S(2)}) %collective-permute-start.28) | collective-permute-done | bytes 524320 | tf_op jit(solution)/shard_map/ppermute | solution.py:310
  1178.3 9.3 qkv_back.6
  1187.7 48.1 %reduce-scatter.14.cloned.1.call-done = bf16[1,512,2048]{2,1,0:T(8,128)(2,1)} async-done(((bf16[4,512,2048]{2,1,0:T(8,128)(2,1)}), bf16[1,512,2048]{2,1,0:T(8,128)(2,1)}) %reduce-scatter.14.cloned.1.call-update) | async-done | bytes 2097168
  1235.8 8.9 qkv_back.7
  1280.5 10.8 collective-permute-done.22
  1328.0 35.8 %all-reduce.13.cloned.1.call-done.refs_0_ = bf16[512,2048]{1,0:T(8,128)(2,1)} async-done(((bf16[512,2048]{1,0:T(8,128)(2,1)}), bf16[512,2048]{1,0:T(8,128)(2,1)}) %all-reduce.13.cloned.1.call-update) | async-done | bytes 2097168 | tf_op jit(solution)/shard_map/psum | solution.py:294
  1376.2 23.9 %collective-permute-done.26 = bf16[256,768]{1,0:T(8,128)(2,1)S(1)} collective-permute-done((bf16[256,768]{1,0:T(8,128)(2,1)S(1)}, bf16[256,768]{1,0:T(8,128)(2,1)S(1)}, u32[]{:S(2)}, u32[]{:S(2)}) %collective-permute-start.26) | collective-permute-done | bytes 393248 | tf_op jit(solution)/shard_map/ppermute | solution.py:310
  1400.2 7.5 collective-permute-done.20
  (403 shorter events, 316.4 us)
Async XLA Ops:
  7.2 58.7 %all-gather.9.cloned.1.call-start = ((), (), s32[]{:S(2)}) async-start(), calls=%async_computation.24 | async-start | bytes 5242880 | tf_op jit(solution)/shard_map/all_gather | solution.py:1009
  9.5 146.6 %all-gather.11.cloned.1.call-start = ((), (), s32[]{:S(2)}) async-start(), calls=%async_computation.25 | async-start | bytes 10485760 | tf_op jit(solution)/shard_map/all_gather | solution.py:1009
  12.6 204.9 %all-gather.13.cloned.1.call-start = ((), (), s32[]{:S(2)}) async-start(), calls=%async_computation.26 | async-start | bytes 5242880 | tf_op jit(solution)/shard_map/all_gather | solution.py:1009
  65.9 20.9 %collective-permute-start = (bf16[4,256,2048]{2,1,0:T(8,128)(2,1)}, bf16[4,256,2048]{2,1,0:T(8,128)(2,1)}, u32[]{:S(2)}, u32[]{:S(2)}) collective-permute-start(bf16[4,256,2048]{2,1,0:T(8,128)(2,1)} %bitcast.164), channel_id=1, source_target_pairs={{0,4},{4,0},{8,12},{12,8},{16,20},{20,16},{24,28},{28,24},{1,5},{5... | collective-permute-start | bytes 12582920 | tf_op jit(solution)/shard_map/ppermute | solution.py:109
  70.2 85.9 %all-to-all-start.6 = ((s32[8,2,64,128]{3,2,1,0:T(8,128)}), s32[8,2,64,128]{3,2,1,0:T(8,128)S(1)}, u32[]{:S(2)}, u32[]{:S(2)}) async-start(s32[8,2,64,128]{3,2,1,0:T(8,128)} %reshape.254), calls=%async_computation.6 | async-start | bytes 1048576 | tf_op jit(solution)/shard_map/all_to_all | solution.py:117
  74.8 299.7 %all-gather.15.cloned.1.call-start = ((), (), s32[]{:S(2)}) async-start(), calls=%async_computation.27 | async-start | bytes 10485760 | tf_op jit(solution)/shard_map/all_gather | solution.py:1009
  156.1 42.4 %all-to-all-start.2 = ((bf16[8,256,384]{2,1,0:T(8,128)(2,1)}), bf16[8,256,384]{2,1,0:T(8,128)(2,1)S(1)}, u32[]{:S(2)}, u32[]{:S(2)}) async-start(bf16[8,256,384]{2,1,0:T(8,128)(2,1)} %bitcast.170), calls=%async_computation.2 | async-start | bytes 3145728 | tf_op jit(solution)/shard_map/all_to_all | solution.py:117
  160.7 142.3 %collective-permute-start.4 = (bf16[4,512,2048]{2,1,0:T(8,128)(2,1)}, bf16[4,512,2048]{2,1,0:T(8,128)(2,1)}, u32[]{:S(2)}, u32[]{:S(2)}) collective-permute-start(bf16[4,512,2048]{2,1,0:T(8,128)(2,1)} %bitcast.158), channel_id=1, source_target_pairs={{0,4},{4,0},{8,12},{12,8},{16,20},{20,16},{24,28},{28,24},{1,5},{5... | collective-permute-start | bytes 25165832 | tf_op jit(solution)/shard_map/ppermute | solution.py:109
  199.7 41.3 %all-to-all-start = ((bf16[8,256,384]{2,1,0:T(8,128)(2,1)}), bf16[8,256,384]{2,1,0:T(8,128)(2,1)S(1)}, u32[]{:S(2)}, u32[]{:S(2)}) async-start(bf16[8,256,384]{2,1,0:T(8,128)(2,1)} %bitcast.168), calls=%async_computation | async-start | bytes 3145728 | tf_op jit(solution)/shard_map/all_to_all | solution.py:117
  217.5 79.0 %collective-permute-start.5 = (bf16[4,256,2048]{2,1,0:T(8,128)(2,1)}, bf16[4,256,2048]{2,1,0:T(8,128)(2,1)}, u32[]{:S(2)}, u32[]{:S(2)}) collective-permute-start(bf16[4,256,2048]{2,1,0:T(8,128)(2,1)} %bitcast.162), channel_id=1, source_target_pairs={{0,4},{4,0},{8,12},{12,8},{16,20},{20,16},{24,28},{28,24},{1,5},{5... | collective-permute-start | bytes 12582920 | tf_op jit(solution)/shard_map/ppermute | solution.py:109
  241.0 30.1 %all-to-all-start.5 = ((bf16[8,256,256]{2,1,0:T(8,128)(2,1)}), bf16[8,256,256]{2,1,0:T(8,128)(2,1)S(1)}, u32[]{:S(2)}, u32[]{:S(2)}) async-start(bf16[8,256,256]{2,1,0:T(8,128)(2,1)} %fusion.10), calls=%async_computation.5 | async-start | bytes 2097152 | tf_op jit(solution)/shard_map/all_to_all | solution.py:117
  290.6 47.4 %all-to-all-start.3 = ((bf16[8,256,128]{2,1,0:T(8,128)(2,1)}), bf16[8,256,128]{2,1,0:T(8,128)(2,1)S(1)}, u32[]{:S(2)}, u32[]{:S(2)}) async-start(bf16[8,256,128]{2,1,0:T(8,128)(2,1)} %get-tuple-element.217), calls=%async_computation.3 | async-start | bytes 1048576 | tf_op jit(solution)/shard_map/all_to_all | solution.py:117
  338.0 43.1 %all-to-all-start.4 = ((bf16[8,256,384]{2,1,0:T(8,128)(2,1)}), bf16[8,256,384]{2,1,0:T(8,128)(2,1)S(1)}, u32[]{:S(2)}, u32[]{:S(2)}) async-start(bf16[8,256,384]{2,1,0:T(8,128)(2,1)} %bitcast.169), calls=%async_computation.4 | async-start | bytes 3145728 | tf_op jit(solution)/shard_map/all_to_all | solution.py:117
  374.5 161.6 %collective-permute-start.6 = (bf16[4,512,2048]{2,1,0:T(8,128)(2,1)}, bf16[4,512,2048]{2,1,0:T(8,128)(2,1)}, u32[]{:S(2)}, u32[]{:S(2)}) collective-permute-start(bf16[4,512,2048]{2,1,0:T(8,128)(2,1)} %bitcast.156), channel_id=1, source_target_pairs={{0,4},{4,0},{8,12},{12,8},{16,20},{20,16},{24,28},{28,24},{1,5},{5... | collective-permute-start | bytes 25165832 | tf_op jit(solution)/shard_map/ppermute | solution.py:109
  381.1 72.7 %all-to-all-start.8 = ((bf16[8,256,384]{2,1,0:T(8,128)(2,1)}), bf16[8,256,384]{2,1,0:T(8,128)(2,1)S(1)}, u32[]{:S(2)}, u32[]{:S(2)}) async-start(bf16[8,256,384]{2,1,0:T(8,128)(2,1)} %bitcast.171), calls=%async_computation.8 | async-start | bytes 3145728 | tf_op jit(solution)/shard_map/all_to_all | solution.py:117
  454.9 74.1 %all-to-all-start.7 = ((bf16[8,256,128]{2,1,0:T(8,128)(2,1)}), bf16[8,256,128]{2,1,0:T(8,128)(2,1)S(1)}, u32[]{:S(2)}, u32[]{:S(2)}) async-start(bf16[8,256,128]{2,1,0:T(8,128)(2,1)} %get-tuple-element.227), calls=%async_computation.7 | async-start | bytes 1048576 | tf_op jit(solution)/shard_map/all_to_all | solution.py:117
  529.0 51.6 %all-to-all-start.9 = ((bf16[8,256,128]{2,1,0:T(8,128)(2,1)}), bf16[8,256,128]{2,1,0:T(8,128)(2,1)S(1)}, u32[]{:S(2)}, u32[]{:S(2)}) async-start(bf16[8,256,128]{2,1,0:T(8,128)(2,1)} %get-tuple-element.230), calls=%async_computation.9 | async-start | bytes 1048576 | tf_op jit(solution)/shard_map/all_to_all | solution.py:117
  580.6 66.0 %all-to-all-start.10 = ((bf16[8,256,128]{2,1,0:T(8,128)(2,1)}), bf16[8,256,128]{2,1,0:T(8,128)(2,1)S(1)}, u32[]{:S(2)}, u32[]{:S(2)}) async-start(bf16[8,256,128]{2,1,0:T(8,128)(2,1)} %get-tuple-element.235), calls=%async_computation.10 | async-start | bytes 1048576 | tf_op jit(solution)/shard_map/all_to_all | solution.py:117
  647.1 23.6 %all-to-all-start.12 = ((bf16[8,256,128]{2,1,0:T(8,128)(2,1)}), bf16[8,256,128]{2,1,0:T(8,128)(2,1)S(1)}, u32[]{:S(2)}, u32[]{:S(2)}) async-start(bf16[8,256,128]{2,1,0:T(8,128)(2,1)} %get-tuple-element.257), calls=%async_computation.12 | async-start | bytes 1048576 | tf_op jit(solution)/shard_map/all_to_all | solution.py:117
  651.9 244.0 %reduce-scatter.10.cloned.1.call-start = ((), (), s32[]{:S(2)}) async-start(), calls=%async_computation.28 | async-start | bytes 10485760
  738.5 72.3 %all-to-all-start.11 = ((bf16[8,256,384]{2,1,0:T(8,128)(2,1)}), bf16[8,256,384]{2,1,0:T(8,128)(2,1)S(1)}, u32[]{:S(2)}, u32[]{:S(2)}) async-start(bf16[8,256,384]{2,1,0:T(8,128)(2,1)} %get-tuple-element.255), calls=%async_computation.11 | async-start | bytes 3145728 | tf_op jit(solution)/shard_map/all_to_all | solution.py:117
  810.8 42.8 %all-to-all-start.13 = ((bf16[8,256,384]{2,1,0:T(8,128)(2,1)}), bf16[8,256,384]{2,1,0:T(8,128)(2,1)S(1)}, u32[]{:S(2)}, u32[]{:S(2)}) async-start(bf16[8,256,384]{2,1,0:T(8,128)(2,1)} %get-tuple-element.276), calls=%async_computation.13 | async-start | bytes 3145728 | tf_op jit(solution)/shard_map/all_to_all | solution.py:117
  815.8 186.9 %all-reduce.9.cloned.1.call-start = ((), (), s32[]{:S(2)}) async-start(), calls=%async_computation.21 | async-start | bytes 4194304 | tf_op jit(solution)/shard_map/psum | solution.py:294
  912.8 49.1 %all-to-all-start.14 = ((bf16[8,256,128]{2,1,0:T(8,128)(2,1)}), bf16[8,256,128]{2,1,0:T(8,128)(2,1)S(1)}, u32[]{:S(2)}, u32[]{:S(2)}) async-start(bf16[8,256,128]{2,1,0:T(8,128)(2,1)} %get-tuple-element.286), calls=%async_computation.14 | async-start | bytes 1048576 | tf_op jit(solution)/shard_map/all_to_all | solution.py:117
  916.3 141.7 %reduce-scatter.12.cloned.1.call-start = ((), (), s32[]{:S(2)}) async-start(), calls=%async_computation.29 | async-start | bytes 5242880
  962.7 34.6 %all-to-all-start.16 = ((bf16[8,256,128]{2,1,0:T(8,128)(2,1)}), bf16[8,256,128]{2,1,0:T(8,128)(2,1)S(1)}, u32[]{:S(2)}, u32[]{:S(2)}) async-start(bf16[8,256,128]{2,1,0:T(8,128)(2,1)} %get-tuple-element.310), calls=%async_computation.16 | async-start | bytes 1048576 | tf_op jit(solution)/shard_map/all_to_all | solution.py:117
  967.6 220.0 %all-reduce.11.cloned.1.call-start = ((), (), s32[]{:S(2)}) async-start(), calls=%async_computation.22 | async-start | bytes 2097152 | tf_op jit(solution)/shard_map/psum | solution.py:294
  1058.0 177.8 %reduce-scatter.14.cloned.1.call-start = ((), (), s32[]{:S(2)}) async-start(), calls=%async_computation.30 | async-start | bytes 10485760
  1072.0 63.3 %all-to-all-start.15 = ((bf16[8,256,384]{2,1,0:T(8,128)(2,1)}), bf16[8,256,384]{2,1,0:T(8,128)(2,1)S(1)}, u32[]{:S(2)}, u32[]{:S(2)}) async-start(bf16[8,256,384]{2,1,0:T(8,128)(2,1)} %get-tuple-element.307), calls=%async_computation.15 | async-start | bytes 3145728 | tf_op jit(solution)/shard_map/all_to_all | solution.py:117
  1135.2 52.5 %all-to-all-start.17 = ((bf16[8,256,384]{2,1,0:T(8,128)(2,1)}), bf16[8,256,384]{2,1,0:T(8,128)(2,1)S(1)}, u32[]{:S(2)}, u32[]{:S(2)}) async-start(bf16[8,256,384]{2,1,0:T(8,128)(2,1)} %get-tuple-element.321), calls=%async_computation.17 | async-start | bytes 3145728 | tf_op jit(solution)/shard_map/all_to_all | solution.py:117
  1138.8 225.0 %all-reduce.13.cloned.1.call-start = ((), (), s32[]{:S(2)}) async-start(), calls=%async_computation.23 | async-start | bytes 4194304 | tf_op jit(solution)/shard_map/psum | solution.py:294
  1149.4 26.0 %collective-permute-start.28 = (bf16[2,256,512]{2,1,0:T(8,128)(2,1)S(1)}, bf16[2,256,512]{2,1,0:T(8,128)(2,1)}, u32[]{:S(2)}, u32[]{:S(2)}) collective-permute-start(bf16[2,256,512]{2,1,0:T(8,128)(2,1)S(1)} %add_convert_fusion.5), channel_id=1, source_target_pairs={{0,1},{1,0},{2,3},{3,2},{4,5},{5,4},{6,7},{7,6},{8,9},{9,8},{10,11... | collective-permute-start | bytes 1572872 | tf_op jit(solution)/shard_map/ppermute | solution.py:310
  1176.5 81.0 %collective-permute-start.29 = (bf16[1,256,512]{2,1,0:T(8,128)(2,1)S(1)}, bf16[1,256,512]{2,1,0:T(8,128)(2,1)S(1)}, u32[]{:S(2)}, u32[]{:S(2)}) collective-permute-start(bf16[1,256,512]{2,1,0:T(8,128)(2,1)S(1)} %add_convert_fusion.17), channel_id=1, source_target_pairs={{0,2},{1,3},{2,0},{3,1},{4,6},{5,7},{6,4},{7,5},{8,10},{9,11},{10,... | collective-permute-start | bytes 786440 | tf_op jit(solution)/shard_map/ppermute | solution.py:310
  1268.3 27.5 %collective-permute-start.31 = (bf16[256,512]{1,0:T(8,128)(2,1)S(1)}, bf16[256,512]{1,0:T(8,128)(2,1)S(1)}, u32[]{:S(2)}, u32[]{:S(2)}) collective-permute-start(bf16[256,512]{1,0:T(8,128)(2,1)S(1)} %add_convert_fusion.15), channel_id=1, source_target_pairs={{8,16},{12,20},{16,8},{20,12},{9,17},{13,21},{17,9},{21,13},{10,18... | collective-permute-start | bytes 786440 | tf_op jit(solution)/shard_map/ppermute | solution.py:310
  1269.2 50.7 %collective-permute-start.38 = (bf16[512,2048]{1,0:T(8,128)(2,1)S(1)}, bf16[512,2048]{1,0:T(8,128)(2,1)}, u32[]{:S(2)}, u32[]{:S(2)}) collective-permute-start(bf16[512,2048]{1,0:T(8,128)(2,1)S(1)} %copy-done.7), channel_id=1, source_target_pairs={{0,4},{4,0},{8,12},{12,8},{16,20},{20,16},{24,28},{28,24},{1,5},{5... | collective-permute-start | bytes 6291464 | tf_op jit(solution)/shard_map/ppermute | solution.py:109
  1271.7 19.6 %collective-permute-start.22 = (bf16[2,256,768]{2,1,0:T(8,128)(2,1)S(1)}, bf16[2,256,768]{2,1,0:T(8,128)(2,1)S(1)}, u32[]{:S(2)}, u32[]{:S(2)}) collective-permute-start(bf16[2,256,768]{2,1,0:T(8,128)(2,1)S(1)} %add_convert_fusion.3), channel_id=1, source_target_pairs={{0,2},{1,3},{2,0},{3,1},{4,6},{5,7},{6,4},{7,5},{8,10},{9,11},{10,... | collective-permute-start | bytes 2359304 | tf_op jit(solution)/shard_map/ppermute | solution.py:310
  1275.2 21.9 %collective-permute-start.11 = (f32[4,2304]{1,0:T(4,128)S(1)}, f32[4,2304]{1,0:T(4,128)S(1)}, u32[]{:S(2)}, u32[]{:S(2)}) collective-permute-start(f32[4,2304]{1,0:T(4,128)S(1)} %pad_add_fusion.5), channel_id=1, source_target_pairs={{0,8},{4,12},{8,0},{12,4},{16,24},{20,28},{24,16},{28,20},{1,9},{5... | collective-permute-start | bytes 110600 | tf_op jit(solution)/shard_map/ppermute | solution.py:109
  1295.8 23.9 %collective-permute-start.32 = (bf16[256,512]{1,0:T(8,128)(2,1)S(1)}, bf16[256,512]{1,0:T(8,128)(2,1)S(1)}, u32[]{:S(2)}, u32[]{:S(2)}) collective-permute-start(bf16[256,512]{1,0:T(8,128)(2,1)S(1)} %add_convert_fusion.14), channel_id=1, source_target_pairs={{8,0},{12,4},{16,24},{20,28},{9,1},{13,5},{17,25},{21,29},{10,2},{... | collective-permute-start | bytes 786440 | tf_op jit(solution)/shard_map/ppermute | solution.py:310
  1297.1 28.8 %collective-permute-start.12 = (f32[4,2304]{1,0:T(4,128)S(1)}, f32[4,2304]{1,0:T(4,128)S(1)}, u32[]{:S(2)}, u32[]{:S(2)}) collective-permute-start(f32[4,2304]{1,0:T(4,128)S(1)} %add.210), channel_id=1, source_target_pairs={{0,16},{4,20},{8,24},{12,28},{16,0},{20,4},{24,8},{28,12},{1,17},{... | collective-permute-start | bytes 110600 | tf_op jit(solution)/shard_map/ppermute | solution.py:109
  1304.0 59.8 %collective-permute-start.24 = (bf16[256,768]{1,0:T(8,128)(2,1)S(1)}, bf16[256,768]{1,0:T(8,128)(2,1)S(1)}, u32[]{:S(2)}, u32[]{:S(2)}) collective-permute-start(bf16[256,768]{1,0:T(8,128)(2,1)S(1)} %fusion.1), channel_id=1, source_target_pairs={{0,8},{4,12},{24,16},{28,20},{1,9},{5,13},{25,17},{29,21},{2,10},{... | collective-permute-start | bytes 1179656 | tf_op jit(solution)/shard_map/ppermute | solution.py:310
  1312.3 52.3 %collective-permute-start.18 = (bf16[256,768]{1,0:T(8,128)(2,1)S(1)}, bf16[256,768]{1,0:T(8,128)(2,1)}, u32[]{:S(2)}, u32[]{:S(2)}) collective-permute-start(bf16[256,768]{1,0:T(8,128)(2,1)S(1)} %fusion), channel_id=1, source_target_pairs={{0,8},{4,12},{24,16},{28,20},{1,9},{5,13},{25,17},{29,21},{2,10},{... | collective-permute-start | bytes 1179656 | tf_op jit(solution)/shard_map/ppermute | solution.py:310
  1319.8 102.9 %collective-permute-start.35 = (bf16[256,512]{1,0:T(8,128)(2,1)S(1)}, bf16[256,512]{1,0:T(8,128)(2,1)}, u32[]{:S(2)}, u32[]{:S(2)}) collective-permute-start(bf16[256,512]{1,0:T(8,128)(2,1)S(1)} %broadcast_select_fusion.2.refs_2_), channel_id=1, source_target_pairs={{0,4},{4,0},{8,12},{12,8},{16,20},{20,16},{24,28},{28,24},{1,5},{5... | collective-permute-start | bytes 786440 | tf_op jit(solution)/shard_map/ppermute | solution.py:310
  1326.6 42.9 %collective-permute-start.13 = (f32[4,2304]{1,0:T(4,128)}, f32[4,2304]{1,0:T(4,128)}, u32[]{:S(2)}, u32[]{:S(2)}) collective-permute-start(f32[4,2304]{1,0:T(4,128)} %add.211), channel_id=1, source_target_pairs={{0,1},{1,0},{2,3},{3,2},{4,5},{5,4},{6,7},{7,6},{8,9},{9,8},{10,11... | collective-permute-start | bytes 110600 | tf_op jit(solution)/shard_map/ppermute | solution.py:113
  1363.8 51.5 %collective-permute-start.36 = (bf16[512,2048]{1,0:T(8,128)(2,1)}, bf16[512,2048]{1,0:T(8,128)(2,1)S(1)}, u32[]{:S(2)}, u32[]{:S(2)}) collective-permute-start(bf16[512,2048]{1,0:T(8,128)(2,1)} %all-reduce.13.cloned.1.call-done.refs_0_), channel_id=1, source_target_pairs={{0,4},{4,0},{8,12},{12,8},{16,20},{20,16},{24,28},{28,24},{1,5},{5... | collective-permute-start | bytes 6291464 | tf_op jit(solution)/shard_map/ppermute | solution.py:109
  1369.5 42.0 %collective-permute-start.37 = (bf16[256,2048]{1,0:T(8,128)(2,1)}, bf16[256,2048]{1,0:T(8,128)(2,1)}, u32[]{:S(2)}, u32[]{:S(2)}) collective-permute-start(bf16[256,2048]{1,0:T(8,128)(2,1)} %all-reduce.11.cloned.1.call-done.refs_0_), channel_id=1, source_target_pairs={{0,4},{4,0},{8,12},{12,8},{16,20},{20,16},{24,28},{28,24},{1,5},{5... | collective-permute-start | bytes 3145736 | tf_op jit(solution)/shard_map/ppermute | solution.py:109
  1372.5 27.5 %collective-permute-start.26 = (bf16[256,768]{1,0:T(8,128)(2,1)S(1)}, bf16[256,768]{1,0:T(8,128)(2,1)S(1)}, u32[]{:S(2)}, u32[]{:S(2)}) collective-permute-start(bf16[256,768]{1,0:T(8,128)(2,1)S(1)} %add_convert_fusion.6), channel_id=1, source_target_pairs={{8,0},{12,4},{16,24},{20,28},{9,1},{13,5},{17,25},{21,29},{10,2},{... | collective-permute-start | bytes 1179656 | tf_op jit(solution)/shard_map/ppermute | solution.py:310
  1374.9 32.8 %collective-permute-start.20 = (bf16[256,768]{1,0:T(8,128)(2,1)S(1)}, bf16[256,768]{1,0:T(8,128)(2,1)S(1)}, u32[]{:S(2)}, u32[]{:S(2)}) collective-permute-start(bf16[256,768]{1,0:T(8,128)(2,1)S(1)} %add_convert_fusion.10), channel_id=1, source_target_pairs={{8,0},{12,4},{16,24},{20,28},{9,1},{13,5},{17,25},{21,29},{10,2},{... | collective-permute-start | bytes 1179656 | tf_op jit(solution)/shard_map/ppermute | solution.py:310
  1400.1 22.6 %collective-permute-start.34 = (bf16[256,768]{1,0:T(8,128)(2,1)S(1)}, bf16[256,768]{1,0:T(8,128)(2,1)S(1)}, u32[]{:S(2)}, u32[]{:S(2)}) collective-permute-start(bf16[256,768]{1,0:T(8,128)(2,1)S(1)} %broadcast_select_fusion.refs_1_), channel_id=1, source_target_pairs={{0,4},{4,0},{8,12},{12,8},{16,20},{20,16},{24,28},{28,24},{1,5},{5... | collective-permute-start | bytes 1179656 | tf_op jit(solution)/shard_map/ppermute | solution.py:310
  (87 other events, 1772.1 us)
Sparse Core Ops, SparseCore 0:
  10.4 55.3 all-gather.8
  68.3 87.7 all-gather.10
  158.5 52.7 all-gather.12
  213.6 87.6 all-gather.14
  670.9 86.7 reduce-scatter.9
  896.1 106.6 all-reduce.8
  1006.3 51.6 reduce-scatter.11
  1060.4 76.1 all-reduce.10
  1139.7 96.0 reduce-scatter.13
  1269.5 94.3 all-reduce.12

commit v2 on v1

--- a/solution.py
+++ b/solution.py
@@ -111,10 +111,6 @@
 
 def swap_fsdp(x, bit):
     return lax.ppermute(x, "fsdp", xor_perm(lax.axis_size("fsdp"), bit))
-
-
-def exchange(x):
-    return lax.all_to_all(x, "ctx", 0, 0, tiled=False)
 
 
 def side_columns(side, half):
@@ -192,9 +188,8 @@
         last.wait()
 
 
-def unfold_weights(mine, weights, plan, core):
+def unfold_weights(mine, twin, weights, plan, core):
     count = lax.axis_size("fsdp")
-    twin = swap_ctx(mine, 1)
     shards = [w.shape[0] for w in weights]
     full = [(w.shape[0] * count, w.shape[1]) for w in weights]
     return pl.pallas_call(
@@ -257,19 +252,25 @@
 def reduce_steps(keep, send, bits):
     count = lax.axis_size("fsdp")
     ctx_count = lax.axis_size("ctx")
-    me_ctx = lax.axis_index("ctx")
-    core = me_ctx & 1
-    z = (me_ctx >> 1) & (LINE - 1)
     terms = [keep, (yield "ctx", xor_perm(ctx_count, 1), send)]
     left = count
     for bit in bits:
         left //= 2
         got = yield "fsdp", xor_perm(count, bit), add_terms([t[left:] for t in terms])
         terms = [t[:left] for t in terms] + [got]
-    mine = add_terms([t[0] for t in terms])
+    return add_terms([t[0] for t in terms])
+
+
+def lines():
+    return [[g for g in range(lax.axis_size("ctx")) if g % 2 == c] for c in range(2)]
+
+
+def line_steps(mine):
+    ctx_count = lax.axis_size("ctx")
+    z = (lax.axis_index("ctx") >> 1) & (LINE - 1)
+    stride = 2 * LINE
 
     def along(pairs):
-        stride = 2 * LINE
         return [
             (g * stride + 2 * a + c, g * stride + 2 * b + c)
             for g in range(ctx_count // stride)
@@ -281,17 +282,15 @@
     both = add_terms([inner, (yield "ctx", along([(1, 2), (2, 1)]), inner)])
     outer = yield "ctx", along([(1, 0), (2, 3)]), both
     full = jnp.where((z == 0) | (z == LINE - 1), outer, both)
-    bit = 2 * LINE
+    bit = stride
     while bit < ctx_count:
         full = add_terms([full, (yield "ctx", xor_perm(ctx_count, bit), full)])
         bit *= 2
     return full, (yield "ctx", xor_perm(ctx_count, 1), full)
 
 
-def sum_lines(mine):
-    ctx_count = lax.axis_size("ctx")
-    groups = [[g for g in range(ctx_count) if g % 2 == c] for c in range(2)]
-    return lax.psum(mine, "ctx", axis_index_groups=groups)
+def all_steps(keep, send, bits):
+    return (yield from line_steps((yield from reduce_steps(keep, send, bits))))
 
 
 class Lane:
@@ -302,22 +301,46 @@
     def add(self, key, steps):
         self.active.append((key, steps, next(steps)))
 
+    def advance(self, value=None):
+        operands = [request[2] for _, _, request in self.active]
+        if value is not None and operands:
+            value, operands = lax.optimization_barrier((value, operands))
+        left = []
+        for (key, steps, (axis, pairs, _)), operand in zip(self.active, operands):
+            try:
+                left.append((key, steps, steps.send(lax.ppermute(operand, axis, pairs))))
+            except StopIteration as stop:
+                self.done[key] = stop.value
+        self.active = left
+        return value
+
     def drain(self):
         while self.active:
-            left = []
-            for key, steps, (axis, pairs, operand) in self.active:
-                try:
-                    left.append((key, steps, steps.send(lax.ppermute(operand, axis, pairs))))
-                except StopIteration as stop:
-                    self.done[key] = stop.value
-            self.active = left
+            self.advance()
+
+
+class Turns:
+    def __init__(self):
+        self.last = None
+
+    def next(self, value):
+        if self.last is not None:
+            value, _ = lax.optimization_barrier((value, self.last))
+        return value
+
+    def ran(self, value):
+        self.last = value
+        return value
 
 
 def grad_kernel(key, a0, a1, k0, k1, s0, s1, *refs):
     keep, send = refs[-2:]
-    left0, left1 = a0[...], a1[...]
-    keep[0] = (dot_tn(left0, k0[...]) + dot_tn(left1, k1[...])).astype(BF16)
-    send[0] = (dot_tn(left0, s0[...]) + dot_tn(left1, s1[...])).astype(BF16)
+    shard, tile = keep.shape[1], k0.shape[1]
+    for n in range(a0.shape[1] // shard):
+        left0, left1 = (x[:, n * shard : (n + 1) * shard] for x in (a0, a1))
+        span = slice(n * tile, (n + 1) * tile)
+        keep[0, :, span] = (dot_tn(left0, k0[...]) + dot_tn(left1, k1[...])).astype(BF16)
+        send[0, :, span] = (dot_tn(left0, s0[...]) + dot_tn(left1, s1[...])).astype(BF16)
 
 
 def shard_order(bits):
@@ -338,21 +361,20 @@
     key = jnp.concatenate([core.reshape(1), order]).astype(jnp.int32)
     dims = dims or (count, shard, chunks * tiles * tile)
     row, column = place
-    a_spec = pl.BlockSpec((rows, shard), lambda i, t, k: (0, k[1 + i] * chunks + t // tiles))
+    a_spec = pl.BlockSpec((rows, chunks * shard), lambda t, i, k: (0, k[1 + i]))
 
     def b_spec(twin):
         return pl.BlockSpec(
-            (rows, tile),
-            lambda i, t, k: (0, (1 - k[0] if twin else k[0]) * across + first + t % tiles),
+            (rows, tile), lambda t, i, k: (0, (1 - k[0] if twin else k[0]) * across + first + t)
         )
 
-    o_spec = pl.BlockSpec((1, shard, tile), lambda i, t, k: (i, row, column + t))
+    o_spec = pl.BlockSpec((1, shard, chunks * tile), lambda t, i, k: (i, row, column + t))
     extra = list(into or [])
     return pl.pallas_call(
         grad_kernel,
         grid_spec=pltpu.PrefetchScalarGridSpec(
             num_scalar_prefetch=1,
-            grid=(count, chunks * tiles),
+            grid=(tiles, count),
             in_specs=[a_spec, a_spec, b_spec(False), b_spec(False), b_spec(True), b_spec(True)]
             + [anyspace()] * len(extra),
             out_specs=[o_spec, o_spec],
@@ -639,45 +661,54 @@
 
 
 def pick_scores(score_ref, index_ref, base, chunk):
-    rows = pl.ds(pl.multiple_of(chunk * CHUNK, CHUNK), CHUNK)
-    index = index_ref[pl.ds(pl.multiple_of(base + chunk * CHUNK, CHUNK), CHUNK), :]
-    low = index & (HD - 1)
-    high = index >> 7
-    found = jnp.zeros((CHUNK, HD), F32)
-    for tile in range(score_ref.shape[1] // HD):
-        part = jnp.take_along_axis(
-            score_ref[rows, tile * HD : (tile + 1) * HD], low, axis=1, mode="promise_in_bounds"
-        )
-        found = jnp.where(high == tile, part, found)
-    return found
+    parts = []
+    for r in range(CHUNK // 8):
+        at = chunk * CHUNK + r * 8
+        rows = pl.ds(pl.multiple_of(at, 8), 8)
+        index = index_ref[pl.ds(pl.multiple_of(base + at, 8), 8), :]
+        low = index & (HD - 1)
+        high = index >> 7
+        found = jnp.zeros((8, HD), F32)
+        for tile in range(score_ref.shape[1] // HD):
+            part = jnp.take_along_axis(
+                score_ref[rows, tile * HD : (tile + 1) * HD], low, axis=1, mode="promise_in_bounds"
+            )
+            found = jnp.where(high == tile, part, found)
+        parts.append(found)
+    return jnp.concatenate(parts, 0)
 
 
 def scatter_rows(value_ref, value_base, index_ref, flat_ref, base, dense_ref, group):
-    wide = 2 * HD
-    start = pl.multiple_of(base + group * 16, 16)
-    values = value_ref[pl.ds(pl.multiple_of(value_base + group * 16, 16), 16), :].astype(BF16)
-    high = (index_ref[pl.ds(start, 16), :] >> 8).astype(F32).astype(BF16)
-    query = lax.broadcasted_iota(jnp.int32, (16, HD), 0)
+    high_count = dense_ref.shape[1] // HD
+    row = lax.broadcasted_iota(jnp.int32, (16, HD), 0) & 7
     lane = lax.broadcasted_iota(jnp.int32, (16, HD), 1) >> 5
-    zero = jnp.zeros((16, HD), BF16)
-    spots = [
-        values * (query == lane + 4 * u).astype(F32).astype(BF16) for u in range(4)
-    ]
-    bands = []
-    for h in range(dense_ref.shape[1] // wide):
-        hit = high == jnp.array(h, BF16)
-        bands.append(jnp.concatenate([jnp.where(hit, spot, zero) for spot in spots], 1))
-    left = jnp.concatenate(bands, 0)
-    flat = (flat_ref[pl.ds(pl.multiple_of((base + group * 16) // 4, 4), 4), :] & (wide - 1)).astype(F32).astype(BF16)
-    place = lax.broadcasted_iota(jnp.int32, (wide, HD), 0).astype(F32).astype(BF16)
-    one, none = jnp.ones((wide, HD), BF16), jnp.zeros((wide, HD), BF16)
-    right = jnp.concatenate(
-        [jnp.where(place == flat[u : u + 1, :], one, none) for u in range(4)], 1
-    )
-    spreadout = dot_nt(left, right)
+    masks = [(row == lane + 4 * u).astype(F32).astype(BF16) for u in range(2)]
+    place = lax.broadcasted_iota(jnp.int32, (HD, HD), 0).astype(F32).astype(BF16)
+    zero, one, none = jnp.zeros((16, HD), BF16), jnp.ones((HD, HD), BF16), jnp.zeros((HD, HD), BF16)
+    found = []
+    for g in range(2):
+        at = group * 16 + g * 8
+        value = value_ref[pl.ds(pl.multiple_of(value_base + at, 8), 8), :]
+        high = (index_ref[pl.ds(pl.multiple_of(base + at, 8), 8), :] >> 7).astype(F32)
+        value = jnp.concatenate([value, value], 0).astype(BF16)
+        high = jnp.concatenate([high, high - 1.0], 0).astype(BF16)
+        spots = [value * mask for mask in masks]
+        bands = []
+        for h in range(0, high_count, 2):
+            hit = high == jnp.array(h, BF16)
+            bands.append(jnp.concatenate([jnp.where(hit, spot, zero) for spot in spots], 1))
+        left = jnp.concatenate(bands, 0)
+        columns = []
+        for u in range(2):
+            flat = flat_ref[pl.ds((base + at) // 4 + u, 1), :]
+            flat = jnp.broadcast_to(flat, (16, HD)).astype(BF16)
+            flat = jnp.concatenate([flat] * (HD // 16), 0)
+            columns.append(jnp.where(place == flat, one, none))
+        found.append(dot_nt(left, jnp.concatenate(columns, 1)))
     rows = pl.ds(pl.multiple_of(group * 16, 16), 16)
-    for h in range(dense_ref.shape[1] // wide):
-        dense_ref[rows, h * wide : (h + 1) * wide] = spreadout[h * 16 : (h + 1) * 16, :].astype(BF16)
+    for h in range(high_count):
+        both = [f[h * 8 : (h + 1) * 8, :] for f in found]
+        dense_ref[rows, h * HD : (h + 1) * HD] = jnp.concatenate(both, 0).astype(BF16)
 
 
 def attend_kernel(recall, count, info, rel, buckets, pieces, *refs):
@@ -731,22 +762,22 @@
             mixed[mine, :] = dot(prob, values[pl.ds(row, SPAN), :])
         if recall:
             tile = pl.ds(base, ROWS)
-            scores[...] = dot_nt(queries[tile, :], mem[:, :HD]) * SCALE
+            scores[...] = dot_nt(queries[tile, :], mem[:, :HD])
 
             def choose(chunk, inner):
-                found = pick_scores(scores, index, base, chunk)
+                found = pick_scores(scores, index, base, chunk) * SCALE
                 exps = jnp.exp(found - jnp.max(found, -1, keepdims=True))
                 weight = exps * ((HD // TOPK) / jnp.sum(exps, -1, keepdims=True))
                 weights[pl.ds(pl.multiple_of(base + chunk * CHUNK, CHUNK), CHUNK), :] = weight
                 return inner
 
-            lax.fori_loop(0, ROWS // CHUNK, choose, 0)
+            lax.fori_loop(0, ROWS // CHUNK, choose, 0, unroll=4)
 
             def place(group, inner):
                 scatter_rows(weights, base, index, flat, base, dense, group)
                 return inner
 
-            lax.fori_loop(0, ROWS // 16, place, 0)
+            lax.fori_loop(0, ROWS // 16, place, 0, unroll=16)
             found = dot(dense[...], mem[:, HD:])
             near = mixed[tile, :]
             gap[tile, :] = found - near
@@ -848,13 +879,13 @@
                 picked[local_rows, :] = product - weight * centre
                 return inner
 
-            lax.fori_loop(0, ROWS // CHUNK, choose, 0)
+            lax.fori_loop(0, ROWS // CHUNK, choose, 0, unroll=4)
 
             def place(group, inner):
                 scatter_rows(picked, 0, index, flat, base, dense, group)
                 return inner
 
-            lax.fori_loop(0, ROWS // 16, place, 0)
+            lax.fori_loop(0, ROWS // 16, place, 0, unroll=16)
             dq[tile, :] += dot(dense[...], mem[:, :HD]) * SCALE
         return carry
 
@@ -912,7 +943,7 @@
     return list(result[:-1]), result[-1]
 
 
-def memory_rows(keys, values):
+def memory_rows(keys, values, exchange):
     count = lax.axis_size("ctx")
 
     def pieces(array):
@@ -923,7 +954,7 @@
     return exchange(stacked).reshape(count * ROWS, 2 * HD)
 
 
-def memory_index(mem_index):
+def memory_index(mem_index, exchange):
     count = lax.axis_size("ctx")
     micro = mem_index.shape[0]
     by_head = jnp.transpose(mem_index, (2, 0, 1, 3)).reshape(HEADS, micro, ROWS * TOPK // HD, HD)
@@ -932,7 +963,7 @@
     for m in range(micro):
         flat = got[:, m].reshape(-1, HD)
         index = jnp.tile(flat.reshape(count * ROWS, TOPK), (1, HD // TOPK))
-        result.append((index, flat))
+        result.append((index, (flat & (HD - 1)).astype(F32)))
     return result
 
 
@@ -990,65 +1021,97 @@
     wide = layers[0][7].shape[1]
     chunks = layers[0][8].shape[0] // shard
     half, half_qkv, half_in = width // 2, 3 * width // 2, wide // 2
-    plan_a = [(0, 0, shard, half_qkv, 0, 0), (1, 0, shard, half, 0, half_qkv)]
-    plan_b = [(0, 0, shard, half_in, 0, 0)] + [
-        (1, n * shard, shard, half, shard, n * half) for n in range(chunks)
-    ]
-
+    quarter = shard // 4
+    down = [(n * shard, shard, half, n * half) for n in range(chunks)]
     groups = [
-        (n, ids, plan, units * shard)
-        for n in range(2)
-        for ids, plan, units in (((2, 4), plan_a, 1), ((7, 8), plan_b, 2))
+        ([(0, 2)], [(0, 0, shard, half_qkv, 0, 0)], shard),
+        (
+            [(0, 4), (1, 2), (0, 7), (0, 8)],
+            [
+                (0, 0, shard, half, 0, 0),
+                (1, 0, shard, half_qkv, 0, half),
+                (2, 0, shard, half_in, shard, 0),
+            ]
+            + [(3, row, rows, wide_half, 2 * shard, col) for row, rows, wide_half, col in down],
+            3 * shard,
+        ),
+        (
+            [(1, 7), (1, 8), (1, 4)],
+            [(0, 0, shard, half_in, 0, 0)]
+            + [(1, row, rows, wide_half, shard, col) for row, rows, wide_half, col in down]
+            + [(2, n * quarter, quarter, half, 2 * shard, n * half) for n in range(4)],
+            2 * shard + quarter,
+        ),
     ]
     packed = []
-    for n, ids, plan, count_rows in groups:
-        raw = [layers[n][i] for i in ids]
+    for ids, plan, count_rows in groups:
+        raw = [layers[n][i] for n, i in ids]
         if packed:
             packed[-1], raw = tie((packed[-1], raw))
         packed.append(pack(raw, plan, count_rows, core))
     gathered = [lax.all_gather(p, "fsdp", axis=0, tiled=False) for p in packed]
     full = [{}, {}]
 
-    def unfold(g, value):
-        n, ids, plan, _ = groups[g]
-        mine = gathered[g]
-        if value is not None:
-            value, mine = tie((value, mine))
-        for i, w in zip(ids, unfold_weights(mine, [layers[n][i] for i in ids], plan, core)):
+    twins = {}
+    turns = Turns()
+
+    def hand_over(g, value):
+        value, gathered[g] = tie((value, gathered[g]))
+        twins[g] = swap_ctx(gathered[g], 1)
+        return value
+
+    def unfold(g):
+        ids, plan, _ = groups[g]
+        raw = [layers[n][i] for n, i in ids]
+        result = unfold_weights(turns.next(gathered[g]), twins[g], raw, plan, core)
+        for (n, i), w in zip(ids, result):
             full[n][i] = w
-        return value
-
-    unfold(0, None)
+        turns.ran(result[0])
+
 
     infos = [
         jnp.concatenate([block_slots[m, 0], doc_starts[m, 0]]).astype(jnp.int32) for m in range(micro)
     ]
-    rows = memory_rows(mem_keys[0], mem_values[0])
-    indices = memory_index(mem_index[:, 0])
+    links = Turns()
+
+    def exchange(x):
+        return links.ran(lax.all_to_all(links.next(x), "ctx", 0, 0, tiled=False))
+
+    rows = memory_rows(mem_keys[0], mem_values[0], exchange)
+    indices = memory_index(mem_index[:, 0], exchange)
+    hand_over(0, links.last)
+    unfold(0)
     memories = [(rows, *indices[m]) for m in range(micro)]
 
     state = [inputs[m, 0] for m in range(micro)]
-    kept = [[None] * micro, [None] * micro]
+    kept = [None, None]
+    projected = [{} for _ in range(micro)]
     for n in range(2):
         gain_in, bias_in, gain_mid, bias_mid = norms[n]
         w = full[n]
         work = [dict(x=state[m]) for m in range(micro)]
+
+        def project(m):
+            work[m]["n1"], pieces = qkv_forward(turns.next(work[m]["x"]), gain_in, bias_in, w[2])
+            work[m]["pieces"] = exchange(turns.ran(pieces))
+
+        if n == 0:
+            for m in range(micro):
+                project(m)
         for m in range(micro):
-            work[m]["n1"], pieces = qkv_forward(work[m]["x"], gain_in, bias_in, w[2])
+            pieces = turns.next(projected[m]["pieces"] if n else work[m]["pieces"])
             if m == micro - 1:
-                pieces = unfold(1 + 2 * n, pieces)
-            work[m]["pieces"] = exchange(pieces)
+                pieces = hand_over(1 + n, pieces)
+            work[m]["saved"], outs = attend(
+                pieces, infos[m], mine[n], buckets, memories[m] if n else None
+            )
+            work[m]["outs"] = exchange(turns.ran(outs))
+        unfold(1 + n)
         for m in range(micro):
-            work[m]["saved"], outs = attend(
-                work[m]["pieces"], infos[m], mine[n], buckets, memories[m] if n else None
-            )
-            if n == 0 and m == micro - 1:
-                outs = unfold(2, outs)
-            work[m]["outs"] = exchange(outs)
-        for m in range(micro):
+            outs = turns.next(work[m]["outs"])
             mixed, hidden, normed_mid, up, act, state[m] = mlp_forward(
                 work[m]["x"],
-                work[m]["outs"],
+                outs,
                 w[4],
                 gain_mid,
                 bias_mid,
@@ -1056,118 +1119,162 @@
                 w[8],
                 BF16 if n else F32,
             )
+            turns.ran(act)
             work[m].update(mixed=mixed, hidden=hidden, n2=normed_mid, up=up, act=act)
+            if n == 0:
+                gain, bias = norms[1][:2]
+                projected[m]["n1"], pieces = qkv_forward(
+                    turns.next(state[m]), gain, bias, full[1][2]
+                )
+                projected[m]["pieces"] = exchange(turns.ran(pieces))
+        if n:
+            for m in range(micro):
+                work[m]["n1"] = projected[m]["n1"]
         kept[n] = work
     outputs = jnp.stack(state)[:, None]
 
     lane = Lane()
     smalls = [None, None]
-    top = [out_grad[m, 0] for m in range(micro)]
-    top_low = top
 
     def pair(source, name):
         return [item[name] for item in source]
 
+    def grad_pair(a, *rest, bits=None, **more):
+        both = weight_grad([turns.next(a[0]), *a[1:]], *rest, bits=bits, **more)
+        return turns.ran(both)
+
     def launch(key, bits, *what):
-        lane.add(key, reduce_steps(*weight_grad(*what, bits=bits), bits))
-
-    def chip_sum(keep, send):
-        return add_terms([keep, swap_ctx(send, 1)])
+        lane.add(key, reduce_steps(*grad_pair(*what, bits=bits), bits))
 
     def shard_sum(x):
         return lax.psum_scatter(x, "fsdp", scatter_dimension=0, tiled=False)
 
+    def dense_back(n, m, grad):
+        k = kept[n][m]
+        w = full[n]
+        du, hb, dh, g_gain, g_bias, pieces = mlp_backward(
+            turns.next(grad), k["up"], w[7], w[8], k["hidden"], norms[n][2], w[4]
+        )
+        turns.ran(pieces)
+        back[n][m].update(
+            du=du, hb=hb, dh=dh, norms=[g_gain, g_bias], pieces=exchange(pieces)
+        )
+
+    def heads_back(n, m, pieces):
+        item = back[n][m]
+        item["extra"], outs = attend_back(
+            turns.next(pieces), infos[m], mine[n], buckets, kept[n][m]["saved"],
+            memories[m] if n else None,
+        )
+        item["outs"] = exchange(turns.ran(outs))
+
+    def input_back(n, m, outs):
+        k, item = kept[n][m], back[n][m]
+        dqkv, dx, dx_low, g_gain, g_bias = qkv_backward(
+            k["x"], norms[n][0], item["dh"], full[n][2], turns.next(outs)
+        )
+        turns.ran(dqkv)
+        item.update(dqkv=dqkv, dx=dx, dx_low=dx_low)
+        item["norms"] = [g_gain, g_bias] + item["norms"]
+
+    def grad_b(n, top_low):
+        ks, items = kept[n], back[n]
+        both = grad_pair(
+            pair(ks, "n2"), pair(items, "du"), shard, width, 0, half_in // width, dims=dims_b
+        )
+        return grad_pair(
+            pair(ks, "act"), top_low, shard, half, 0, 1, into=both, place=(1, 0), dims=dims_b
+        )
+
+    back = [[{} for _ in range(micro)] for _ in range(2)]
     dims_a = (fsdp, shard, 2 * width)
     dims_b = (fsdp, 2 * shard, half_in)
-    sums = {}
-    for n in (1, 0):
-        gain_in, bias_in, gain_mid, bias_mid = norms[n]
-        w = full[n]
-        ks = kept[n]
-        back = [None] * micro
-        for m in range(micro):
-            k = ks[m]
-            grad = top[m]
-            if n == 0 and m == 0:
-                grad, sums["b1"], sums["a1"] = tie((grad, sums["b1"], sums["a1"]))
-                sums["b1"] = sum_lines(sums["b1"])
-                sums["a1"] = shard_sum(sums["a1"])
-            du, hb, dh, g_gain_mid, g_bias_mid, pieces = mlp_backward(
-                grad, k["up"], w[7], w[8], k["hidden"], gain_mid, w[4]
-            )
-            back[m] = dict(
-                du=du, hb=hb, dh=dh, norms=[g_gain_mid, g_bias_mid], pieces=exchange(pieces)
-            )
-        act, n2, mixed = pair(ks, "act"), pair(ks, "n2"), pair(ks, "mixed")
-        du, hb = pair(back, "du"), pair(back, "hb")
-        both = weight_grad(n2, du, shard, width, 0, half_in // width, dims=dims_b)
-        both = weight_grad(act, top_low, shard, half, 0, 1, into=both, place=(1, 0), dims=dims_b)
-        back[0]["pieces"], both = tie((back[0]["pieces"], both))
-        chip = chip_sum(*both)
-        for m in range(micro):
-            pieces = back[m]["pieces"]
-            if m == 1:
-                pieces, chip = tie((pieces, chip))
-                sums["b%d" % n] = shard_sum(chip)
-                if n == 0:
-                    pieces, sums["a1"], sums["b1"] = tie((pieces, sums["a1"], sums["b1"]))
-                    sums["a1"] = sum_lines(sums["a1"])
-            back[m]["extra"], outs = attend_back(
-                pieces, infos[m], mine[n], buckets, ks[m]["saved"], memories[m] if n else None
-            )
-            back[m]["outs"] = exchange(outs)
-        for m in range(micro):
-            k = ks[m]
-            outs = back[m]["outs"]
-            if n == 0 and m == 1:
-                outs, sums["b0"], sums["a1"] = tie((outs, sums["b0"], sums["a1"]))
-                sums["b0"] = sum_lines(sums["b0"])
-            dqkv, dx, dx_low, g_gain_in, g_bias_in = qkv_backward(
-                k["x"], gain_in, back[m]["dh"], w[2], outs
-            )
-            back[m].update(dqkv=dqkv, dx=dx, dx_low=dx_low)
-            back[m]["norms"] = [g_gain_in, g_bias_in] + back[m]["norms"]
-        n1, dqkv = pair(ks, "n1"), pair(back, "dqkv")
-        if n:
-            both = weight_grad(n1, dqkv, shard, half, 0, 3, dims=dims_a)
-            both = weight_grad(mixed, hb, shard, half, 0, 1, into=both, place=(0, 3), dims=dims_a)
-            sums["a1"] = chip_sum(*both)
-        else:
-            launch("out", ups, mixed, hb, shard, half, 0, 1)
-            launch("low", ups, n1, dqkv, shard, half_qkv // 2, 0, 1)
-            launch("high", downs, n1, dqkv, shard, half_qkv // 2, 1, 1)
+    top = [out_grad[m, 0] for m in range(micro)]
+    for m in range(micro):
+        dense_back(1, m, top[m])
+    keep_b, send_b = grad_b(1, top)
+    pieces, send_b = tie((back[1][0]["pieces"], send_b))
+    got_b = swap_ctx(send_b, 1)
+    heads_back(1, 0, pieces)
+    pieces, chip = tie((back[1][1]["pieces"], add_terms([keep_b, turns.next(got_b)])))
+    sum_b = shard_sum(chip)
+    heads_back(1, 1, pieces)
+    both = grad_pair(
+        pair(kept[1], "mixed"), pair(back[1], "hb"), shard, half, 0, 1, place=(0, 3), dims=dims_a
+    )
+    for m in range(micro):
+        outs = back[1][m]["outs"]
+        if m == 1:
+            outs, sum_b = tie((outs, sum_b))
+            full_b = lax.psum(sum_b, "ctx", axis_index_groups=lines())
+        input_back(1, m, outs)
+        dense_back(0, m, back[1][m]["dx"])
+    heads_back(0, 0, back[0][0]["pieces"])
+    for key, bits, left, right, tile in (
+        ("in0", ups, pair(kept[0], "n2"), pair(back[0], "du"), width),
+        ("down0", downs, pair(kept[0], "act"), pair(back[1], "dx_low"), half),
+    ):
+        tiles = right[0].shape[1] // 2 // tile
+        both_0 = grad_pair(left, right, shard, tile, 0, tiles, bits=bits)
+        lane.add(key, all_steps(*both_0, bits))
+    heads_back(0, 1, lane.advance(back[0][1]["pieces"]))
+    keep_a, send_a = grad_pair(
+        pair(kept[1], "n1"), pair(back[1], "dqkv"), shard, half_qkv, 0, 1, into=both, dims=dims_a
+    )
+    got_a = swap_ctx(send_a, 1)
+    input_back(0, 0, lane.advance(back[0][0]["outs"]))
+    outs, chip = tie((back[0][1]["outs"], add_terms([keep_a, turns.next(got_a)])))
+    sum_a = shard_sum(chip)
+    input_back(0, 1, lane.advance(outs))
+    n1, dqkv = pair(kept[0], "n1"), pair(back[0], "dqkv")
+    launch("low", ups, n1, dqkv, shard, half_qkv // 2, 0, 1)
+    launch("high", downs, n1, dqkv, shard, half_qkv // 2, 1, 1)
+    launch("out", ups, pair(kept[0], "mixed"), pair(back[0], "hb"), shard, half, 0, 1)
+    full_b = turns.next(full_b)
+    lane.done["b1"] = full_b, swap_ctx(full_b, 1)
+    lane.add("a1", line_steps(sum_a))
+    top = pair(back[0], "dx")
+    for n in range(2):
+        items = back[n]
         share = HEADS / count
         spot = (jnp.arange(HEADS) == my_head).astype(F32) * share
-        rel = jnp.sum(sum(item["extra"][0] for item in back), -1)
-        parts = [sum(item["norms"][i] for item in back).reshape(fsdp, -1) for i in range(4)]
+        rel = jnp.sum(sum(item["extra"][0] for item in items), -1)
+        parts = [sum(item["norms"][i] for item in items).reshape(fsdp, -1) for i in range(4)]
         parts.append((spot[:, None] * rel[None, :]).reshape(fsdp, -1))
         if n:
-            value = sum(jnp.sum(item["extra"][1]) for item in back) * (gate * (1.0 - gate))[0]
+            value = sum(jnp.sum(item["extra"][1]) for item in items) * (gate * (1.0 - gate))[0]
             parts.append((spot * value).reshape(fsdp, -1))
         smalls[n] = parts
-        top = pair(back, "dx")
-        top_low = pair(back, "dx_low")
+    lane.drain()
+    last = jnp.concatenate([lane.done[key] for key in ("low", "high", "out")], 1)
+    for n in range(2):
+        lane.add("a0%d" % n, line_steps(last[n * (shard // 2) : (n + 1) * (shard // 2)]))
     lane.drain()
     dims = [(shard, 3 * width), (shard, width), (shard, wide), (chunks * shard, width)]
 
     def joined(parts, plan, sizes):
         return merge([p[0] for p in parts], [p[1] for p in parts], plan, sizes, core)
 
-    ready = {key: (value, swap_ctx(value, 1)) for key, value in sums.items()}
-    move_b = [(0, 0, shard, half_in, 0, 0, 0, 0, half_in)] + [
-        (1, n * shard, shard, half, 0, shard, n * half, 0, half) for n in range(chunks)
-    ]
+    done = lane.done
+    move_in = (0, 0, shard, half_in, 0, 0, 0, 0, half_in)
     move_qkv = (0, 0, shard, half_qkv, 0, 0, 0, 0, half_qkv)
     move_out = (1, 0, shard, half, 0, 0, half_qkv, 0, half)
+
+    def move_down(n, row):
+        return [(1, i * shard, shard, half, n, row, i * half, 0, half) for i in range(chunks)]
+
     grads = [{}, {}]
-    for n in range(2):
-        grads[n][7], grads[n][8] = joined([ready["b%d" % n]], move_b, dims[2:])
-    grads[1][2], grads[1][4] = joined([ready["a1"]], [move_qkv, move_out], dims[:2])
-    size = half_qkv // 2
-    moves = [(0, 0, shard, half_qkv, n, 0, 0, n * size, size) for n in range(2)]
-    moves.append((1, 0, shard, half, 2, 0, 0, 0, half))
-    done = lane.done
-    grads[0][2], grads[0][4] = joined([done["low"], done["high"], done["out"]], moves, dims[:2])
+    grads[1][7], grads[1][8] = joined([done["b1"]], [move_in] + move_down(0, shard), dims[2:])
+    parts = [done["in0"], done["down0"]]
+    grads[0][7], grads[0][8] = joined(parts, [move_in] + move_down(1, 0), dims[2:])
+    grads[1][2], grads[1][4] = joined([done["a1"]], [move_qkv, move_out], dims[:2])
+    mid = shard // 2
+    moves = [
+        (i, n * mid, mid, wide_half, n, 0, col, 0, wide_half)
+        for n in range(2)
+        for i, wide_half, col in ((0, half_qkv, 0), (1, half, half_qkv))
+    ]
+    grads[0][2], grads[0][4] = joined([done["a00"], done["a01"]], moves, dims[:2])
 
     flat = jnp.concatenate(smalls[0] + smalls[1], 1)
     columns = flat.shape[1]

time: 1450 us -> 1130 us (0.78)
  Pallas kernels: 679 us -> 515 us
  waiting for transfers between devices: 503 us -> 342 us
    all_gather x4 -> x3, waiting for transfers between devices: 107 us -> 1.13 us  [local(): gathered = [lax.all_gather(p, 'fsdp', axis=0, tiled=False) for p in packed]]
    unnamed x13 -> x8, waiting for transfers between devices: 104 us -> 0.12 us
    ppermute x21 -> x35, waiting for transfers between devices: 73.2 us -> 170 us  [advance(): left.append((key, steps, steps.send(lax.ppermute(operand, axis, pairs))))]
    pallas_call x4, Pallas kernels: 162 us -> 90.6 us  [attend(): pl.pallas_call(functools.partial(attend_kernel, recall, count), grid=(1,)...]
    pallas_call x4, Pallas kernels: 161 us -> 91.3 us  [attend_back(): pl.pallas_call(functools.partial(attend_back_kernel, recall, count), grid...]
    psum x3 -> x1, waiting for transfers between devices: 41.3 us -> 0.01 us  [local(): full_b = lax.psum(sum_b, 'ctx', axis_index_groups=lines())]
    ppermute x13 -> x9, waiting for transfers between devices: 22.8 us -> 0.02 us  [swap_ctx(): return lax.ppermute(x, 'ctx', xor_perm(lax.axis_size('ctx'), bit))]
    pallas_call x9, Pallas kernels: 92.9 us -> 72.3 us  [weight_grad(): pl.pallas_call(grad_kernel, grid_spec=pltpu.PrefetchScalarGridSpec(num_sc...]
  transfers between devices with their start and end apart: 66 -> 72, of which waited for: 26 -> 26; matrix products, arithmetic and copies ran while one was open for 6% -> 8% of each run, Pallas kernels for 47% -> 43%
where the time goes in v2:
time: 1130 us; the launch traced here: 1110 us
  Pallas kernels  515 us (46%)
  waiting for transfers between devices  342 us (30%)
  starting transfers between devices  124 us (11%)
  other arithmetic  67 us (6%)
  local copies, waits for them, and re-layouts  28 us (2%)
  between operations  18.8 us (2%)
  blocking collectives  18.4 us (2%)
    ppermute x35, waiting for transfers between devices, advance(): left.append((key, steps, steps.send(lax.ppermute(operand, axis, pairs))))  170 us
    all_to_all x17, waiting for transfers between devices, exchange(): return links.ran(lax.all_to_all(links.next(x), 'ctx', 0, 0, tiled=False))  160 us
    pallas_call x4, Pallas kernels, attend_back(): pl.pallas_call(functools.partial(attend_back_kernel, recall, count), grid...  91.3 us
    pallas_call x4, Pallas kernels, attend(): pl.pallas_call(functools.partial(attend_kernel, recall, count), grid=(1,)...  90.6 us
    all_to_all x17, starting transfers between devices, exchange(): return links.ran(lax.all_to_all(links.next(x), 'ctx', 0, 0, tiled=False))  75.6 us
    pallas_call x9, Pallas kernels, weight_grad(): pl.pallas_call(grad_kernel, grid_spec=pltpu.PrefetchScalarGridSpec(num_sc...  72.3 us
    pallas_call x4, Pallas kernels, mlp_backward(): pl.pallas_call(functools.partial(mlp_back_kernel, steps), grid=(steps,),...  67.5 us
    pallas_call x4, Pallas kernels, mlp_forward(): pl.pallas_call(functools.partial(mlp_kernel, steps), grid=(steps,), in_sp...  63 us
  transfers between devices with their start and end apart: 72, of which 26 were waited for; matrix products, arithmetic and copies ran while one was open for 8% of the time, Pallas kernels for 43%

profile of v2, /device:TPU:0, one launch (start us, length us, event | category | flops | bytes accessed | tf_op | source)
XLA Modules:
  0.0 1113.8 jit_solution(15657907874869446352)
XLA Ops:
  27.3 25.5 %all-to-all-done = bf16[8,256,256]{2,1,0:T(8,128)(2,1)} async-done(((bf16[8,256,256]{2,1,0:T(8,128)(2,1)}), bf16[8,256,256]{2,1,0:T(8,128)(2,1)}, u32[]{:S(2)}, u32[]{:S(2)}) %all-to-all-start) | async-done | bytes 1048608 | tf_op jit(solution)/shard_map/all_to_all | solution.py:1078
  52.8 18.4 %all_to_all.90 = s32[8,2,64,128]{3,2,1,0:T(8,128)} all-to-all(s32[8,2,64,128]{3,2,1,0:T(8,128)S(1)} %reshape.258), channel_id=1, replica_groups=mesh['ctx'=8,'fsdp'=4] {'ctx'}, dimensions={0} | all-to-all | bytes 1048576 | tf_op jit(solution)/shard_map/all_to_all | solution.py:1078
  90.2 7.2 qkv.4
  101.0 7.2 qkv.5
  108.2 30.5 %all-to-all-done.2.pieces = bf16[8,256,384]{2,1,0:T(8,128)(2,1)S(1)} async-done(((bf16[8,256,384]{2,1,0:T(8,128)(2,1)}), bf16[8,256,384]{2,1,0:T(8,128)(2,1)S(1)}, u32[]{:S(2)}, u32[]{:S(2)}) %all-to-all-start.2) | async-done | bytes 1572896 | tf_op jit(solution)/shard_map/all_to_all | solution.py:1078
  146.2 12.1 %local_attend.2 = (bf16[2048,128]{1,0:T(8,128)(2,1)}, bf16[2560,128]{1,0:T(8,128)(2,1)}, bf16[2560,128]{1,0:T(8,128)(2,1)}, bf16[16,128,640]{2,1,0:T(8,128)(2,1)}, bf16[8,256,128]{2,1,0:T(8,128)(2,1)}) custom-call(s32[20]{0:T(128)} %get-tuple-element.604.info, f32[33]{0:T(128)} %pad_maximum_fusion.2.rel, s32[128,640]{1,0:T(8,128)} %constant.64.clone.buckets, ...), custom_call_target="tpu_custom_call" | custom-call | flops 12000000000 | bytes 8000000 | tf_op jit(solution)/shard_map/local_attend/pallas_call | solution.py:811
  158.3 22.9 %all-to-all-done.3.pieces = bf16[8,256,384]{2,1,0:T(8,128)(2,1)S(1)} async-done(((bf16[8,256,384]{2,1,0:T(8,128)(2,1)}), bf16[8,256,384]{2,1,0:T(8,128)(2,1)S(1)}, u32[]{:S(2)}, u32[]{:S(2)}) %all-to-all-start.3) | async-done | bytes 1572896 | tf_op jit(solution)/shard_map/all_to_all | solution.py:1078
  190.2 12.1 %local_attend.3 = (bf16[2048,128]{1,0:T(8,128)(2,1)}, bf16[2560,128]{1,0:T(8,128)(2,1)}, bf16[2560,128]{1,0:T(8,128)(2,1)}, bf16[16,128,640]{2,1,0:T(8,128)(2,1)}, bf16[8,256,128]{2,1,0:T(8,128)(2,1)}) custom-call(s32[20]{0:T(128)} %get-tuple-element.605.info, f32[33]{0:T(128)} %pad_maximum_fusion.2.rel, s32[128,640]{1,0:T(8,128)} %constant.64.clone.buckets, ...), custom_call_target="tpu_custom_call" | custom-call | flops 12000000000 | bytes 8000000 | tf_op jit(solution)/shard_map/local_attend/pallas_call | solution.py:811
  211.4 18.1 %unfold.4 = (bf16[1024,1024]{1,0:T(8,128)(2,1)}, bf16[1024,3072]{1,0:T(8,128)(2,1)}, bf16[1024,4096]{1,0:T(8,128)(2,1)}, bf16[4096,1024]{1,0:T(8,128)(2,1)}) custom-call(s32[1]{0:T(128)} %bitcast.1.key, bf16[4,768,2048]{2,1,0:T(8,128)(2,1)} %bitcast.160, bf16[4,768,2048]{2,1,0:T(8,128)(2,1)} %collective-permute-done.4.twin), custom_call_target="tpu_custom_call" | custom-call | bytes 50331648 | tf_op jit(solution)/shard_map/unfold/pallas_call | solution.py:195
  229.5 16.6 %mlp.4 = (bf16[256,1024]{1,0:T(8,128)(2,1)}, f32[256,1024]{1,0:T(8,128)}, bf16[256,1024]{1,0:T(8,128)(2,1)}, bf16[256,4096]{1,0:T(8,128)(2,1)}, bf16[256,4096]{1,0:T(8,128)(2,1)}, /*index=5*/f32[256,1024]{1,0:T(8,128)}) custom-call(bf16[256,1024]{1,0:T(8,128)(2,1)} %get-tuple-element.251.x_ref, bf16[1024,1024]{1,0:T(8,128)(2,1)} %get-tuple-element.269.w_out, ...), custom_call_target="tpu_custom_call" | custom-call | flops 4831838208 | bytes 18874368 | tf_op jit(solution)/shard_map/mlp/pallas_call | solution.py:496
  246.1 7.4 qkv.6
  264.4 15.5 %mlp.5 = (bf16[256,1024]{1,0:T(8,128)(2,1)}, f32[256,1024]{1,0:T(8,128)}, bf16[256,1024]{1,0:T(8,128)(2,1)}, bf16[256,4096]{1,0:T(8,128)(2,1)}, bf16[256,4096]{1,0:T(8,128)(2,1)}, /*index=5*/f32[256,1024]{1,0:T(8,128)}) custom-call(bf16[256,1024]{1,0:T(8,128)(2,1)} %get-tuple-element.253.x_ref, bf16[1024,1024]{1,0:T(8,128)(2,1)} %get-tuple-element.269.w_out, ...), custom_call_target="tpu_custom_call" | custom-call | flops 4831838208 | bytes 18874368 | tf_op jit(solution)/shard_map/mlp/pallas_call | solution.py:496
  279.9 7.4 qkv.7
  287.2 9.7 all-to-all-done.6.pieces
  300.6 33.1 %recall_attend.2 = (bf16[2048,128]{1,0:T(8,128)(2,1)}, bf16[2560,128]{1,0:T(8,128)(2,1)}, bf16[2560,128]{1,0:T(8,128)(2,1)}, bf16[16,128,640]{2,1,0:T(8,128)(2,1...) custom-call(s32[20]{0:T(128)} %get-tuple-element.604.info, f32[33]{0:T(128)} %pad_maximum_fusion.3.rel, ...), custom_call_target="tpu_custom_call" | custom-call | flops 44999999488 | bytes 8000000 | tf_op jit(solution)/shard_map/recall_attend/pallas_call | solution.py:811
  345.0 33.3 %recall_attend.3 = (bf16[2048,128]{1,0:T(8,128)(2,1)}, bf16[2560,128]{1,0:T(8,128)(2,1)}, bf16[2560,128]{1,0:T(8,128)(2,1)}, bf16[16,128,640]{2,1,0:T(8,128)(2,1...) custom-call(s32[20]{0:T(128)} %get-tuple-element.605.info, f32[33]{0:T(128)} %pad_maximum_fusion.3.rel, ...), custom_call_target="tpu_custom_call" | custom-call | flops 44999999488 | bytes 8000000 | tf_op jit(solution)/shard_map/recall_attend/pallas_call | solution.py:811
  386.4 13.3 %unfold.5 = (bf16[1024,4096]{1,0:T(8,128)(2,1)}, bf16[4096,1024]{1,0:T(8,128)(2,1)}, bf16[1024,1024]{1,0:T(8,128)(2,1)}) custom-call(s32[1]{0:T(128)} %bitcast.1.key, bf16[4,576,2048]{2,1,0:T(8,128)(2,1)} %bitcast.162, bf16[4,576,2048]{2,1,0:T(8,128)(2,1)} %collective-permute-done.5.twin), custom_call_target="tpu_custom_call" | custom-call | bytes 37748736 | tf_op jit(solution)/shard_map/unfold/pallas_call | solution.py:195
  399.7 15.5 %mlp.6 = (bf16[256,1024]{1,0:T(8,128)(2,1)}, f32[256,1024]{1,0:T(8,128)}, bf16[256,1024]{1,0:T(8,128)(2,1)}, bf16[256,4096]{1,0:T(8,128)(2,1)}, bf16[256,4096]{1,0:T(8,128)(2,1)}, /*index=5*/bf16[256,1024]{1,0:T(8,128)(2,1)}) custom-call(f32[256,1024]{1,0:T(8,128)} %get-tuple-element.277.x_ref, bf16[1024,1024]{1,0:T(8,128)(2,1)} %get-tuple-element.297.w_out, ...), custom_call_target="tpu_custom_call" | custom-call | flops 4831838208 | bytes 18874368 | tf_op jit(solution)/shard_map/mlp/pallas_call | solution.py:496
  416.0 15.4 %mlp.7 = (bf16[256,1024]{1,0:T(8,128)(2,1)}, f32[256,1024]{1,0:T(8,128)}, bf16[256,1024]{1,0:T(8,128)(2,1)}, bf16[256,4096]{1,0:T(8,128)(2,1)}, bf16[256,4096]{1,0:T(8,128)(2,1)}, /*index=5*/bf16[256,1024]{1,0:T(8,128)(2,1)}) custom-call(f32[256,1024]{1,0:T(8,128)} %get-tuple-element.283.x_ref, bf16[1024,1024]{1,0:T(8,128)(2,1)} %get-tuple-element.297.w_out, ...), custom_call_target="tpu_custom_call" | custom-call | flops 4831838208 | bytes 18874368 | tf_op jit(solution)/shard_map/mlp/pallas_call | solution.py:496
  431.5 16.8 %mlp_back.4 = (bf16[256,4096]{1,0:T(8,128)(2,1)}, bf16[256,1024]{1,0:T(8,128)(2,1)}, f32[256,1024]{1,0:T(8,128)}, f32[1,1024]{1,0:T(1,128)}, f32[1,1024]{1,0:T(1,128)}, /*index=5*/bf16[8,256,128]{2,1,0:T(8,128)(2,1)}) custom-call(bf16[256,1024]{1,0:T(8,128)(2,1)} %get-tuple-element.308.g_ref.k0.s0, bf16[256,4096]{1,0:T(8,128)(2,1)} %get-tuple-element.309.up, ...), custom_call_target="tpu_custom_call" | custom-call | flops 4831838208 | bytes 18874368 | tf_op jit(solution)/shard_map/mlp_back/pallas_call | solution.py:567
  453.4 16.8 %mlp_back.5 = (bf16[256,4096]{1,0:T(8,128)(2,1)}, bf16[256,1024]{1,0:T(8,128)(2,1)}, f32[256,1024]{1,0:T(8,128)}, f32[1,1024]{1,0:T(1,128)}, f32[1,1024]{1,0:T(1,128)}, /*index=5*/bf16[8,256,128]{2,1,0:T(8,128)(2,1)}) custom-call(bf16[256,1024]{1,0:T(8,128)(2,1)} %get-tuple-element.315.g_ref.k1.s1, bf16[256,4096]{1,0:T(8,128)(2,1)} %get-tuple-element.316.up, ...), custom_call_target="tpu_custom_call" | custom-call | flops 4831838208 | bytes 18874368 | tf_op jit(solution)/shard_map/mlp_back/pallas_call | solution.py:567
  470.1 11.6 %weight_grad.9 = (bf16[4,512,2048]{2,1,0:T(8,128)(2,1)}, bf16[4,512,2048]{2,1,0:T(8,128)(2,1)}) custom-call(s32[5]{0:T(128)} %get-tuple-element.594.key, bf16[256,1024]{1,0:T(8,128)(2,1)} %get-tuple-element.319.a0, bf16[256,1024]{1,0:T(8,128)(2,1)} %get-tuple-element.320.a1, bf16[256,4096]{1,0:T(8,128)(2,1)} %get-tuple-element.321.k0.s0, ...), custom_call_target="tpu_custom_call" | custom-call | flops 4294967296 | bytes 16777216 | tf_op jit(solution)/shard_map/weight_grad/pallas_call | solution.py:373
  481.7 9.3 weight_grad.10
  496.6 32.1 %recall_back.2 = (f32[32,128]{1,0:T(8,128)}, f32[8,128]{1,0:T(8,128)}, bf16[8,256,384]{2,1,0:T(8,128)(2,1)}) custom-call(s32[20]{0:T(128)} %get-tuple-element.604.info, f32[33]{0:T(128)} %pad_maximum_fusion.3.rel, s32[128,640]{1,0:T(8,128)} %constant.64.clone.buckets, bf16[8,256,128]{2,1,0:T(8,128)(2,1)} %copy-done.30, ...), custom_call_target="tpu_custom_call" | custom-call | flops 49999998976 | bytes 8000000 | tf_op jit(solution)/shard_map/recall_back/pallas_call | solution.py:932
  528.6 10.5 add_convert_fusion
  545.0 32.7 %recall_back.3 = (f32[32,128]{1,0:T(8,128)}, f32[8,128]{1,0:T(8,128)}, bf16[8,256,384]{2,1,0:T(8,128)(2,1)}) custom-call(s32[20]{0:T(128)} %get-tuple-element.605.info, f32[33]{0:T(128)} %pad_maximum_fusion.3.rel, s32[128,640]{1,0:T(8,128)} %constant.64.clone.buckets, bf16[8,256,128]{2,1,0:T(8,128)(2,1)} %copy-done.32, ...), custom_call_target="tpu_custom_call" | custom-call | flops 49999998976 | bytes 8000000 | tf_op jit(solution)/shard_map/recall_back/pallas_call | solution.py:932
  592.3 9.1 qkv_back.4
  601.3 17.1 %mlp_back.6 = (bf16[256,4096]{1,0:T(8,128)(2,1)}, bf16[256,1024]{1,0:T(8,128)(2,1)}, f32[256,1024]{1,0:T(8,128)}, f32[1,1024]{1,0:T(1,128)}, f32[1,1024]{1,0:T(1,128)}, /*index=5*/bf16[8,256,128]{2,1,0:T(8,128)(2,1)}) custom-call(f32[256,1024]{1,0:T(8,128)} %get-tuple-element.360.g_ref, bf16[256,4096]{1,0:T(8,128)(2,1)} %get-tuple-element.361.up, ...), custom_call_target="tpu_custom_call" | custom-call | flops 4831838208 | bytes 18874368 | tf_op jit(solution)/shard_map/mlp_back/pallas_call | solution.py:567
  628.7 9.0 qkv_back.5
  637.7 16.9 %mlp_back.7 = (bf16[256,4096]{1,0:T(8,128)(2,1)}, bf16[256,1024]{1,0:T(8,128)(2,1)}, f32[256,1024]{1,0:T(8,128)}, f32[1,1024]{1,0:T(1,128)}, f32[1,1024]{1,0:T(1,128)}, /*index=5*/bf16[8,256,128]{2,1,0:T(8,128)(2,1)}) custom-call(f32[256,1024]{1,0:T(8,128)} %get-tuple-element.373.g_ref, bf16[256,4096]{1,0:T(8,128)(2,1)} %get-tuple-element.374.up, ...), custom_call_target="tpu_custom_call" | custom-call | flops 4831838208 | bytes 18874368 | tf_op jit(solution)/shard_map/mlp_back/pallas_call | solution.py:567
  659.9 13.2 %local_back.2 = (f32[32,128]{1,0:T(8,128)}, bf16[8,256,384]{2,1,0:T(8,128)(2,1)}) custom-call(s32[20]{0:T(128)} %get-tuple-element.604.info, f32[33]{0:T(128)} %pad_maximum_fusion.2.rel, s32[128,640]{1,0:T(8,128)} %constant.64.clone.buckets, bf16[8,256,128]{2,1,0:T(8,128)(2,1)} %copy-done.33, bf16[2048,128]{1,0:T(8,128)(2,1)} %get-tuple-element.378.refs_0_, ...), custom_call_target="tpu_custom_call" | custom-call | flops 20000000000 | bytes 8000000 | tf_op jit(solution)/shard_map/local_back/pallas_call | solution.py:932
  673.1 11.5 %weight_grad.12 = (bf16[4,256,2048]{2,1,0:T(8,128)(2,1)}, bf16[4,256,2048]{2,1,0:T(8,128)(2,1)}) custom-call(s32[5]{0:T(128)} %get-tuple-element.595.key, bf16[256,1024]{1,0:T(8,128)(2,1)} %get-tuple-element.386.a0, bf16[256,1024]{1,0:T(8,128)(2,1)} %get-tuple-element.387.a1, bf16[256,4096]{1,0:T(8,128)(2,1)} %get-tuple-element.388.k0.s0, ...), custom_call_target="tpu_custom_call" | custom-call | flops 4294967296 | bytes 16777216 | tf_op jit(solution)/shard_map/weight_grad/pallas_call | solution.py:373
  684.6 9.2 weight_grad.13
  699.7 13.2 %local_back.3 = (f32[32,128]{1,0:T(8,128)}, bf16[8,256,384]{2,1,0:T(8,128)(2,1)}) custom-call(s32[20]{0:T(128)} %get-tuple-element.605.info, f32[33]{0:T(128)} %pad_maximum_fusion.2.rel, s32[128,640]{1,0:T(8,128)} %constant.64.clone.buckets, bf16[8,256,128]{2,1,0:T(8,128)(2,1)} %copy-done.31, bf16[2048,128]{1,0:T(8,128)(2,1)} %get-tuple-element.403.refs_0_, ...), custom_call_target="tpu_custom_call" | custom-call | flops 20000000000 | bytes 8000000 | tf_op jit(solution)/shard_map/local_back/pallas_call | solution.py:932
  712.9 8.0 weight_grad.14
  722.5 29.7 %all-to-all-done.16.pieces = bf16[8,256,384]{2,1,0:T(8,128)(2,1)S(1)} async-done(((bf16[8,256,384]{2,1,0:T(8,128)(2,1)}), bf16[8,256,384]{2,1,0:T(8,128)(2,1)S(1)}, u32[]{:S(2)}, u32[]{:S(2)}) %all-to-all-start.16) | async-done | bytes 1572896 | tf_op jit(solution)/shard_map/all_to_all | solution.py:1078
  768.6 9.1 qkv_back.6
  777.7 6.5 add_convert_fusion.1
  784.2 22.6 %all-to-all-done.17.pieces = bf16[8,256,384]{2,1,0:T(8,128)(2,1)S(1)} async-done(((bf16[8,256,384]{2,1,0:T(8,128)(2,1)}), bf16[8,256,384]{2,1,0:T(8,128)(2,1)S(1)}, u32[]{:S(2)}, u32[]{:S(2)}) %all-to-all-start.17) | async-done | bytes 1572896 | tf_op jit(solution)/shard_map/all_to_all | solution.py:1078
  819.7 9.0 qkv_back.7
  858.3 8.3 collective-permute-done.16
  876.0 28.9 %collective-permute-done.38 = bf16[1,256,2048]{2,1,0:T(8,128)(2,1)S(1)} collective-permute-done((bf16[1,256,2048]{2,1,0:T(8,128)(2,1)}, bf16[1,256,2048]{2,1,0:T(8,128)(2,1)S(1)}, u32[]{:S(2)}, u32[]{:S(2)}) %collective-permute-start.38) | collective-permute-done | bytes 1048608 | tf_op jit(solution)/shard_map/ppermute | solution.py:311
  908.8 10.0 collective-permute-done.24
  926.4 6.7 collective-permute-done.25
  937.3 10.3 collective-permute-done.21
  966.6 29.3 %collective-permute-done.29 = bf16[128,2048]{1,0:T(8,128)(2,1)S(1)} collective-permute-done((bf16[128,2048]{1,0:T(8,128)(2,1)S(1)}, bf16[128,2048]{1,0:T(8,128)(2,1)S(1)}, u32[]{:S(2)}, u32[]{:S(2)}) %collective-permute-start.29) | collective-permute-done | bytes 524320 | tf_op jit(solution)/shard_map/ppermute | solution.py:311
  1016.6 26.8 %collective-permute-done.41 = bf16[256,2048]{1,0:T(8,128)(2,1)S(1)} collective-permute-done((bf16[256,2048]{1,0:T(8,128)(2,1)S(1)}, bf16[256,2048]{1,0:T(8,128)(2,1)S(1)}, u32[]{:S(2)}, u32[]{:S(2)}) %collective-permute-start.41) | collective-permute-done | bytes 1048608 | tf_op jit(solution)/shard_map/ppermute | solution.py:311
  1049.8 32.8 %collective-permute-done.46 = bf16[256,2048]{1,0:T(8,128)(2,1)S(1)} collective-permute-done((bf16[256,2048]{1,0:T(8,128)(2,1)S(1)}, bf16[256,2048]{1,0:T(8,128)(2,1)S(1)}, u32[]{:S(2)}, u32[]{:S(2)}) %collective-permute-start.46) | collective-permute-done | bytes 1048608 | tf_op jit(solution)/shard_map/ppermute | solution.py:311
  (429 shorter events, 306.9 us)
Async XLA Ops:
  7.2 64.0 %all-gather.7.cloned.1.call-start = ((), (), s32[]{:S(2)}) async-start(), calls=%async_computation.21 | async-start | bytes 3932160 | tf_op jit(solution)/shard_map/all_gather | solution.py:1052
  9.3 173.1 %all-gather.9.cloned.1.call-start = ((), (), s32[]{:S(2)}) async-start(), calls=%async_computation.22 | async-start | bytes 15728640 | tf_op jit(solution)/shard_map/all_gather | solution.py:1052
  19.8 33.0 %all-to-all-start = ((bf16[8,256,256]{2,1,0:T(8,128)(2,1)}), bf16[8,256,256]{2,1,0:T(8,128)(2,1)}, u32[]{:S(2)}, u32[]{:S(2)}) async-start(bf16[8,256,256]{2,1,0:T(8,128)(2,1)} %fusion.12), calls=%async_computation | async-start | bytes 2097152 | tf_op jit(solution)/shard_map/all_to_all | solution.py:1078
  97.4 41.3 %all-to-all-start.2 = ((bf16[8,256,384]{2,1,0:T(8,128)(2,1)}), bf16[8,256,384]{2,1,0:T(8,128)(2,1)S(1)}, u32[]{:S(2)}, u32[]{:S(2)}) async-start(bf16[8,256,384]{2,1,0:T(8,128)(2,1)} %bitcast.171), calls=%async_computation.2 | async-start | bytes 3145728 | tf_op jit(solution)/shard_map/all_to_all | solution.py:1078
  139.9 41.3 %all-to-all-start.3 = ((bf16[8,256,384]{2,1,0:T(8,128)(2,1)}), bf16[8,256,384]{2,1,0:T(8,128)(2,1)S(1)}, u32[]{:S(2)}, u32[]{:S(2)}) async-start(bf16[8,256,384]{2,1,0:T(8,128)(2,1)} %bitcast.168), calls=%async_computation.3 | async-start | bytes 3145728 | tf_op jit(solution)/shard_map/all_to_all | solution.py:1078
  143.5 194.8 %all-gather.11.cloned.1.call-start = ((), (), s32[]{:S(2)}) async-start(), calls=%async_computation.23 | async-start | bytes 11796480 | tf_op jit(solution)/shard_map/all_gather | solution.py:1052
  182.4 29.1 %collective-permute-start.4 = (bf16[4,768,2048]{2,1,0:T(8,128)(2,1)}, bf16[4,768,2048]{2,1,0:T(8,128)(2,1)}, u32[]{:S(2)}, u32[]{:S(2)}) collective-permute-start(bf16[4,768,2048]{2,1,0:T(8,128)(2,1)} %bitcast.159), channel_id=1, source_target_pairs={{0,4},{4,0},{8,12},{12,8},{16,20},{20,16},{24,28},{28,24},{1,5},{5... | collective-permute-start | bytes 37748744 | tf_op jit(solution)/shard_map/ppermute | solution.py:109
  205.5 48.0 %all-to-all-start.5 = ((bf16[8,256,128]{2,1,0:T(8,128)(2,1)}), bf16[8,256,128]{2,1,0:T(8,128)(2,1)S(1)}, u32[]{:S(2)}, u32[]{:S(2)}) async-start(bf16[8,256,128]{2,1,0:T(8,128)(2,1)} %get-tuple-element.275), calls=%async_computation.5 | async-start | bytes 1048576 | tf_op jit(solution)/shard_map/all_to_all | solution.py:1078
  253.5 43.4 %all-to-all-start.6 = ((bf16[8,256,384]{2,1,0:T(8,128)(2,1)}), bf16[8,256,384]{2,1,0:T(8,128)(2,1)S(1)}, u32[]{:S(2)}, u32[]{:S(2)}) async-start(bf16[8,256,384]{2,1,0:T(8,128)(2,1)} %bitcast.169), calls=%async_computation.6 | async-start | bytes 3145728 | tf_op jit(solution)/shard_map/all_to_all | solution.py:1078
  297.0 41.3 %all-to-all-start.7 = ((bf16[8,256,384]{2,1,0:T(8,128)(2,1)}), bf16[8,256,384]{2,1,0:T(8,128)(2,1)S(1)}, u32[]{:S(2)}, u32[]{:S(2)}) async-start(bf16[8,256,384]{2,1,0:T(8,128)(2,1)} %bitcast.170), calls=%async_computation.7 | async-start | bytes 3145728 | tf_op jit(solution)/shard_map/all_to_all | solution.py:1078
  338.3 48.1 %collective-permute-start.5 = (bf16[4,576,2048]{2,1,0:T(8,128)(2,1)}, bf16[4,576,2048]{2,1,0:T(8,128)(2,1)}, u32[]{:S(2)}, u32[]{:S(2)}) collective-permute-start(bf16[4,576,2048]{2,1,0:T(8,128)(2,1)} %bitcast.161), channel_id=1, source_target_pairs={{0,4},{4,0},{8,12},{12,8},{16,20},{20,16},{24,28},{28,24},{1,5},{5... | collective-permute-start | bytes 28311560 | tf_op jit(solution)/shard_map/ppermute | solution.py:109
  341.4 36.8 %all-to-all-start.8 = ((bf16[8,256,128]{2,1,0:T(8,128)(2,1)}), bf16[8,256,128]{2,1,0:T(8,128)(2,1)S(1)}, u32[]{:S(2)}, u32[]{:S(2)}) async-start(bf16[8,256,128]{2,1,0:T(8,128)(2,1)} %get-tuple-element.300), calls=%async_computation.8 | async-start | bytes 1048576 | tf_op jit(solution)/shard_map/all_to_all | solution.py:1078
  378.3 36.9 %all-to-all-start.9 = ((bf16[8,256,128]{2,1,0:T(8,128)(2,1)}), bf16[8,256,128]{2,1,0:T(8,128)(2,1)S(1)}, u32[]{:S(2)}, u32[]{:S(2)}) async-start(bf16[8,256,128]{2,1,0:T(8,128)(2,1)} %get-tuple-element.303), calls=%async_computation.9 | async-start | bytes 1048576 | tf_op jit(solution)/shard_map/all_to_all | solution.py:1078
  448.3 42.7 %all-to-all-start.10 = ((bf16[8,256,128]{2,1,0:T(8,128)(2,1)}), bf16[8,256,128]{2,1,0:T(8,128)(2,1)S(1)}, u32[]{:S(2)}, u32[]{:S(2)}) async-start(bf16[8,256,128]{2,1,0:T(8,128)(2,1)} %get-tuple-element.313), calls=%async_computation.10 | async-start | bytes 1048576 | tf_op jit(solution)/shard_map/all_to_all | solution.py:1078
  491.0 37.7 %collective-permute-start.6 = (bf16[4,512,2048]{2,1,0:T(8,128)(2,1)}, bf16[4,512,2048]{2,1,0:T(8,128)(2,1)}, u32[]{:S(2)}, u32[]{:S(2)}) collective-permute-start(bf16[4,512,2048]{2,1,0:T(8,128)(2,1)} %get-tuple-element.340), channel_id=1, source_target_pairs={{0,4},{4,0},{8,12},{12,8},{16,20},{20,16},{24,28},{28,24},{1,5},{5... | collective-permute-start | bytes 25165832 | tf_op jit(solution)/shard_map/ppermute | solution.py:109
  491.6 47.6 %all-to-all-start.11 = ((bf16[8,256,128]{2,1,0:T(8,128)(2,1)}), bf16[8,256,128]{2,1,0:T(8,128)(2,1)S(1)}, u32[]{:S(2)}, u32[]{:S(2)}) async-start(bf16[8,256,128]{2,1,0:T(8,128)(2,1)} %get-tuple-element.337), calls=%async_computation.11 | async-start | bytes 1048576 | tf_op jit(solution)/shard_map/all_to_all | solution.py:1078
  496.3 132.3 %reduce-scatter.7.cloned.1.call-start = ((), (), s32[]{:S(2)}) async-start(), calls=%async_computation.24 | async-start | bytes 10485760
  539.9 42.9 %all-to-all-start.12 = ((bf16[8,256,384]{2,1,0:T(8,128)(2,1)}), bf16[8,256,384]{2,1,0:T(8,128)(2,1)S(1)}, u32[]{:S(2)}, u32[]{:S(2)}) async-start(bf16[8,256,384]{2,1,0:T(8,128)(2,1)} %get-tuple-element.338), calls=%async_computation.12 | async-start | bytes 3145728 | tf_op jit(solution)/shard_map/all_to_all | solution.py:1078
  582.8 41.7 %all-to-all-start.13 = ((bf16[8,256,384]{2,1,0:T(8,128)(2,1)}), bf16[8,256,384]{2,1,0:T(8,128)(2,1)S(1)}, u32[]{:S(2)}, u32[]{:S(2)}) async-start(bf16[8,256,384]{2,1,0:T(8,128)(2,1)} %get-tuple-element.365), calls=%async_computation.13 | async-start | bytes 3145728 | tf_op jit(solution)/shard_map/all_to_all | solution.py:1078
  624.6 30.0 %all-to-all-start.14 = ((bf16[8,256,128]{2,1,0:T(8,128)(2,1)}), bf16[8,256,128]{2,1,0:T(8,128)(2,1)S(1)}, u32[]{:S(2)}, u32[]{:S(2)}) async-start(bf16[8,256,128]{2,1,0:T(8,128)(2,1)} %get-tuple-element.366), calls=%async_computation.14 | async-start | bytes 1048576 | tf_op jit(solution)/shard_map/all_to_all | solution.py:1078
  654.6 39.2 %all-to-all-start.15 = ((bf16[8,256,128]{2,1,0:T(8,128)(2,1)}), bf16[8,256,128]{2,1,0:T(8,128)(2,1)S(1)}, u32[]{:S(2)}, u32[]{:S(2)}) async-start(bf16[8,256,128]{2,1,0:T(8,128)(2,1)} %get-tuple-element.383), calls=%async_computation.15 | async-start | bytes 1048576 | tf_op jit(solution)/shard_map/all_to_all | solution.py:1078
  693.8 62.2 %collective-permute-start.7 = (bf16[4,256,2048]{2,1,0:T(8,128)(2,1)}, bf16[4,256,2048]{2,1,0:T(8,128)(2,1)}, u32[]{:S(2)}, u32[]{:S(2)}) collective-permute-start(bf16[4,256,2048]{2,1,0:T(8,128)(2,1)} %get-tuple-element.396), channel_id=1, source_target_pairs={{0,4},{4,0},{8,12},{12,8},{16,20},{20,16},{24,28},{28,24},{1,5},{5... | collective-permute-start | bytes 12582920 | tf_op jit(solution)/shard_map/ppermute | solution.py:311
  694.4 57.8 %all-to-all-start.16 = ((bf16[8,256,384]{2,1,0:T(8,128)(2,1)}), bf16[8,256,384]{2,1,0:T(8,128)(2,1)S(1)}, u32[]{:S(2)}, u32[]{:S(2)}) async-start(bf16[8,256,384]{2,1,0:T(8,128)(2,1)} %get-tuple-element.384), calls=%async_computation.16 | async-start | bytes 3145728 | tf_op jit(solution)/shard_map/all_to_all | solution.py:1078
  699.2 159.1 %all-reduce.6.cloned.1.call-start = ((), (), s32[]{:S(2)}) async-start(), calls=%async_computation.20 | async-start | bytes 4194304 | tf_op jit(solution)/shard_map/psum | solution.py:1209
  699.2 61.6 %collective-permute-start.8 = (bf16[4,256,2048]{2,1,0:T(8,128)(2,1)}, bf16[4,256,2048]{2,1,0:T(8,128)(2,1)}, u32[]{:S(2)}, u32[]{:S(2)}) collective-permute-start(bf16[4,256,2048]{2,1,0:T(8,128)(2,1)} %get-tuple-element.398), channel_id=1, source_target_pairs={{0,4},{4,0},{8,12},{12,8},{16,20},{20,16},{24,28},{28,24},{1,5},{5... | collective-permute-start | bytes 12582920 | tf_op jit(solution)/shard_map/ppermute | solution.py:311
  720.9 56.8 %collective-permute-start.9 = (bf16[4,256,2048]{2,1,0:T(8,128)(2,1)}, bf16[4,256,2048]{2,1,0:T(8,128)(2,1)}, u32[]{:S(2)}, u32[]{:S(2)}) collective-permute-start(bf16[4,256,2048]{2,1,0:T(8,128)(2,1)} %get-tuple-element.411), channel_id=1, source_target_pairs={{0,4},{4,0},{8,12},{12,8},{16,20},{20,16},{24,28},{28,24},{1,5},{5... | collective-permute-start | bytes 12582920 | tf_op jit(solution)/shard_map/ppermute | solution.py:109
  752.2 54.6 %all-to-all-start.17 = ((bf16[8,256,384]{2,1,0:T(8,128)(2,1)}), bf16[8,256,384]{2,1,0:T(8,128)(2,1)S(1)}, u32[]{:S(2)}, u32[]{:S(2)}) async-start(bf16[8,256,384]{2,1,0:T(8,128)(2,1)} %get-tuple-element.415), calls=%async_computation.17 | async-start | bytes 3145728 | tf_op jit(solution)/shard_map/all_to_all | solution.py:1078
  755.8 203.2 %reduce-scatter.9.cloned.1.call-start = ((), (), s32[]{:S(2)}) async-start(), calls=%async_computation.25 | async-start | bytes 5242880
  764.5 48.2 %collective-permute-start.10 = (bf16[2,256,2048]{2,1,0:T(8,128)(2,1)}, bf16[2,256,2048]{2,1,0:T(8,128)(2,1)}, u32[]{:S(2)}, u32[]{:S(2)}) collective-permute-start(bf16[2,256,2048]{2,1,0:T(8,128)(2,1)} %add_convert_fusion.3), channel_id=1, source_target_pairs={{0,1},{1,0},{2,3},{3,2},{4,5},{5,4},{6,7},{7,6},{8,9},{9,8},{10,11... | collective-permute-start | bytes 6291464 | tf_op jit(solution)/shard_map/ppermute | solution.py:311
  768.0 48.2 %collective-permute-start.11 = (bf16[2,256,2048]{2,1,0:T(8,128)(2,1)}, bf16[2,256,2048]{2,1,0:T(8,128)(2,1)}, u32[]{:S(2)}, u32[]{:S(2)}) collective-permute-start(bf16[2,256,2048]{2,1,0:T(8,128)(2,1)} %add_convert_fusion.2), channel_id=1, source_target_pairs={{0,2},{1,3},{2,0},{3,1},{4,6},{5,7},{6,4},{7,5},{8,10},{9,11},{10,... | collective-permute-start | bytes 6291464 | tf_op jit(solution)/shard_map/ppermute | solution.py:311
  831.4 36.1 %collective-permute-start.34 = (bf16[1,256,2048]{2,1,0:T(8,128)(2,1)}, bf16[1,256,2048]{2,1,0:T(8,128)(2,1)}, u32[]{:S(2)}, u32[]{:S(2)}) collective-permute-start(bf16[1,256,2048]{2,1,0:T(8,128)(2,1)} %add_convert_fusion.13), channel_id=1, source_target_pairs={{0,2},{1,3},{2,0},{3,1},{4,6},{5,7},{6,4},{7,5},{8,10},{9,11},{10,... | collective-permute-start | bytes 3145736 | tf_op jit(solution)/shard_map/ppermute | solution.py:311
  839.6 84.7 %collective-permute-start.17 = (bf16[4,256,768]{2,1,0:T(8,128)(2,1)}, bf16[4,256,768]{2,1,0:T(8,128)(2,1)S(1)}, u32[]{:S(2)}, u32[]{:S(2)}) collective-permute-start(bf16[4,256,768]{2,1,0:T(8,128)(2,1)} %get-tuple-element.451), channel_id=1, source_target_pairs={{0,4},{4,0},{8,12},{12,8},{16,20},{20,16},{24,28},{28,24},{1,5},{5... | collective-permute-start | bytes 4718600 | tf_op jit(solution)/shard_map/ppermute | solution.py:311
  848.1 75.7 %collective-permute-start.20 = (bf16[4,256,768]{2,1,0:T(8,128)(2,1)}, bf16[4,256,768]{2,1,0:T(8,128)(2,1)S(1)}, u32[]{:S(2)}, u32[]{:S(2)}) collective-permute-start(bf16[4,256,768]{2,1,0:T(8,128)(2,1)} %get-tuple-element.454), channel_id=1, source_target_pairs={{0,4},{4,0},{8,12},{12,8},{16,20},{20,16},{24,28},{28,24},{1,5},{5... | collective-permute-start | bytes 4718600 | tf_op jit(solution)/shard_map/ppermute | solution.py:311
  866.5 38.3 %collective-permute-start.38 = (bf16[1,256,2048]{2,1,0:T(8,128)(2,1)}, bf16[1,256,2048]{2,1,0:T(8,128)(2,1)S(1)}, u32[]{:S(2)}, u32[]{:S(2)}) collective-permute-start(bf16[1,256,2048]{2,1,0:T(8,128)(2,1)} %add_convert_fusion.12), channel_id=1, source_target_pairs={{0,1},{1,0},{2,3},{3,2},{4,5},{5,4},{6,7},{7,6},{8,9},{9,8},{10,11... | collective-permute-start | bytes 3145736 | tf_op jit(solution)/shard_map/ppermute | solution.py:311
  867.6 216.6 %collective-permute-start.48 = (bf16[512,2048]{1,0:T(8,128)(2,1)}, bf16[512,2048]{1,0:T(8,128)(2,1)}, u32[]{:S(2)}, u32[]{:S(2)}) collective-permute-start(bf16[512,2048]{1,0:T(8,128)(2,1)} %all-reduce.6.cloned.1.call-done.refs_0_), channel_id=1, source_target_pairs={{0,4},{4,0},{8,12},{12,8},{16,20},{20,16},{24,28},{28,24},{1,5},{5... | collective-permute-start | bytes 6291464 | tf_op jit(solution)/shard_map/ppermute | solution.py:109
  870.7 64.6 %collective-permute-start.35 = (bf16[256,2048]{1,0:T(8,128)(2,1)S(1)}, bf16[256,2048]{1,0:T(8,128)(2,1)S(1)}, u32[]{:S(2)}, u32[]{:S(2)}) collective-permute-start(bf16[256,2048]{1,0:T(8,128)(2,1)S(1)} %fusion), channel_id=1, source_target_pairs={{0,8},{4,12},{24,16},{28,20},{1,9},{5,13},{25,17},{29,21},{2,10},{... | collective-permute-start | bytes 3145736 | tf_op jit(solution)/shard_map/ppermute | solution.py:311
  918.9 30.5 %collective-permute-start.39 = (bf16[256,2048]{1,0:T(8,128)(2,1)S(1)}, bf16[256,2048]{1,0:T(8,128)(2,1)S(1)}, u32[]{:S(2)}, u32[]{:S(2)}) collective-permute-start(bf16[256,2048]{1,0:T(8,128)(2,1)S(1)} %fusion.1), channel_id=1, source_target_pairs={{0,8},{4,12},{24,16},{28,20},{1,9},{5,13},{25,17},{29,21},{2,10},{... | collective-permute-start | bytes 3145736 | tf_op jit(solution)/shard_map/ppermute | solution.py:311
  935.6 26.8 %collective-permute-start.36 = (bf16[256,2048]{1,0:T(8,128)(2,1)S(1)}, bf16[256,2048]{1,0:T(8,128)(2,1)}, u32[]{:S(2)}, u32[]{:S(2)}) collective-permute-start(bf16[256,2048]{1,0:T(8,128)(2,1)S(1)} %add_convert_fusion.10), channel_id=1, source_target_pairs={{8,16},{12,20},{16,8},{20,12},{9,17},{13,21},{17,9},{21,13},{10,18... | collective-permute-start | bytes 3145736 | tf_op jit(solution)/shard_map/ppermute | solution.py:311
  949.8 55.6 %collective-permute-start.40 = (bf16[256,2048]{1,0:T(8,128)(2,1)S(1)}, bf16[256,2048]{1,0:T(8,128)(2,1)}, u32[]{:S(2)}, u32[]{:S(2)}) collective-permute-start(bf16[256,2048]{1,0:T(8,128)(2,1)S(1)} %add_convert_fusion.7), channel_id=1, source_target_pairs={{8,16},{12,20},{16,8},{20,12},{9,17},{13,21},{17,9},{21,13},{10,18... | collective-permute-start | bytes 3145736 | tf_op jit(solution)/shard_map/ppermute | solution.py:311
  959.0 45.3 %collective-permute-start.44 = (bf16[256,2048]{1,0:T(8,128)(2,1)}, bf16[256,2048]{1,0:T(8,128)(2,1)S(1)}, u32[]{:S(2)}, u32[]{:S(2)}) collective-permute-start(bf16[256,2048]{1,0:T(8,128)(2,1)} %bitcast.172), channel_id=1, source_target_pairs={{0,8},{4,12},{24,16},{28,20},{1,9},{5,13},{25,17},{29,21},{2,10},{... | collective-permute-start | bytes 3145736 | tf_op jit(solution)/shard_map/ppermute | solution.py:311
  961.1 34.9 %collective-permute-start.29 = (bf16[128,2048]{1,0:T(8,128)(2,1)S(1)}, bf16[128,2048]{1,0:T(8,128)(2,1)S(1)}, u32[]{:S(2)}, u32[]{:S(2)}) collective-permute-start(bf16[128,2048]{1,0:T(8,128)(2,1)S(1)} %get-tuple-element.542), channel_id=1, source_target_pairs={{0,8},{4,12},{24,16},{28,20},{1,9},{5,13},{25,17},{29,21},{2,10},{... | collective-permute-start | bytes 1572872 | tf_op jit(solution)/shard_map/ppermute | solution.py:311
  962.4 40.8 %collective-permute-start.26 = (bf16[128,2048]{1,0:T(8,128)(2,1)S(1)}, bf16[128,2048]{1,0:T(8,128)(2,1)S(1)}, u32[]{:S(2)}, u32[]{:S(2)}) collective-permute-start(bf16[128,2048]{1,0:T(8,128)(2,1)S(1)} %get-tuple-element.543), channel_id=1, source_target_pairs={{0,8},{4,12},{24,16},{28,20},{1,9},{5,13},{25,17},{29,21},{2,10},{... | collective-permute-start | bytes 1572872 | tf_op jit(solution)/shard_map/ppermute | solution.py:311
  1007.8 35.5 %collective-permute-start.41 = (bf16[256,2048]{1,0:T(8,128)(2,1)S(1)}, bf16[256,2048]{1,0:T(8,128)(2,1)S(1)}, u32[]{:S(2)}, u32[]{:S(2)}) collective-permute-start(bf16[256,2048]{1,0:T(8,128)(2,1)S(1)} %add_convert_fusion.6), channel_id=1, source_target_pairs={{8,0},{12,4},{16,24},{20,28},{9,1},{13,5},{17,25},{21,29},{10,2},{... | collective-permute-start | bytes 3145736 | tf_op jit(solution)/shard_map/ppermute | solution.py:311
  1009.2 39.7 %collective-permute-start.31 = (bf16[128,2048]{1,0:T(8,128)(2,1)S(1)}, bf16[128,2048]{1,0:T(8,128)(2,1)S(1)}, u32[]{:S(2)}, u32[]{:S(2)}) collective-permute-start(bf16[128,2048]{1,0:T(8,128)(2,1)S(1)} %add_convert_fusion.16), channel_id=1, source_target_pairs={{8,0},{12,4},{16,24},{20,28},{9,1},{13,5},{17,25},{21,29},{10,2},{... | collective-permute-start | bytes 1572872 | tf_op jit(solution)/shard_map/ppermute | solution.py:311
  1010.7 72.1 %collective-permute-start.28 = (bf16[128,2048]{1,0:T(8,128)(2,1)S(1)}, bf16[128,2048]{1,0:T(8,128)(2,1)S(1)}, u32[]{:S(2)}, u32[]{:S(2)}) collective-permute-start(bf16[128,2048]{1,0:T(8,128)(2,1)S(1)} %add_convert_fusion.18), channel_id=1, source_target_pairs={{8,0},{12,4},{16,24},{20,28},{9,1},{13,5},{17,25},{21,29},{10,2},{... | collective-permute-start | bytes 1572872 | tf_op jit(solution)/shard_map/ppermute | solution.py:311
  1015.1 67.5 %collective-permute-start.46 = (bf16[256,2048]{1,0:T(8,128)(2,1)S(1)}, bf16[256,2048]{1,0:T(8,128)(2,1)S(1)}, u32[]{:S(2)}, u32[]{:S(2)}) collective-permute-start(bf16[256,2048]{1,0:T(8,128)(2,1)S(1)} %add_convert_fusion.4), channel_id=1, source_target_pairs={{8,0},{12,4},{16,24},{20,28},{9,1},{13,5},{17,25},{21,29},{10,2},{... | collective-permute-start | bytes 3145736 | tf_op jit(solution)/shard_map/ppermute | solution.py:311
  1043.3 53.4 %collective-permute-start.42 = (bf16[256,2048]{1,0:T(8,128)(2,1)S(1)}, bf16[256,2048]{1,0:T(8,128)(2,1)}, u32[]{:S(2)}, u32[]{:S(2)}) collective-permute-start(bf16[256,2048]{1,0:T(8,128)(2,1)S(1)} %broadcast_select_fusion.2.refs_0_), channel_id=1, source_target_pairs={{0,4},{4,0},{8,12},{12,8},{16,20},{20,16},{24,28},{28,24},{1,5},{5... | collective-permute-start | bytes 3145736 | tf_op jit(solution)/shard_map/ppermute | solution.py:311
  1048.9 47.8 %collective-permute-start.43 = (bf16[256,2048]{1,0:T(8,128)(2,1)S(1)}, bf16[256,2048]{1,0:T(8,128)(2,1)}, u32[]{:S(2)}, u32[]{:S(2)}) collective-permute-start(bf16[256,2048]{1,0:T(8,128)(2,1)S(1)} %broadcast_select_fusion.1.refs_1_), channel_id=1, source_target_pairs={{0,4},{4,0},{8,12},{12,8},{16,20},{20,16},{24,28},{28,24},{1,5},{5... | collective-permute-start | bytes 3145736 | tf_op jit(solution)/shard_map/ppermute | solution.py:311
  (98 other events, 1484.2 us)
Sparse Core Ops, SparseCore 0:
  10.4 46.6 all-gather.6
  59.6 122.7 all-gather.8
  185.6 96.4 all-gather.10
  539.3 87.2 reduce-scatter.6
  722.6 116.8 all-reduce.5
  842.9 68.1 reduce-scatter.8

commit v3 on v2

--- a/solution.py
+++ b/solution.py
@@ -265,7 +265,7 @@
     return [[g for g in range(lax.axis_size("ctx")) if g % 2 == c] for c in range(2)]
 
 
-def line_steps(mine):
+def line_steps(mine, after=None, leave=None):
     ctx_count = lax.axis_size("ctx")
     z = (lax.axis_index("ctx") >> 1) & (LINE - 1)
     stride = 2 * LINE
@@ -278,7 +278,13 @@
             for c in range(2)
         ]
 
-    inner = add_terms([mine, (yield "ctx", along([(0, 1), (3, 2)]), mine)])
+    if after is not None:
+        yield None, None, mine
+        mine, _ = lax.optimization_barrier((mine, after[0]))
+    got = yield "ctx", along([(0, 1), (3, 2)]), mine
+    if leave is not None:
+        leave.append(got)
+    inner = add_terms([mine, got])
     both = add_terms([inner, (yield "ctx", along([(1, 2), (2, 1)]), inner)])
     outer = yield "ctx", along([(1, 0), (2, 3)]), both
     full = jnp.where((z == 0) | (z == LINE - 1), outer, both)
@@ -289,8 +295,8 @@
     return full, (yield "ctx", xor_perm(ctx_count, 1), full)
 
 
-def all_steps(keep, send, bits):
-    return (yield from line_steps((yield from reduce_steps(keep, send, bits))))
+def all_steps(keep, send, bits, after, leave):
+    return (yield from line_steps((yield from reduce_steps(keep, send, bits)), after, leave))
 
 
 class Lane:
@@ -307,8 +313,9 @@
             value, operands = lax.optimization_barrier((value, operands))
         left = []
         for (key, steps, (axis, pairs, _)), operand in zip(self.active, operands):
+            got = None if axis is None else lax.ppermute(operand, axis, pairs)
             try:
-                left.append((key, steps, steps.send(lax.ppermute(operand, axis, pairs))))
+                left.append((key, steps, steps.send(got)))
             except StopIteration as stop:
                 self.done[key] = stop.value
         self.active = left
@@ -409,7 +416,7 @@
     return out, grad_gain, grad_bias
 
 
-GROUP = 4
+GROUP = 8
 
 
 def qkv_kernel(x_ref, gain, bias, weight, normed, pieces):
@@ -490,7 +497,7 @@
 def mlp_forward(x, pieces, w_out, gain, bias, w_in, w_down, kind):
     width = x.shape[1]
     ff = w_in.shape[1]
-    tile = 512
+    tile = 1024
     steps = ff // tile
     row = (ROWS, width)
     return pl.pallas_call(
@@ -561,7 +568,7 @@
     count = lax.axis_size("ctx")
     width = hidden.shape[1]
     ff = w_in.shape[1]
-    tile = 512
+    tile = 1024
     steps = ff // tile
     row = (ROWS, width)
     return pl.pallas_call(
@@ -1210,13 +1217,14 @@
         input_back(1, m, outs)
         dense_back(0, m, back[1][m]["dx"])
     heads_back(0, 0, back[0][0]["pieces"])
-    for key, bits, left, right, tile in (
-        ("in0", ups, pair(kept[0], "n2"), pair(back[0], "du"), width),
-        ("down0", downs, pair(kept[0], "act"), pair(back[1], "dx_low"), half),
+    first_in, first_a = [], []
+    for key, bits, left, right, tile, after, leave in (
+        ("in0", ups, pair(kept[0], "n2"), pair(back[0], "du"), width, None, first_in),
+        ("down0", downs, pair(kept[0], "act"), pair(back[1], "dx_low"), half, first_in, None),
     ):
         tiles = right[0].shape[1] // 2 // tile
         both_0 = grad_pair(left, right, shard, tile, 0, tiles, bits=bits)
-        lane.add(key, all_steps(*both_0, bits))
+        lane.add(key, all_steps(*both_0, bits, after, leave))
     heads_back(0, 1, lane.advance(back[0][1]["pieces"]))
     keep_a, send_a = grad_pair(
         pair(kept[1], "n1"), pair(back[1], "dqkv"), shard, half_qkv, 0, 1, into=both, dims=dims_a
@@ -1245,11 +1253,6 @@
             value = sum(jnp.sum(item["extra"][1]) for item in items) * (gate * (1.0 - gate))[0]
             parts.append((spot * value).reshape(fsdp, -1))
         smalls[n] = parts
-    lane.drain()
-    last = jnp.concatenate([lane.done[key] for key in ("low", "high", "out")], 1)
-    for n in range(2):
-        lane.add("a0%d" % n, line_steps(last[n * (shard // 2) : (n + 1) * (shard // 2)]))
-    lane.drain()
     dims = [(shard, 3 * width), (shard, width), (shard, wide), (chunks * shard, width)]
 
     def joined(parts, plan, sizes):
@@ -1264,7 +1267,15 @@
         return [(1, i * shard, shard, half, n, row, i * half, 0, half) for i in range(chunks)]
 
     grads = [{}, {}]
-    grads[1][7], grads[1][8] = joined([done["b1"]], [move_in] + move_down(0, shard), dims[2:])
+    while not all(key in lane.done for key in ("low", "high", "out")):
+        lane.advance()
+    merged = joined([lane.done["b1"]], [move_in] + move_down(0, shard), dims[2:])
+    last = jnp.concatenate([lane.done[key] for key in ("low", "high", "out")], 1)
+    last, merged = tie((last, merged))
+    grads[1][7], grads[1][8] = merged
+    lane.add("a00", line_steps(last[: shard // 2], None, first_a))
+    lane.add("a01", line_steps(last[shard // 2 :], first_a, None))
+    lane.drain()
     parts = [done["in0"], done["down0"]]
     grads[0][7], grads[0][8] = joined(parts, [move_in] + move_down(1, 0), dims[2:])
     grads[1][2], grads[1][4] = joined([done["a1"]], [move_qkv, move_out], dims[:2])

time: 1130 us -> 1110 us (0.982)
  Pallas kernels: 515 us -> 493 us
    convert_element_type x21 -> x22, other arithmetic: 40.6 us -> 46.1 us  [add_terms(): return total.astype(BF16)]
  transfers between devices with their start and end apart: 72 -> 72, of which waited for: 26 -> 27; matrix products, arithmetic and copies ran while one was open for 8% -> 9% of each run, Pallas kernels for 43% -> 42%
where the time goes in v3:
time: 1110 us; the launch traced here: 1100 us
  Pallas kernels  493 us (44%)
  waiting for transfers between devices  337 us (30%)
  starting transfers between devices  128 us (12%)
  other arithmetic  76.2 us (7%)
  local copies, waits for them, and re-layouts  30.2 us (3%)
  between operations  18.8 us (2%)
  blocking collectives  18.4 us (2%)
    all_to_all x17, waiting for transfers between devices, exchange(): return links.ran(lax.all_to_all(links.next(x), 'ctx', 0, 0, tiled=False))  165 us
    ppermute x35, waiting for transfers between devices, advance(): got = None if axis is None else lax.ppermute(operand, axis, pairs)  160 us
    pallas_call x4, Pallas kernels, attend_back(): pl.pallas_call(functools.partial(attend_back_kernel, recall, count), grid...  91.3 us
    pallas_call x4, Pallas kernels, attend(): pl.pallas_call(functools.partial(attend_kernel, recall, count), grid=(1,)...  90.6 us
    all_to_all x17, starting transfers between devices, exchange(): return links.ran(lax.all_to_all(links.next(x), 'ctx', 0, 0, tiled=False))  76 us
    pallas_call x9, Pallas kernels, weight_grad(): pl.pallas_call(grad_kernel, grid_spec=pltpu.PrefetchScalarGridSpec(num_sc...  72.4 us
    pallas_call x4, Pallas kernels, mlp_backward(): pl.pallas_call(functools.partial(mlp_back_kernel, steps), grid=(steps,),...  61.3 us
    pallas_call x4, Pallas kernels, mlp_forward(): pl.pallas_call(functools.partial(mlp_kernel, steps), grid=(steps,), in_sp...  54.7 us
  transfers between devices with their start and end apart: 72, of which 27 were waited for; matrix products, arithmetic and copies ran while one was open for 9% of the time, Pallas kernels for 42%

profile of v3, /device:TPU:0, one launch (start us, length us, event | category | flops | bytes accessed | tf_op | source)
XLA Modules:
  0.0 1102.6 jit_solution(14982284570962844901)
XLA Ops:
  19.8 6.3 all-to-all-start
  27.3 25.5 %all-to-all-done = bf16[8,256,256]{2,1,0:T(8,128)(2,1)} async-done(((bf16[8,256,256]{2,1,0:T(8,128)(2,1)}), bf16[8,256,256]{2,1,0:T(8,128)(2,1)}, u32[]{:S(2)}, u32[]{:S(2)}) %all-to-all-start) | async-done | bytes 1048608 | tf_op jit(solution)/shard_map/all_to_all | solution.py:1085
  52.8 18.4 %all_to_all.90 = s32[8,2,64,128]{3,2,1,0:T(8,128)} all-to-all(s32[8,2,64,128]{3,2,1,0:T(8,128)S(1)} %reshape.258), channel_id=1, replica_groups=mesh['ctx'=8,'fsdp'=4] {'ctx'}, dimensions={0} | all-to-all | bytes 1048576 | tf_op jit(solution)/shard_map/all_to_all | solution.py:1085
  90.2 6.3 qkv.4
  100.1 6.3 qkv.5
  106.4 31.4 %all-to-all-done.2.pieces = bf16[8,256,384]{2,1,0:T(8,128)(2,1)S(1)} async-done(((bf16[8,256,384]{2,1,0:T(8,128)(2,1)}), bf16[8,256,384]{2,1,0:T(8,128)(2,1)S(1)}, u32[]{:S(2)}, u32[]{:S(2)}) %all-to-all-start.2) | async-done | bytes 1572896 | tf_op jit(solution)/shard_map/all_to_all | solution.py:1085
  145.3 12.1 %local_attend.2 = (bf16[2048,128]{1,0:T(8,128)(2,1)}, bf16[2560,128]{1,0:T(8,128)(2,1)}, bf16[2560,128]{1,0:T(8,128)(2,1)}, bf16[16,128,640]{2,1,0:T(8,128)(2,1)}, bf16[8,256,128]{2,1,0:T(8,128)(2,1)}) custom-call(s32[20]{0:T(128)} %get-tuple-element.604.info, f32[33]{0:T(128)} %pad_maximum_fusion.2.rel, s32[128,640]{1,0:T(8,128)} %constant.64.clone.buckets, ...), custom_call_target="tpu_custom_call" | custom-call | flops 12000000000 | bytes 8000000 | tf_op jit(solution)/shard_map/local_attend/pallas_call | solution.py:818
  157.4 22.9 %all-to-all-done.3.pieces = bf16[8,256,384]{2,1,0:T(8,128)(2,1)S(1)} async-done(((bf16[8,256,384]{2,1,0:T(8,128)(2,1)}), bf16[8,256,384]{2,1,0:T(8,128)(2,1)S(1)}, u32[]{:S(2)}, u32[]{:S(2)}) %all-to-all-start.3) | async-done | bytes 1572896 | tf_op jit(solution)/shard_map/all_to_all | solution.py:1085
  190.2 12.1 %local_attend.3 = (bf16[2048,128]{1,0:T(8,128)(2,1)}, bf16[2560,128]{1,0:T(8,128)(2,1)}, bf16[2560,128]{1,0:T(8,128)(2,1)}, bf16[16,128,640]{2,1,0:T(8,128)(2,1)}, bf16[8,256,128]{2,1,0:T(8,128)(2,1)}) custom-call(s32[20]{0:T(128)} %get-tuple-element.605.info, f32[33]{0:T(128)} %pad_maximum_fusion.2.rel, s32[128,640]{1,0:T(8,128)} %constant.64.clone.buckets, ...), custom_call_target="tpu_custom_call" | custom-call | flops 12000000000 | bytes 8000000 | tf_op jit(solution)/shard_map/local_attend/pallas_call | solution.py:818
  211.4 18.1 %unfold.4 = (bf16[1024,1024]{1,0:T(8,128)(2,1)}, bf16[1024,3072]{1,0:T(8,128)(2,1)}, bf16[1024,4096]{1,0:T(8,128)(2,1)}, bf16[4096,1024]{1,0:T(8,128)(2,1)}) custom-call(s32[1]{0:T(128)} %bitcast.1.key, bf16[4,768,2048]{2,1,0:T(8,128)(2,1)} %bitcast.160, bf16[4,768,2048]{2,1,0:T(8,128)(2,1)} %collective-permute-done.4.twin), custom_call_target="tpu_custom_call" | custom-call | bytes 50331648 | tf_op jit(solution)/shard_map/unfold/pallas_call | solution.py:195
  229.5 14.4 %mlp.4 = (bf16[256,1024]{1,0:T(8,128)(2,1)}, f32[256,1024]{1,0:T(8,128)}, bf16[256,1024]{1,0:T(8,128)(2,1)}, bf16[256,4096]{1,0:T(8,128)(2,1)}, bf16[256,4096]{1,0:T(8,128)(2,1)}, /*index=5*/f32[256,1024]{1,0:T(8,128)}) custom-call(bf16[256,1024]{1,0:T(8,128)(2,1)} %get-tuple-element.256.x_ref, bf16[1024,1024]{1,0:T(8,128)(2,1)} %get-tuple-element.274.w_out, ...), custom_call_target="tpu_custom_call" | custom-call | flops 4831838208 | bytes 18874368 | tf_op jit(solution)/shard_map/mlp/pallas_call | solution.py:503
  244.0 6.5 qkv.6
  261.3 13.4 %mlp.5 = (bf16[256,1024]{1,0:T(8,128)(2,1)}, f32[256,1024]{1,0:T(8,128)}, bf16[256,1024]{1,0:T(8,128)(2,1)}, bf16[256,4096]{1,0:T(8,128)(2,1)}, bf16[256,4096]{1,0:T(8,128)(2,1)}, /*index=5*/f32[256,1024]{1,0:T(8,128)}) custom-call(bf16[256,1024]{1,0:T(8,128)(2,1)} %get-tuple-element.258.x_ref, bf16[1024,1024]{1,0:T(8,128)(2,1)} %get-tuple-element.274.w_out, ...), custom_call_target="tpu_custom_call" | custom-call | flops 4831838208 | bytes 18874368 | tf_op jit(solution)/shard_map/mlp/pallas_call | solution.py:503
  274.7 6.5 qkv.7
  281.2 12.7 %all-to-all-done.6.pieces = bf16[8,256,384]{2,1,0:T(8,128)(2,1)S(1)} async-done(((bf16[8,256,384]{2,1,0:T(8,128)(2,1)}), bf16[8,256,384]{2,1,0:T(8,128)(2,1)S(1)}, u32[]{:S(2)}, u32[]{:S(2)}) %all-to-all-start.6) | async-done | bytes 1572896 | tf_op jit(solution)/shard_map/all_to_all | solution.py:1085
  297.5 33.2 %recall_attend.2 = (bf16[2048,128]{1,0:T(8,128)(2,1)}, bf16[2560,128]{1,0:T(8,128)(2,1)}, bf16[2560,128]{1,0:T(8,128)(2,1)}, bf16[16,128,640]{2,1,0:T(8,128)(2,1...) custom-call(s32[20]{0:T(128)} %get-tuple-element.604.info, f32[33]{0:T(128)} %pad_maximum_fusion.3.rel, ...), custom_call_target="tpu_custom_call" | custom-call | flops 44999999488 | bytes 8000000 | tf_op jit(solution)/shard_map/recall_attend/pallas_call | solution.py:818
  341.9 33.2 %recall_attend.3 = (bf16[2048,128]{1,0:T(8,128)(2,1)}, bf16[2560,128]{1,0:T(8,128)(2,1)}, bf16[2560,128]{1,0:T(8,128)(2,1)}, bf16[16,128,640]{2,1,0:T(8,128)(2,1...) custom-call(s32[20]{0:T(128)} %get-tuple-element.605.info, f32[33]{0:T(128)} %pad_maximum_fusion.3.rel, ...), custom_call_target="tpu_custom_call" | custom-call | flops 44999999488 | bytes 8000000 | tf_op jit(solution)/shard_map/recall_attend/pallas_call | solution.py:818
  383.3 13.3 %unfold.5 = (bf16[1024,4096]{1,0:T(8,128)(2,1)}, bf16[4096,1024]{1,0:T(8,128)(2,1)}, bf16[1024,1024]{1,0:T(8,128)(2,1)}) custom-call(s32[1]{0:T(128)} %bitcast.1.key, bf16[4,576,2048]{2,1,0:T(8,128)(2,1)} %bitcast.162, bf16[4,576,2048]{2,1,0:T(8,128)(2,1)} %collective-permute-done.5.twin), custom_call_target="tpu_custom_call" | custom-call | bytes 37748736 | tf_op jit(solution)/shard_map/unfold/pallas_call | solution.py:195
  396.6 13.4 %mlp.6 = (bf16[256,1024]{1,0:T(8,128)(2,1)}, f32[256,1024]{1,0:T(8,128)}, bf16[256,1024]{1,0:T(8,128)(2,1)}, bf16[256,4096]{1,0:T(8,128)(2,1)}, bf16[256,4096]{1,0:T(8,128)(2,1)}, /*index=5*/bf16[256,1024]{1,0:T(8,128)(2,1)}) custom-call(f32[256,1024]{1,0:T(8,128)} %get-tuple-element.282.x_ref, bf16[1024,1024]{1,0:T(8,128)(2,1)} %get-tuple-element.302.w_out, ...), custom_call_target="tpu_custom_call" | custom-call | flops 4831838208 | bytes 18874368 | tf_op jit(solution)/shard_map/mlp/pallas_call | solution.py:503
  410.9 13.4 %mlp.7 = (bf16[256,1024]{1,0:T(8,128)(2,1)}, f32[256,1024]{1,0:T(8,128)}, bf16[256,1024]{1,0:T(8,128)(2,1)}, bf16[256,4096]{1,0:T(8,128)(2,1)}, bf16[256,4096]{1,0:T(8,128)(2,1)}, /*index=5*/bf16[256,1024]{1,0:T(8,128)(2,1)}) custom-call(f32[256,1024]{1,0:T(8,128)} %get-tuple-element.288.x_ref, bf16[1024,1024]{1,0:T(8,128)(2,1)} %get-tuple-element.302.w_out, ...), custom_call_target="tpu_custom_call" | custom-call | flops 4831838208 | bytes 18874368 | tf_op jit(solution)/shard_map/mlp/pallas_call | solution.py:503
  424.3 15.1 %mlp_back.4 = (bf16[256,4096]{1,0:T(8,128)(2,1)}, bf16[256,1024]{1,0:T(8,128)(2,1)}, f32[256,1024]{1,0:T(8,128)}, f32[1,1024]{1,0:T(1,128)}, f32[1,1024]{1,0:T(1,128)}, /*index=5*/bf16[8,256,128]{2,1,0:T(8,128)(2,1)}) custom-call(bf16[256,1024]{1,0:T(8,128)(2,1)} %get-tuple-element.313.g_ref.k0.s0, bf16[256,4096]{1,0:T(8,128)(2,1)} %get-tuple-element.314.up, ...), custom_call_target="tpu_custom_call" | custom-call | flops 4831838208 | bytes 18874368 | tf_op jit(solution)/shard_map/mlp_back/pallas_call | solution.py:574
  444.8 15.1 %mlp_back.5 = (bf16[256,4096]{1,0:T(8,128)(2,1)}, bf16[256,1024]{1,0:T(8,128)(2,1)}, f32[256,1024]{1,0:T(8,128)}, f32[1,1024]{1,0:T(1,128)}, f32[1,1024]{1,0:T(1,128)}, /*index=5*/bf16[8,256,128]{2,1,0:T(8,128)(2,1)}) custom-call(bf16[256,1024]{1,0:T(8,128)(2,1)} %get-tuple-element.320.g_ref.k1.s1, bf16[256,4096]{1,0:T(8,128)(2,1)} %get-tuple-element.321.up, ...), custom_call_target="tpu_custom_call" | custom-call | flops 4831838208 | bytes 18874368 | tf_op jit(solution)/shard_map/mlp_back/pallas_call | solution.py:574
  459.9 11.6 %weight_grad.9 = (bf16[4,512,2048]{2,1,0:T(8,128)(2,1)}, bf16[4,512,2048]{2,1,0:T(8,128)(2,1)}) custom-call(s32[5]{0:T(128)} %pad_add_fusion.2.key, bf16[256,1024]{1,0:T(8,128)(2,1)} %get-tuple-element.324.a0, bf16[256,1024]{1,0:T(8,128)(2,1)} %get-tuple-element.325.a1, bf16[256,4096]{1,0:T(8,128)(2,1)} %get-tuple-element.326.k0.s0, ...), custom_call_target="tpu_custom_call" | custom-call | flops 4294967296 | bytes 16777216 | tf_op jit(solution)/shard_map/weight_grad/pallas_call | solution.py:380
  471.5 9.3 weight_grad.10
  486.2 32.1 %recall_back.2 = (f32[32,128]{1,0:T(8,128)}, f32[8,128]{1,0:T(8,128)}, bf16[8,256,384]{2,1,0:T(8,128)(2,1)}) custom-call(s32[20]{0:T(128)} %get-tuple-element.604.info, f32[33]{0:T(128)} %pad_maximum_fusion.3.rel, s32[128,640]{1,0:T(8,128)} %constant.64.clone.buckets, bf16[8,256,128]{2,1,0:T(8,128)(2,1)} %copy-done.32, ...), custom_call_target="tpu_custom_call" | custom-call | flops 49999998976 | bytes 8000000 | tf_op jit(solution)/shard_map/recall_back/pallas_call | solution.py:939
  518.2 10.5 add_convert_fusion
  535.0 32.7 %recall_back.3 = (f32[32,128]{1,0:T(8,128)}, f32[8,128]{1,0:T(8,128)}, bf16[8,256,384]{2,1,0:T(8,128)(2,1)}) custom-call(s32[20]{0:T(128)} %get-tuple-element.605.info, f32[33]{0:T(128)} %pad_maximum_fusion.3.rel, s32[128,640]{1,0:T(8,128)} %constant.64.clone.buckets, bf16[8,256,128]{2,1,0:T(8,128)(2,1)} %copy-done.34, ...), custom_call_target="tpu_custom_call" | custom-call | flops 49999998976 | bytes 8000000 | tf_op jit(solution)/shard_map/recall_back/pallas_call | solution.py:939
  581.8 8.1 qkv_back.4
  590.0 15.7 %mlp_back.6 = (bf16[256,4096]{1,0:T(8,128)(2,1)}, bf16[256,1024]{1,0:T(8,128)(2,1)}, f32[256,1024]{1,0:T(8,128)}, f32[1,1024]{1,0:T(1,128)}, f32[1,1024]{1,0:T(1,128)}, /*index=5*/bf16[8,256,128]{2,1,0:T(8,128)(2,1)}) custom-call(f32[256,1024]{1,0:T(8,128)} %get-tuple-element.365.g_ref, bf16[256,4096]{1,0:T(8,128)(2,1)} %get-tuple-element.366.up, ...), custom_call_target="tpu_custom_call" | custom-call | flops 4831838208 | bytes 18874368 | tf_op jit(solution)/shard_map/mlp_back/pallas_call | solution.py:574
  605.6 8.5 all-to-all-done.13.pieces
  619.0 8.1 qkv_back.5
  627.1 15.3 %mlp_back.7 = (bf16[256,4096]{1,0:T(8,128)(2,1)}, bf16[256,1024]{1,0:T(8,128)(2,1)}, f32[256,1024]{1,0:T(8,128)}, f32[1,1024]{1,0:T(1,128)}, f32[1,1024]{1,0:T(1,128)}, /*index=5*/bf16[8,256,128]{2,1,0:T(8,128)(2,1)}) custom-call(f32[256,1024]{1,0:T(8,128)} %get-tuple-element.378.g_ref, bf16[256,4096]{1,0:T(8,128)(2,1)} %get-tuple-element.379.up, ...), custom_call_target="tpu_custom_call" | custom-call | flops 4831838208 | bytes 18874368 | tf_op jit(solution)/shard_map/mlp_back/pallas_call | solution.py:574
  647.5 13.2 %local_back.2 = (f32[32,128]{1,0:T(8,128)}, bf16[8,256,384]{2,1,0:T(8,128)(2,1)}) custom-call(s32[20]{0:T(128)} %get-tuple-element.604.info, f32[33]{0:T(128)} %pad_maximum_fusion.2.rel, s32[128,640]{1,0:T(8,128)} %constant.64.clone.buckets, bf16[8,256,128]{2,1,0:T(8,128)(2,1)} %copy-done.33, bf16[2048,128]{1,0:T(8,128)(2,1)} %get-tuple-element.383.refs_0_, ...), custom_call_target="tpu_custom_call" | custom-call | flops 20000000000 | bytes 8000000 | tf_op jit(solution)/shard_map/local_back/pallas_call | solution.py:939
  660.7 11.5 %weight_grad.12 = (bf16[4,256,2048]{2,1,0:T(8,128)(2,1)}, bf16[4,256,2048]{2,1,0:T(8,128)(2,1)}) custom-call(s32[5]{0:T(128)} %pad_add_fusion.3.key, bf16[256,1024]{1,0:T(8,128)(2,1)} %get-tuple-element.391.a0, bf16[256,1024]{1,0:T(8,128)(2,1)} %get-tuple-element.392.a1, bf16[256,4096]{1,0:T(8,128)(2,1)} %get-tuple-element.393.k0.s0, ...), custom_call_target="tpu_custom_call" | custom-call | flops 4294967296 | bytes 16777216 | tf_op jit(solution)/shard_map/weight_grad/pallas_call | solution.py:380
  672.3 9.2 weight_grad.13
  687.6 13.2 %local_back.3 = (f32[32,128]{1,0:T(8,128)}, bf16[8,256,384]{2,1,0:T(8,128)(2,1)}) custom-call(s32[20]{0:T(128)} %get-tuple-element.605.info, f32[33]{0:T(128)} %pad_maximum_fusion.2.rel, s32[128,640]{1,0:T(8,128)} %constant.64.clone.buckets, bf16[8,256,128]{2,1,0:T(8,128)(2,1)} %copy-done.35, bf16[2048,128]{1,0:T(8,128)(2,1)} %get-tuple-element.408.refs_0_, ...), custom_call_target="tpu_custom_call" | custom-call | flops 20000000000 | bytes 8000000 | tf_op jit(solution)/shard_map/local_back/pallas_call | solution.py:939
  700.8 8.0 weight_grad.14
  710.3 28.3 %all-to-all-done.16.pieces = bf16[8,256,384]{2,1,0:T(8,128)(2,1)S(1)} async-done(((bf16[8,256,384]{2,1,0:T(8,128)(2,1)}), bf16[8,256,384]{2,1,0:T(8,128)(2,1)S(1)}, u32[]{:S(2)}, u32[]{:S(2)}) %all-to-all-start.16) | async-done | bytes 1572896 | tf_op jit(solution)/shard_map/all_to_all | solution.py:1085
  756.2 8.4 qkv_back.6
  764.6 6.5 add_convert_fusion.1
  771.1 23.2 %all-to-all-done.17.pieces = bf16[8,256,384]{2,1,0:T(8,128)(2,1)S(1)} async-done(((bf16[8,256,384]{2,1,0:T(8,128)(2,1)}), bf16[8,256,384]{2,1,0:T(8,128)(2,1)S(1)}, u32[]{:S(2)}, u32[]{:S(2)}) %all-to-all-start.17) | async-done | bytes 1572896 | tf_op jit(solution)/shard_map/all_to_all | solution.py:1085
  806.5 8.0 qkv_back.7
  859.5 45.7 %collective-permute-done.24 = bf16[2,256,512]{2,1,0:T(8,128)(2,1)S(1)} collective-permute-done((bf16[2,256,512]{2,1,0:T(8,128)(2,1)S(1)}, bf16[2,256,512]{2,1,0:T(8,128)(2,1)S(1)}, u32[]{:S(2)}, u32[]{:S(2)}) %collective-permute-start.24) | collective-permute-done | bytes 524320 | tf_op jit(solution)/shard_map/ppermute | solution.py:316
  918.5 14.3 %collective-permute-done.21 = bf16[2,256,768]{2,1,0:T(8,128)(2,1)S(1)} collective-permute-done((bf16[2,256,768]{2,1,0:T(8,128)(2,1)S(1)}, bf16[2,256,768]{2,1,0:T(8,128)(2,1)S(1)}, u32[]{:S(2)}, u32[]{:S(2)}) %collective-permute-start.21) | collective-permute-done | bytes 786464 | tf_op jit(solution)/shard_map/ppermute | solution.py:316
  959.4 15.3 %collective-permute-done.27 = bf16[128,2048]{1,0:T(8,128)(2,1)S(1)} collective-permute-done((bf16[128,2048]{1,0:T(8,128)(2,1)S(1)}, bf16[128,2048]{1,0:T(8,128)(2,1)S(1)}, u32[]{:S(2)}, u32[]{:S(2)}) %collective-permute-start.27) | collective-permute-done | bytes 524320 | tf_op jit(solution)/shard_map/ppermute | solution.py:316
  995.8 13.4 %collective-permute-done.45 = bf16[256,2048]{1,0:T(8,128)(2,1)S(1)} collective-permute-done((bf16[256,2048]{1,0:T(8,128)(2,1)}, bf16[256,2048]{1,0:T(8,128)(2,1)S(1)}, u32[]{:S(2)}, u32[]{:S(2)}) %collective-permute-start.45) | collective-permute-done | bytes 1048608 | tf_op jit(solution)/shard_map/ppermute | solution.py:316
  1018.0 22.2 %collective-permute-done.42 = bf16[256,2048]{1,0:T(8,128)(2,1)S(1)} collective-permute-done((bf16[256,2048]{1,0:T(8,128)(2,1)S(1)}, bf16[256,2048]{1,0:T(8,128)(2,1)S(1)}, u32[]{:S(2)}, u32[]{:S(2)}) %collective-permute-start.42) | collective-permute-done | bytes 1048608 | tf_op jit(solution)/shard_map/ppermute | solution.py:316
  1040.5 32.0 %collective-permute-done.47 = bf16[256,2048]{1,0:T(8,128)(2,1)S(1)} collective-permute-done((bf16[256,2048]{1,0:T(8,128)(2,1)S(1)}, bf16[256,2048]{1,0:T(8,128)(2,1)S(1)}, u32[]{:S(2)}, u32[]{:S(2)}) %collective-permute-start.47) | collective-permute-done | bytes 1048608 | tf_op jit(solution)/shard_map/ppermute | solution.py:316
  (434 shorter events, 309.6 us)
Async XLA Ops:
  7.2 64.1 %all-gather.7.cloned.1.call-start = ((), (), s32[]{:S(2)}) async-start(), calls=%async_computation.21 | async-start | bytes 3932160 | tf_op jit(solution)/shard_map/all_gather | solution.py:1059
  9.3 173.1 %all-gather.9.cloned.1.call-start = ((), (), s32[]{:S(2)}) async-start(), calls=%async_computation.22 | async-start | bytes 15728640 | tf_op jit(solution)/shard_map/all_gather | solution.py:1059
  19.8 33.0 %all-to-all-start = ((bf16[8,256,256]{2,1,0:T(8,128)(2,1)}), bf16[8,256,256]{2,1,0:T(8,128)(2,1)}, u32[]{:S(2)}, u32[]{:S(2)}) async-start(bf16[8,256,256]{2,1,0:T(8,128)(2,1)} %fusion.12), calls=%async_computation | async-start | bytes 2097152 | tf_op jit(solution)/shard_map/all_to_all | solution.py:1085
  96.5 41.3 %all-to-all-start.2 = ((bf16[8,256,384]{2,1,0:T(8,128)(2,1)}), bf16[8,256,384]{2,1,0:T(8,128)(2,1)S(1)}, u32[]{:S(2)}, u32[]{:S(2)}) async-start(bf16[8,256,384]{2,1,0:T(8,128)(2,1)} %bitcast.171), calls=%async_computation.2 | async-start | bytes 3145728 | tf_op jit(solution)/shard_map/all_to_all | solution.py:1085
  139.0 41.3 %all-to-all-start.3 = ((bf16[8,256,384]{2,1,0:T(8,128)(2,1)}), bf16[8,256,384]{2,1,0:T(8,128)(2,1)S(1)}, u32[]{:S(2)}, u32[]{:S(2)}) async-start(bf16[8,256,384]{2,1,0:T(8,128)(2,1)} %bitcast.168), calls=%async_computation.3 | async-start | bytes 3145728 | tf_op jit(solution)/shard_map/all_to_all | solution.py:1085
  142.6 192.7 %all-gather.11.cloned.1.call-start = ((), (), s32[]{:S(2)}) async-start(), calls=%async_computation.23 | async-start | bytes 11796480 | tf_op jit(solution)/shard_map/all_gather | solution.py:1059
  182.4 29.1 %collective-permute-start.4 = (bf16[4,768,2048]{2,1,0:T(8,128)(2,1)}, bf16[4,768,2048]{2,1,0:T(8,128)(2,1)}, u32[]{:S(2)}, u32[]{:S(2)}) collective-permute-start(bf16[4,768,2048]{2,1,0:T(8,128)(2,1)} %bitcast.159), channel_id=1, source_target_pairs={{0,4},{4,0},{8,12},{12,8},{16,20},{20,16},{24,28},{28,24},{1,5},{5... | collective-permute-start | bytes 37748744 | tf_op jit(solution)/shard_map/ppermute | solution.py:109
  205.5 44.9 %all-to-all-start.5 = ((bf16[8,256,128]{2,1,0:T(8,128)(2,1)}), bf16[8,256,128]{2,1,0:T(8,128)(2,1)S(1)}, u32[]{:S(2)}, u32[]{:S(2)}) async-start(bf16[8,256,128]{2,1,0:T(8,128)(2,1)} %get-tuple-element.280), calls=%async_computation.5 | async-start | bytes 1048576 | tf_op jit(solution)/shard_map/all_to_all | solution.py:1085
  250.4 43.5 %all-to-all-start.6 = ((bf16[8,256,384]{2,1,0:T(8,128)(2,1)}), bf16[8,256,384]{2,1,0:T(8,128)(2,1)S(1)}, u32[]{:S(2)}, u32[]{:S(2)}) async-start(bf16[8,256,384]{2,1,0:T(8,128)(2,1)} %bitcast.169), calls=%async_computation.6 | async-start | bytes 3145728 | tf_op jit(solution)/shard_map/all_to_all | solution.py:1085
  293.9 41.3 %all-to-all-start.7 = ((bf16[8,256,384]{2,1,0:T(8,128)(2,1)}), bf16[8,256,384]{2,1,0:T(8,128)(2,1)S(1)}, u32[]{:S(2)}, u32[]{:S(2)}) async-start(bf16[8,256,384]{2,1,0:T(8,128)(2,1)} %bitcast.170), calls=%async_computation.7 | async-start | bytes 3145728 | tf_op jit(solution)/shard_map/all_to_all | solution.py:1085
  335.3 48.0 %collective-permute-start.5 = (bf16[4,576,2048]{2,1,0:T(8,128)(2,1)}, bf16[4,576,2048]{2,1,0:T(8,128)(2,1)}, u32[]{:S(2)}, u32[]{:S(2)}) collective-permute-start(bf16[4,576,2048]{2,1,0:T(8,128)(2,1)} %bitcast.161), channel_id=1, source_target_pairs={{0,4},{4,0},{8,12},{12,8},{16,20},{20,16},{24,28},{28,24},{1,5},{5... | collective-permute-start | bytes 28311560 | tf_op jit(solution)/shard_map/ppermute | solution.py:109
  338.4 36.7 %all-to-all-start.8 = ((bf16[8,256,128]{2,1,0:T(8,128)(2,1)}), bf16[8,256,128]{2,1,0:T(8,128)(2,1)S(1)}, u32[]{:S(2)}, u32[]{:S(2)}) async-start(bf16[8,256,128]{2,1,0:T(8,128)(2,1)} %get-tuple-element.305), calls=%async_computation.8 | async-start | bytes 1048576 | tf_op jit(solution)/shard_map/all_to_all | solution.py:1085
  375.1 34.9 %all-to-all-start.9 = ((bf16[8,256,128]{2,1,0:T(8,128)(2,1)}), bf16[8,256,128]{2,1,0:T(8,128)(2,1)S(1)}, u32[]{:S(2)}, u32[]{:S(2)}) async-start(bf16[8,256,128]{2,1,0:T(8,128)(2,1)} %get-tuple-element.308), calls=%async_computation.9 | async-start | bytes 1048576 | tf_op jit(solution)/shard_map/all_to_all | solution.py:1085
  439.4 41.4 %all-to-all-start.10 = ((bf16[8,256,128]{2,1,0:T(8,128)(2,1)}), bf16[8,256,128]{2,1,0:T(8,128)(2,1)S(1)}, u32[]{:S(2)}, u32[]{:S(2)}) async-start(bf16[8,256,128]{2,1,0:T(8,128)(2,1)} %get-tuple-element.318), calls=%async_computation.10 | async-start | bytes 1048576 | tf_op jit(solution)/shard_map/all_to_all | solution.py:1085
  480.8 37.4 %collective-permute-start.6 = (bf16[4,512,2048]{2,1,0:T(8,128)(2,1)}, bf16[4,512,2048]{2,1,0:T(8,128)(2,1)}, u32[]{:S(2)}, u32[]{:S(2)}) collective-permute-start(bf16[4,512,2048]{2,1,0:T(8,128)(2,1)} %get-tuple-element.345), channel_id=1, source_target_pairs={{0,4},{4,0},{8,12},{12,8},{16,20},{20,16},{24,28},{28,24},{1,5},{5... | collective-permute-start | bytes 25165832 | tf_op jit(solution)/shard_map/ppermute | solution.py:109
  481.4 47.3 %all-to-all-start.11 = ((bf16[8,256,128]{2,1,0:T(8,128)(2,1)}), bf16[8,256,128]{2,1,0:T(8,128)(2,1)S(1)}, u32[]{:S(2)}, u32[]{:S(2)}) async-start(bf16[8,256,128]{2,1,0:T(8,128)(2,1)} %get-tuple-element.342), calls=%async_computation.11 | async-start | bytes 1048576 | tf_op jit(solution)/shard_map/all_to_all | solution.py:1085
  486.1 132.9 %reduce-scatter.7.cloned.1.call-start = ((), (), s32[]{:S(2)}) async-start(), calls=%async_computation.24 | async-start | bytes 10485760
  529.5 43.3 %all-to-all-start.12 = ((bf16[8,256,384]{2,1,0:T(8,128)(2,1)}), bf16[8,256,384]{2,1,0:T(8,128)(2,1)S(1)}, u32[]{:S(2)}, u32[]{:S(2)}) async-start(bf16[8,256,384]{2,1,0:T(8,128)(2,1)} %get-tuple-element.343), calls=%async_computation.12 | async-start | bytes 3145728 | tf_op jit(solution)/shard_map/all_to_all | solution.py:1085
  572.8 41.3 %all-to-all-start.13 = ((bf16[8,256,384]{2,1,0:T(8,128)(2,1)}), bf16[8,256,384]{2,1,0:T(8,128)(2,1)S(1)}, u32[]{:S(2)}, u32[]{:S(2)}) async-start(bf16[8,256,384]{2,1,0:T(8,128)(2,1)} %get-tuple-element.370), calls=%async_computation.13 | async-start | bytes 3145728 | tf_op jit(solution)/shard_map/all_to_all | solution.py:1085
  614.2 28.3 %all-to-all-start.14 = ((bf16[8,256,128]{2,1,0:T(8,128)(2,1)}), bf16[8,256,128]{2,1,0:T(8,128)(2,1)S(1)}, u32[]{:S(2)}, u32[]{:S(2)}) async-start(bf16[8,256,128]{2,1,0:T(8,128)(2,1)} %get-tuple-element.371), calls=%async_computation.14 | async-start | bytes 1048576 | tf_op jit(solution)/shard_map/all_to_all | solution.py:1085
  642.4 39.0 %all-to-all-start.15 = ((bf16[8,256,128]{2,1,0:T(8,128)(2,1)}), bf16[8,256,128]{2,1,0:T(8,128)(2,1)S(1)}, u32[]{:S(2)}, u32[]{:S(2)}) async-start(bf16[8,256,128]{2,1,0:T(8,128)(2,1)} %get-tuple-element.388), calls=%async_computation.15 | async-start | bytes 1048576 | tf_op jit(solution)/shard_map/all_to_all | solution.py:1085
  681.5 60.8 %collective-permute-start.7 = (bf16[4,256,2048]{2,1,0:T(8,128)(2,1)}, bf16[4,256,2048]{2,1,0:T(8,128)(2,1)}, u32[]{:S(2)}, u32[]{:S(2)}) collective-permute-start(bf16[4,256,2048]{2,1,0:T(8,128)(2,1)} %get-tuple-element.401), channel_id=1, source_target_pairs={{0,4},{4,0},{8,12},{12,8},{16,20},{20,16},{24,28},{28,24},{1,5},{5... | collective-permute-start | bytes 12582920 | tf_op jit(solution)/shard_map/ppermute | solution.py:316
  682.0 56.5 %all-to-all-start.16 = ((bf16[8,256,384]{2,1,0:T(8,128)(2,1)}), bf16[8,256,384]{2,1,0:T(8,128)(2,1)S(1)}, u32[]{:S(2)}, u32[]{:S(2)}) async-start(bf16[8,256,384]{2,1,0:T(8,128)(2,1)} %get-tuple-element.389), calls=%async_computation.16 | async-start | bytes 3145728 | tf_op jit(solution)/shard_map/all_to_all | solution.py:1085
  686.8 166.3 %all-reduce.6.cloned.1.call-start = ((), (), s32[]{:S(2)}) async-start(), calls=%async_computation.20 | async-start | bytes 4194304 | tf_op jit(solution)/shard_map/psum | solution.py:1216
  687.1 60.0 %collective-permute-start.8 = (bf16[4,256,2048]{2,1,0:T(8,128)(2,1)}, bf16[4,256,2048]{2,1,0:T(8,128)(2,1)}, u32[]{:S(2)}, u32[]{:S(2)}) collective-permute-start(bf16[4,256,2048]{2,1,0:T(8,128)(2,1)} %get-tuple-element.403), channel_id=1, source_target_pairs={{0,4},{4,0},{8,12},{12,8},{16,20},{20,16},{24,28},{28,24},{1,5},{5... | collective-permute-start | bytes 12582920 | tf_op jit(solution)/shard_map/ppermute | solution.py:316
  708.8 55.8 %collective-permute-start.9 = (bf16[4,256,2048]{2,1,0:T(8,128)(2,1)}, bf16[4,256,2048]{2,1,0:T(8,128)(2,1)}, u32[]{:S(2)}, u32[]{:S(2)}) collective-permute-start(bf16[4,256,2048]{2,1,0:T(8,128)(2,1)} %get-tuple-element.416), channel_id=1, source_target_pairs={{0,4},{4,0},{8,12},{12,8},{16,20},{20,16},{24,28},{28,24},{1,5},{5... | collective-permute-start | bytes 12582920 | tf_op jit(solution)/shard_map/ppermute | solution.py:109
  738.6 55.8 %all-to-all-start.17 = ((bf16[8,256,384]{2,1,0:T(8,128)(2,1)}), bf16[8,256,384]{2,1,0:T(8,128)(2,1)S(1)}, u32[]{:S(2)}, u32[]{:S(2)}) async-start(bf16[8,256,384]{2,1,0:T(8,128)(2,1)} %get-tuple-element.420), calls=%async_computation.17 | async-start | bytes 3145728 | tf_op jit(solution)/shard_map/all_to_all | solution.py:1085
  742.2 239.3 %reduce-scatter.9.cloned.1.call-start = ((), (), s32[]{:S(2)}) async-start(), calls=%async_computation.25 | async-start | bytes 5242880
  750.8 48.2 %collective-permute-start.10 = (bf16[2,256,2048]{2,1,0:T(8,128)(2,1)}, bf16[2,256,2048]{2,1,0:T(8,128)(2,1)}, u32[]{:S(2)}, u32[]{:S(2)}) collective-permute-start(bf16[2,256,2048]{2,1,0:T(8,128)(2,1)} %add_convert_fusion.3), channel_id=1, source_target_pairs={{0,1},{1,0},{2,3},{3,2},{4,5},{5,4},{6,7},{7,6},{8,9},{9,8},{10,11... | collective-permute-start | bytes 6291464 | tf_op jit(solution)/shard_map/ppermute | solution.py:316
  755.1 48.0 %collective-permute-start.11 = (bf16[2,256,2048]{2,1,0:T(8,128)(2,1)}, bf16[2,256,2048]{2,1,0:T(8,128)(2,1)}, u32[]{:S(2)}, u32[]{:S(2)}) collective-permute-start(bf16[2,256,2048]{2,1,0:T(8,128)(2,1)} %add_convert_fusion.2), channel_id=1, source_target_pairs={{0,2},{1,3},{2,0},{3,1},{4,6},{5,7},{6,4},{7,5},{8,10},{9,11},{10,... | collective-permute-start | bytes 6291464 | tf_op jit(solution)/shard_map/ppermute | solution.py:316
  816.1 39.6 %collective-permute-start.35 = (bf16[1,256,2048]{2,1,0:T(8,128)(2,1)}, bf16[1,256,2048]{2,1,0:T(8,128)(2,1)S(1)}, u32[]{:S(2)}, u32[]{:S(2)}) collective-permute-start(bf16[1,256,2048]{2,1,0:T(8,128)(2,1)} %add_convert_fusion.13), channel_id=1, source_target_pairs={{0,2},{1,3},{2,0},{3,1},{4,6},{5,7},{6,4},{7,5},{8,10},{9,11},{10,... | collective-permute-start | bytes 3145736 | tf_op jit(solution)/shard_map/ppermute | solution.py:316
  846.1 62.9 %collective-permute-start.20 = (bf16[4,256,768]{2,1,0:T(8,128)(2,1)}, bf16[4,256,768]{2,1,0:T(8,128)(2,1)}, u32[]{:S(2)}, u32[]{:S(2)}) collective-permute-start(bf16[4,256,768]{2,1,0:T(8,128)(2,1)} %get-tuple-element.459), channel_id=1, source_target_pairs={{0,4},{4,0},{8,12},{12,8},{16,20},{20,16},{24,28},{28,24},{1,5},{5... | collective-permute-start | bytes 4718600 | tf_op jit(solution)/shard_map/ppermute | solution.py:316
  846.1 65.7 %collective-permute-start.17 = (bf16[4,256,768]{2,1,0:T(8,128)(2,1)}, bf16[4,256,768]{2,1,0:T(8,128)(2,1)}, u32[]{:S(2)}, u32[]{:S(2)}) collective-permute-start(bf16[4,256,768]{2,1,0:T(8,128)(2,1)} %get-tuple-element.456), channel_id=1, source_target_pairs={{0,4},{4,0},{8,12},{12,8},{16,20},{20,16},{24,28},{28,24},{1,5},{5... | collective-permute-start | bytes 4718600 | tf_op jit(solution)/shard_map/ppermute | solution.py:316
  853.4 60.5 %collective-permute-start.39 = (bf16[1,256,2048]{2,1,0:T(8,128)(2,1)}, bf16[1,256,2048]{2,1,0:T(8,128)(2,1)S(1)}, u32[]{:S(2)}, u32[]{:S(2)}) collective-permute-start(bf16[1,256,2048]{2,1,0:T(8,128)(2,1)} %add_convert_fusion.12), channel_id=1, source_target_pairs={{0,1},{1,0},{2,3},{3,2},{4,5},{5,4},{6,7},{7,6},{8,9},{9,8},{10,11... | collective-permute-start | bytes 3145736 | tf_op jit(solution)/shard_map/ppermute | solution.py:316
  854.6 90.1 %collective-permute-start.26 = (bf16[512,2048]{1,0:T(8,128)(2,1)}, bf16[512,2048]{1,0:T(8,128)(2,1)S(1)}, u32[]{:S(2)}, u32[]{:S(2)}) collective-permute-start(bf16[512,2048]{1,0:T(8,128)(2,1)} %all-reduce.6.cloned.1.call-done.refs_0_), channel_id=1, source_target_pairs={{0,4},{4,0},{8,12},{12,8},{16,20},{20,16},{24,28},{28,24},{1,5},{5... | collective-permute-start | bytes 6291464 | tf_op jit(solution)/shard_map/ppermute | solution.py:109
  855.8 49.3 %collective-permute-start.24 = (bf16[2,256,512]{2,1,0:T(8,128)(2,1)S(1)}, bf16[2,256,512]{2,1,0:T(8,128)(2,1)S(1)}, u32[]{:S(2)}, u32[]{:S(2)}) collective-permute-start(bf16[2,256,512]{2,1,0:T(8,128)(2,1)S(1)} %add_convert_fusion.20), channel_id=1, source_target_pairs={{0,1},{1,0},{2,3},{3,2},{4,5},{5,4},{6,7},{7,6},{8,9},{9,8},{10,11... | collective-permute-start | bytes 1572872 | tf_op jit(solution)/shard_map/ppermute | solution.py:316
  905.1 33.4 %collective-permute-start.36 = (bf16[256,2048]{1,0:T(8,128)(2,1)S(1)}, bf16[256,2048]{1,0:T(8,128)(2,1)S(1)}, u32[]{:S(2)}, u32[]{:S(2)}) collective-permute-start(bf16[256,2048]{1,0:T(8,128)(2,1)S(1)} %fusion), channel_id=1, source_target_pairs={{0,8},{4,12},{24,16},{28,20},{1,9},{5,13},{25,17},{29,21},{2,10},{... | collective-permute-start | bytes 3145736 | tf_op jit(solution)/shard_map/ppermute | solution.py:316
  940.6 42.6 %collective-permute-start.40 = (bf16[256,2048]{1,0:T(8,128)(2,1)S(1)}, bf16[256,2048]{1,0:T(8,128)(2,1)}, u32[]{:S(2)}, u32[]{:S(2)}) collective-permute-start(bf16[256,2048]{1,0:T(8,128)(2,1)S(1)} %fusion.1), channel_id=1, source_target_pairs={{0,8},{4,12},{24,16},{28,20},{1,9},{5,13},{25,17},{29,21},{2,10},{... | collective-permute-start | bytes 3145736 | tf_op jit(solution)/shard_map/ppermute | solution.py:316
  958.1 52.2 %collective-permute-start.38 = (bf16[256,2048]{1,0:T(8,128)(2,1)S(1)}, bf16[256,2048]{1,0:T(8,128)(2,1)}, u32[]{:S(2)}, u32[]{:S(2)}) collective-permute-start(bf16[256,2048]{1,0:T(8,128)(2,1)S(1)} %add_convert_fusion.9), channel_id=1, source_target_pairs={{8,0},{12,4},{16,24},{20,28},{9,1},{13,5},{17,25},{21,29},{10,2},{... | collective-permute-start | bytes 3145736 | tf_op jit(solution)/shard_map/ppermute | solution.py:316
  981.5 27.7 %collective-permute-start.45 = (bf16[256,2048]{1,0:T(8,128)(2,1)}, bf16[256,2048]{1,0:T(8,128)(2,1)S(1)}, u32[]{:S(2)}, u32[]{:S(2)}) collective-permute-start(bf16[256,2048]{1,0:T(8,128)(2,1)} %bitcast.172), channel_id=1, source_target_pairs={{0,8},{4,12},{24,16},{28,20},{1,9},{5,13},{25,17},{29,21},{2,10},{... | collective-permute-start | bytes 3145736 | tf_op jit(solution)/shard_map/ppermute | solution.py:316
  984.8 27.0 %collective-permute-start.41 = (bf16[256,2048]{1,0:T(8,128)(2,1)S(1)}, bf16[256,2048]{1,0:T(8,128)(2,1)S(1)}, u32[]{:S(2)}, u32[]{:S(2)}) collective-permute-start(bf16[256,2048]{1,0:T(8,128)(2,1)S(1)} %add_convert_fusion.7), channel_id=1, source_target_pairs={{8,16},{12,20},{16,8},{20,12},{9,17},{13,21},{17,9},{21,13},{10,18... | collective-permute-start | bytes 3145736 | tf_op jit(solution)/shard_map/ppermute | solution.py:316
  992.6 22.6 %collective-permute-start.31 = (bf16[128,2048]{1,0:T(8,128)(2,1)S(1)}, bf16[128,2048]{1,0:T(8,128)(2,1)S(1)}, u32[]{:S(2)}, u32[]{:S(2)}) collective-permute-start(bf16[128,2048]{1,0:T(8,128)(2,1)S(1)} %add_convert_fusion.17), channel_id=1, source_target_pairs={{8,16},{12,20},{16,8},{20,12},{9,17},{13,21},{17,9},{21,13},{10,18... | collective-permute-start | bytes 1572872 | tf_op jit(solution)/shard_map/ppermute | solution.py:316
  1011.7 73.7 %collective-permute-start.43 = (bf16[256,2048]{1,0:T(8,128)(2,1)S(1)}, bf16[256,2048]{1,0:T(8,128)(2,1)}, u32[]{:S(2)}, u32[]{:S(2)}) collective-permute-start(bf16[256,2048]{1,0:T(8,128)(2,1)S(1)} %broadcast_select_fusion.2.refs_0_), channel_id=1, source_target_pairs={{0,4},{4,0},{8,12},{12,8},{16,20},{20,16},{24,28},{28,24},{1,5},{5... | collective-permute-start | bytes 3145736 | tf_op jit(solution)/shard_map/ppermute | solution.py:316
  1012.2 28.1 %collective-permute-start.42 = (bf16[256,2048]{1,0:T(8,128)(2,1)S(1)}, bf16[256,2048]{1,0:T(8,128)(2,1)S(1)}, u32[]{:S(2)}, u32[]{:S(2)}) collective-permute-start(bf16[256,2048]{1,0:T(8,128)(2,1)S(1)} %add_convert_fusion.6), channel_id=1, source_target_pairs={{8,0},{12,4},{16,24},{20,28},{9,1},{13,5},{17,25},{21,29},{10,2},{... | collective-permute-start | bytes 3145736 | tf_op jit(solution)/shard_map/ppermute | solution.py:316
  1013.9 58.6 %collective-permute-start.47 = (bf16[256,2048]{1,0:T(8,128)(2,1)S(1)}, bf16[256,2048]{1,0:T(8,128)(2,1)S(1)}, u32[]{:S(2)}, u32[]{:S(2)}) collective-permute-start(bf16[256,2048]{1,0:T(8,128)(2,1)S(1)} %add_convert_fusion.4), channel_id=1, source_target_pairs={{8,0},{12,4},{16,24},{20,28},{9,1},{13,5},{17,25},{21,29},{10,2},{... | collective-permute-start | bytes 3145736 | tf_op jit(solution)/shard_map/ppermute | solution.py:316
  1015.4 62.9 %collective-permute-start.32 = (bf16[128,2048]{1,0:T(8,128)(2,1)S(1)}, bf16[128,2048]{1,0:T(8,128)(2,1)S(1)}, u32[]{:S(2)}, u32[]{:S(2)}) collective-permute-start(bf16[128,2048]{1,0:T(8,128)(2,1)S(1)} %add_convert_fusion.16), channel_id=1, source_target_pairs={{8,0},{12,4},{16,24},{20,28},{9,1},{13,5},{17,25},{21,29},{10,2},{... | collective-permute-start | bytes 1572872 | tf_op jit(solution)/shard_map/ppermute | solution.py:316
  1017.5 64.1 %collective-permute-start.33 = (bf16[128,2048]{1,0:T(8,128)(2,1)}, bf16[128,2048]{1,0:T(8,128)(2,1)}, u32[]{:S(2)}, u32[]{:S(2)}) collective-permute-start(bf16[128,2048]{1,0:T(8,128)(2,1)} %broadcast_select_fusion.4.refs_0_), channel_id=1, source_target_pairs={{0,4},{4,0},{8,12},{12,8},{16,20},{20,16},{24,28},{28,24},{1,5},{5... | collective-permute-start | bytes 1572872 | tf_op jit(solution)/shard_map/ppermute | solution.py:316
  1040.4 45.1 %collective-permute-start.44 = (bf16[256,2048]{1,0:T(8,128)(2,1)S(1)}, bf16[256,2048]{1,0:T(8,128)(2,1)}, u32[]{:S(2)}, u32[]{:S(2)}) collective-permute-start(bf16[256,2048]{1,0:T(8,128)(2,1)S(1)} %broadcast_select_fusion.1.refs_1_), channel_id=1, source_target_pairs={{0,4},{4,0},{8,12},{12,8},{16,20},{20,16},{24,28},{28,24},{1,5},{5... | collective-permute-start | bytes 3145736 | tf_op jit(solution)/shard_map/ppermute | solution.py:316
  (100 other events, 1590.3 us)
Sparse Core Ops, SparseCore 0:
  10.4 46.6 all-gather.6
  59.6 122.7 all-gather.8
  185.5 96.4 all-gather.10
  528.9 87.2 reduce-scatter.6
  710.4 116.1 all-reduce.5
  830.0 68.5 reduce-scatter.8
